TPU v7x, 256 devices: a whole 4x4x8 slice. The times are simulated.
256 devices in a mesh: replica: 16 (over x, z_lo), dp: 16 (over z_hi, y, core).
Axes of the slice: x: 4, y: 4, z: 8 (z_hi: 2, z_lo: 4; z = z_hi * 4 + z_lo), core: 2. Of those that a mesh axis runs over, the one named last changes fastest.
Arguments:
- tokens: bfloat16 [65536, 8192], P(('replica', 'dp')), may hold values from -6 to 6
- norm_gain: float32 [16, 8192], P('replica'), may hold values from 0.1 to 1.9
- key_weight: bfloat16 [16, 8192, 512], P('replica', 'dp'), may hold values from -0.0625 to 0.0625
- key_cotangent: bfloat16 [65536, 512], P(('replica', 'dp')), may hold values from -6 to 6
- quantized: int32 [16, 8192, 512], P('replica', 'dp'), may hold values from -127 to 127
- scale_exponent: int32 [16, 8192, 4], P('replica', 'dp'), may hold values from -7 to -5
- momentum: float32 [8192, 512], P('dp'), may hold values from -6 to 6
- outer_params: float32 [8192, 512], P('dp'), may hold values from -6 to 6
Outputs:
- keys: bfloat16 [65536, 512], P(('replica', 'dp'))
- token_grad: bfloat16 [65536, 8192], P(('replica', 'dp'))
- weight_grad: bfloat16 [16, 8192, 512], P('replica', 'dp')
- gain_grad: bfloat16 [16, 8192], P('replica', 'dp')
- new_momentum: float32 [8192, 512], P('dp')
- new_params: float32 [8192, 512], P('dp')
All inputs are finite; a program needn't handle non-finite values.
Results may differ from a plain program's by a relative error of at most 0.019.
Values may be sent and summed in bfloat16 or wider, within the bound.
No kernel may reach another device: no remote copies, remote signals or barrier semaphores. Data moves between devices by JAX's collectives and lax.ppermute only.
A program may use at most 128 MiB of HBM per device.

v0:
```python
import jax
import jax.numpy as jnp
from jax import lax
from jax.sharding import PartitionSpec as P

epsilon = 1e-05
outer_decay = 0.9
outer_rate = 0.7


def outer_update(average, momentum, outer_params):
    new_momentum = outer_decay * momentum + average
    new_params = outer_params - outer_rate * (average + outer_decay * new_momentum)
    return (new_momentum, new_params)


def shards(
    tokens, norm_gain, key_weight, key_cotangent, quantized, scale_exponent, momentum, outer_params
):
    values = tokens.astype(jnp.float32)
    inverse_rms = lax.rsqrt(jnp.mean(values * values, axis=-1, keepdims=True) + epsilon)
    normed = values * inverse_rms
    gains = norm_gain[0]
    hidden = (normed * gains[None, :]).astype(jnp.bfloat16)
    weight_rows = key_weight[0]
    columns = hidden
    keys_full = jnp.dot(
        columns,
        lax.all_gather(weight_rows, "dp", axis=0, tiled=True),
        preferred_element_type=jnp.float32,
    )
    hidden_grad = lax.dot_general(
        key_cotangent,
        lax.all_gather(weight_rows, "dp", axis=0, tiled=True),
        (((1,), (1,)), ((), ())),
        preferred_element_type=jnp.float32,
    )
    keys = keys_full.astype(jnp.bfloat16)
    scaled = hidden_grad * gains[None, :]
    token_grad = inverse_rms * (scaled - normed * jnp.mean(scaled * normed, axis=-1, keepdims=True))
    gain_term = jnp.sum(hidden_grad * normed, axis=0)
    columns = hidden
    weight_grad = lax.psum_scatter(
        lax.dot_general(
            columns, key_cotangent, (((0,), (0,)), ((), ())), preferred_element_type=jnp.float32
        ).astype(jnp.bfloat16),
        "dp",
        scatter_dimension=0,
        tiled=True,
    ).astype(jnp.float32)
    gain_grad = lax.psum_scatter(
        gain_term.astype(jnp.bfloat16), "dp", scatter_dimension=0, tiled=True
    ).astype(jnp.float32)
    scales = jnp.exp2(scale_exponent[0].astype(jnp.float32))
    frag_rows = quantized.shape[1]
    frag_cols = quantized.shape[2]
    blocks = (
        quantized[0]
        .astype(jnp.float32)
        .reshape(frag_rows, scales.shape[1], frag_cols // scales.shape[1])
        * scales[..., None]
    )
    delta = blocks.reshape(frag_rows, frag_cols)
    replicas = lax.axis_size("replica")
    total = lax.psum(delta.astype(jnp.bfloat16), "replica").astype(jnp.float32)
    new_momentum, new_params = outer_update(total / replicas, momentum, outer_params)
    return (
        keys,
        token_grad.astype(jnp.bfloat16),
        weight_grad[None].astype(jnp.bfloat16),
        gain_grad[None].astype(jnp.bfloat16),
        new_momentum,
        new_params,
    )


def solution(mesh):
    return jax.shard_map(
        shards,
        mesh=mesh,
        in_specs=(
            P(("replica", "dp"), None),
            P("replica", None),
            P("replica", "dp", None),
            P(("replica", "dp"), None),
            P("replica", "dp", None),
            P("replica", "dp", None),
            P("dp", None),
            P("dp", None),
        ),
        out_specs=(
            P(("replica", "dp"), None),
            P(("replica", "dp"), None),
            P("replica", "dp", None),
            P("replica", "dp"),
            P("dp", None),
            P("dp", None),
        ),
        check_vma=False,
    )
```

profile of v0, /device:TPU:1, one launch (start us, length us, event | category | flops | bytes accessed | tf_op | source)
XLA Modules:
  0.0 379.1 jit_solution(7504370320972294480)
XLA Ops:
  8.0 0.0 copy-start
  8.0 0.0 copy-start.5
  8.0 0.0 all-reduce.3.cloned.1.call-start
  8.1 0.7 exponential_bitcast_fusion
  8.8 0.1 copy.15
  9.0 0.6 mul.83
  9.6 2.3 fusion.20
  11.8 0.0 all-reduce.3.cloned.1.call-update
  11.9 0.0 all-gather.3.cloned.1.call-start
  11.9 0.5 all-gather.3.cloned.1.call-update
  12.5 0.0 reduce-scatter.2.cloned.1.call-start
  12.5 3.1 fusion.10
  15.6 0.0 copy-done
  15.6 0.0 copy-done.5
  15.6 8.1 %convolution_convert_fusion = bf16[8192,512]{1,0:T(8,128)(2,1)} fusion(bf16[256,512]{1,0:T(8,128)(2,1)S(1)} %copy-done, bf16[256,8192]{1,0:T(8,128)(2,1)} %param.8, f32[8192]{0:T(1024)S(1)} %bitcast.24, f32[256]{0:T(256)S(1)} %add_rsqrt_fusion), kind=kOutput, calls=%fused_computation | convolution fusion | flops 2160066560 | bytes 12878848 | tf_op jit(solution)/shard_map/dot_general | solution.py:44
  23.8 0.0 copy-start.6
  23.8 0.0 copy-start.3
  23.8 0.0 reduce-scatter.2.cloned.1.call-update
  23.8 0.6 copy-done.6
  24.5 0.6 dynamic-slice
  25.7 230.8 %all-reduce.3.cloned.1.call-done = bf16[512,512]{1,0:T(8,128)(2,1)} async-done(((bf16[512,512]{1,0:T(8,128)(2,1)}), bf16[512,512]{1,0:T(8,128)(2,1)}) %all-reduce.3.cloned.1.call-update) | async-done | bytes 524304 | tf_op jit(solution)/shard_map/psum | solution.py:65
  256.5 0.0 copy-done.3
  256.5 0.0 copy-done.4
  256.5 2.7 multiply_subtract_fusion
  259.2 12.0 %fusion.9 = (bf16[8192]{0:T(1024)(128)(2,1)S(1)}, f32[256]{0:T(256)S(1)}, f32[256,8192]{1,0:T(8,128)}) fusion(bf16[256,8192]{1,0:T(8,128)(2,1)} %param.8, f32[256]{0:T(256)S(1)} %add_rsqrt_fusion, f32[8192]{0:T(1024)S(1)} %bitcast.25, bf16[256,512]{1,0:T(8,128)(2,1)S(1)} %copy-done, bf16[1,8192,512]{2,1,0:T(8,128)(2,1)} %all-gather.3.cloned.1.call-done), kind=kOutput, calls=%fused_computation.12 | convolution fusion | flops 2162155264 | bytes 21284864 | tf_op jit(solution)/shard_map/dot_general | solution.py:32
  271.2 88.1 %all-reduce = bf16[8192]{0:T(1024)(128)(2,1)S(1)} all-reduce(bf16[8192]{0:T(1024)(128)(2,1)S(1)} %get-tuple-element.6), channel_id=4, replica_groups=mesh['replica'=16,'dp'=16] {'dp'}, use_global_device_ids=true, to_apply=%region_4.0.clone | all-reduce | flops 8192 | bytes 32768
  359.3 0.1 dynamic-slice.1
  359.3 0.6 convert_element_type.57
  359.9 7.9 %fusion.15 = bf16[256,512]{1,0:T(8,128)(2,1)} fusion(bf16[1,8192,512]{2,1,0:T(8,128)(2,1)} %all-gather.3.cloned.1.call-done, bf16[256,8192]{1,0:T(8,128)(2,1)} %param.8, f32[8192]{0:T(1024)S(1)} %bitcast.26, f32[256]{0:T(256)S(1)} %add_rsqrt_fusion), kind=kOutput, calls=%fused_computation.18 | convolution fusion | flops 2156003328 | bytes 12878848 | tf_op jit(solution)/shard_map/dot_general | solution.py:27
  367.8 0.0 copy-done.1
  367.8 0.5 copy-done.2
  368.3 3.3 fusion.8
  (7 shorter events, 0.0 us)
Async XLA Ops:
  8.0 7.6 %copy-start = (bf16[256,512]{1,0:T(8,128)(2,1)S(1)}, bf16[256,512]{1,0:T(8,128)(2,1)}, u32[]{:S(2)}) copy-start(bf16[256,512]{1,0:T(8,128)(2,1)} %param.11) | copy-start | bytes 786436
  8.0 7.6 %copy-start.5 = (f32[1,8192]{1,0:T(1,128)S(1)}, f32[1,8192]{1,0:T(1,128)}, u32[]{:S(2)}) copy-start(f32[1,8192]{1,0:T(1,128)} %param.9) | copy-start | bytes 98308
  8.0 248.4 %all-reduce.3.cloned.1.call-start = ((), (), s32[]{:S(2)}) async-start(), calls=%async_computation.2 | async-start | bytes 1048576 | tf_op jit(solution)/shard_map/psum | solution.py:65
  11.9 247.3 %all-gather.3.cloned.1.call-start = ((), (), s32[]{:S(2)}) async-start(), calls=%async_computation.3 | async-start | bytes 8912896 | tf_op jit(solution)/shard_map/all_gather | solution.py:29
  12.5 359.2 %reduce-scatter.2.cloned.1.call-start = ((), (), s32[]{:S(2)}) async-start(), calls=%async_computation.1 | async-start | bytes 8912896 | tf_op jit(solution)/shard_map/reduce_scatter | solution.py:43
  23.8 0.7 copy-start.6
  23.8 232.7 %copy-start.3 = (f32[512,512]{1,0:T(8,128)S(1)}, f32[512,512]{1,0:T(8,128)}, u32[]{:S(2)}) copy-start(f32[512,512]{1,0:T(8,128)} %param.15) | copy-start | bytes 3145732
  23.8 232.7 %copy-start.4 = (f32[512,512]{1,0:T(8,128)S(1)}, f32[512,512]{1,0:T(8,128)}, u32[]{:S(2)}) copy-start(f32[512,512]{1,0:T(8,128)} %param.14) | copy-start | bytes 3145732
  359.9 7.9 %copy-start.1 = (bf16[256,8192]{1,0:T(8,128)(2,1)S(1)}, bf16[256,8192]{1,0:T(8,128)(2,1)}, u32[]{:S(2)}) copy-start(bf16[256,8192]{1,0:T(8,128)(2,1)} %param.8) | copy-start | bytes 12582916
  359.9 8.4 %copy-start.2 = (f32[256,8192]{1,0:T(8,128)S(1)}, f32[256,8192]{1,0:T(8,128)}, u32[]{:S(2)}) copy-start(f32[256,8192]{1,0:T(8,128)} %get-tuple-element.10) | copy-start | bytes 25165828
Sparse Core Ops, SparseCore 0:
  12.0 244.3 all-reduce.2
Sparse Core Ops, SparseCore 1:
  15.1 109.5 all-gather.2
  129.7 134.1 reduce-scatter.1
where the time goes:
time: 384 us; the launch traced here: 379 us
  waiting for transfers between devices  231 us (60%)
  blocking collectives  88.1 us (23%)
  matrix products  28 us (7%)
  between operations  16.2 us (4%)
  other arithmetic  12.2 us (3%)
    psum x1, waiting for transfers between devices, shards(): total = lax.psum(delta.astype(jnp.bfloat16), 'replica').astype(jnp.float32)  231 us
    unnamed x1, blocking collectives  88.1 us
    dot_general x1, matrix products, shards(): lax.dot_general(key_cotangent, lax.all_gather(weight_rows, 'dp', axis=0,...  12 us
    dot_general x1, matrix products, shards(): lax.dot_general(columns, key_cotangent, (((0,), (0,)), ((), ())), preferr...  8.15 us
    dot_general x1, matrix products, shards(): jnp.dot(columns, lax.all_gather(weight_rows, 'dp', axis=0, tiled=True), p...  7.87 us
  transfers between devices with their start and end apart: 3, of which 1 were waited for; matrix products, arithmetic and copies ran while one was open for 10% of the time, Pallas kernels for 0%

commit v1 on v0

v1 whole, which is shorter than its diff:
```python
import functools

import jax
import jax.numpy as jnp
from jax import lax
from jax.experimental import pallas as pl
from jax.experimental.pallas import tpu as pltpu
from jax.sharding import PartitionSpec as P

epsilon = 1e-05
outer_decay = 0.9
outer_rate = 0.7

F32 = jnp.float32
BF16 = jnp.bfloat16
N_Y, N_ZH, N_CORE = 4, 2, 2
N_X, N_ZL = 4, 4
VMEM_LIMIT = 50 * 1024 * 1024


def dp_moves(dy=0, dz=0, dc=0):
    pairs = []
    for zh in range(N_ZH):
        for y in range(N_Y):
            for c in range(N_CORE):
                to = (((zh + dz) % N_ZH) * N_Y + (y + dy) % N_Y) * N_CORE + (c + dc) % N_CORE
                pairs.append(((zh * N_Y + y) * N_CORE + c, to))
    return pairs


def to_up(v):
    return lax.ppermute(v, "dp", dp_moves(dy=1))


def to_down(v):
    return lax.ppermute(v, "dp", dp_moves(dy=-1))


def to_far(v):
    return lax.ppermute(v, "dp", dp_moves(dz=1))


def to_core(v):
    return lax.ppermute(v, "dp", dp_moves(dc=1))


def along_x(v, dx):
    pairs = [(x * N_ZL + z, ((x + dx) % N_X) * N_ZL + z) for x in range(N_X) for z in range(N_ZL)]
    return lax.ppermute(v, "replica", pairs)


def row_block(other_side, other_core, dy):
    me = lax.axis_index("dp")
    c = lax.rem(me, N_CORE)
    y = lax.rem(lax.div(me, N_CORE), N_Y)
    zh = lax.div(me, N_CORE * N_Y)
    if other_side:
        zh = 1 - zh
    if other_core:
        c = 1 - c
    return (zh * N_Y + lax.rem(y + dy, N_Y)) * N_CORE + c


def call(kernel, outs, ins, flops=0, nbytes=0, **kw):
    return pl.pallas_call(
        kernel,
        out_shape=outs,
        compiler_params=pltpu.CompilerParams(vmem_limit_bytes=VMEM_LIMIT),
        cost_estimate=pl.CostEstimate(flops=flops, bytes_accessed=nbytes, transcendentals=0),
        **kw,
    )(*ins)


def full(shape):
    return pl.BlockSpec(shape, lambda j: (0,) * len(shape))


def dot_tn(a, b):
    return lax.dot_general(a, b, (((0,), (0,)), ((), ())), preferred_element_type=F32)


def dot_nt(a, b):
    return lax.dot_general(a, b, (((1,), (1,)), ((), ())), preferred_element_type=F32)


def first_partials(tokens, gains, cot):
    t, d = tokens.shape
    k = cot.shape[1]
    f = k

    def kernel(tok, gain, ct, out, ir_out):
        j = pl.program_id(0)

        @pl.when(j == 0)
        def _():
            total = jnp.zeros((t, 128), F32)
            for i in range(d // 512):
                v = tok[:, i * 512 : (i + 1) * 512].astype(F32)
                v = v * v
                total += (v[:, :128] + v[:, 128:256]) + (v[:, 256:384] + v[:, 384:])
            mean = jnp.sum(total, axis=1, keepdims=True) / d
            ir_out[...] = jnp.broadcast_to(lax.rsqrt(mean + epsilon), (t, 128))

        cols = pl.ds(pl.multiple_of(row_block(True, True, j + 1) * f, f), f)
        hidden = (tok[:, cols].astype(F32) * ir_out[:, 0:1] * gain[:, cols]).astype(BF16)
        out[...] = dot_tn(hidden, ct[...]).astype(BF16)

    return call(
        kernel,
        (jax.ShapeDtypeStruct((N_Y * f, k), BF16), jax.ShapeDtypeStruct((t, 128), F32)),
        (tokens, gains, cot),
        flops=2 * t * N_Y * f * k,
        nbytes=2 * t * d + 2 * N_Y * f * k,
        grid=(N_Y,),
        in_specs=[full((t, d)), full((1, d)), full((t, k))],
        out_specs=(pl.BlockSpec((f, k), lambda j: (j, 0)), full((t, 128))),
    )


def partner_partials(tokens, gains, cot, ir):
    t, d = tokens.shape
    k = cot.shape[1]
    f = k

    def kernel(tok, gain, ct, irr, out):
        hidden = (tok[...].astype(F32) * irr[:, 0:1] * gain[...]).astype(BF16)
        out[...] = dot_tn(hidden, ct[...]).astype(BF16)

    return call(
        kernel,
        jax.ShapeDtypeStruct((N_Y * f, k), BF16),
        (tokens, gains, cot, ir),
        flops=2 * t * N_Y * f * k,
        nbytes=2 * t * N_Y * f + 2 * N_Y * f * k,
        grid=(N_Y,),
        in_specs=[
            pl.BlockSpec((t, f), lambda j: (0, row_block(False, True, j + 1))),
            pl.BlockSpec((1, f), lambda j: (0, row_block(False, True, j + 1))),
            full((t, k)),
            full((t, 128)),
        ],
        out_specs=pl.BlockSpec((f, k), lambda j: (j, 0)),
    )


def own_partials(tokens, gains, cot, ir, arrived, other_side):
    t, d = tokens.shape
    k = cot.shape[1]
    f = k
    h = f // 2

    def kernel(tok, gain, ct, irr, arr, up, down, up_later, down_later, own):
        j = pl.program_id(0)
        hidden = (tok[...].astype(F32) * irr[:, 0:1] * gain[...]).astype(BF16)
        total = (dot_tn(hidden, ct[...]) + arr[...].astype(F32)).astype(BF16)

        @pl.when(j == 0)
        def _():
            up_later[...] = total[:h]
            up[h:, :] = total[h:]

        @pl.when(j == 1)
        def _():
            up[:h, :] = total[:h]
            down[h:, :] = total[h:]

        @pl.when(j == 2)
        def _():
            down[:h, :] = total[:h]
            down_later[...] = total[h:]

        @pl.when(j == 3)
        def _():
            own[...] = total

    block = jax.ShapeDtypeStruct((f, k), BF16)
    half = jax.ShapeDtypeStruct((h, k), BF16)
    return call(
        kernel,
        (block, block, half, half, block),
        (tokens, gains, cot, ir, arrived),
        flops=2 * t * N_Y * f * k,
        nbytes=2 * t * N_Y * f + 4 * N_Y * f * k,
        grid=(N_Y,),
        in_specs=[
            pl.BlockSpec((t, f), lambda j: (0, row_block(other_side, False, j + 1))),
            pl.BlockSpec((1, f), lambda j: (0, row_block(other_side, False, j + 1))),
            full((t, k)),
            full((t, 128)),
            pl.BlockSpec((f, k), lambda j: (j, 0)),
        ],
        out_specs=(full((f, k)), full((f, k)), full((h, k)), full((h, k)), full((f, k))),
    )


def ring_terms(up, down, up_later, down_later):
    h = up_later.shape[0]
    from_down = to_up(up)
    from_up = to_down(down)
    last_down = to_up(up_later + from_down[:h])
    last_up = to_down(down_later + from_up[h:])
    return from_down, from_up, last_down, last_up


def side_sum(own, from_down, from_up, last_down, last_up):
    f, k = own.shape
    h = f // 2

    def kernel(o, fd, fu, ld, lu, out):
        out[:h, :] = (o[:h].astype(F32) + fu[:h].astype(F32) + ld[...].astype(F32)).astype(BF16)
        out[h:, :] = (o[h:].astype(F32) + fd[h:].astype(F32) + lu[...].astype(F32)).astype(BF16)

    return call(
        kernel,
        jax.ShapeDtypeStruct((f, k), BF16),
        (own, from_down, from_up, last_down, last_up),
        flops=4 * f * k,
        nbytes=10 * f * k,
    )


def final_sum(own, from_down, from_up, last_down, last_up, far, weight, gains):
    f, k = own.shape
    h = f // 2

    def kernel(o, fd, fu, ld, lu, fr, w, gain, out, gain_out):
        top = (o[:h].astype(F32) + fu[:h].astype(F32)) + (ld[...].astype(F32) + fr[:h].astype(F32))
        bottom = (o[h:].astype(F32) + fd[h:].astype(F32)) + (lu[...].astype(F32) + fr[h:].astype(F32))
        out[:h, :] = top.astype(BF16)
        out[h:, :] = bottom.astype(BF16)
        ones = jnp.ones((8, k), F32)
        cols = pl.ds(pl.multiple_of(lax.axis_index("dp") * f, f), f)
        g = gain[:, cols]
        for i, part in enumerate((top, bottom)):
            rows = slice(i * h, (i + 1) * h)
            sums = lax.dot_general(
                ones,
                part * w[rows].astype(F32),
                (((1,), (1,)), ((), ())),
                preferred_element_type=F32,
                precision=lax.Precision.HIGHEST,
            )
            gain_out[:, rows] = (sums[0:1] / g[:, rows]).astype(BF16)

    return call(
        kernel,
        (jax.ShapeDtypeStruct((f, k), BF16), jax.ShapeDtypeStruct((1, f), BF16)),
        (own, from_down, from_up, last_down, last_up, far, weight, gains),
        flops=40 * f * k,
        nbytes=14 * f * k,
    )


def ring_gather(rows):
    h = rows.shape[0] // 2
    from_down = to_up(rows)
    from_up = to_down(rows)
    return rows, from_down, from_up, to_up(from_down[:h]), to_down(from_up[h:])


GATHERED = ((0, 0), (3, 0), (1, 0), (2, 0), (2, 1))


def gathered_columns(other_side, other_core, which, f):
    dy, second = GATHERED[which]
    n = f // 2 if which >= 3 else f
    start = row_block(other_side, other_core, dy) * f + second * (f // 2)
    return pl.ds(pl.multiple_of(start, f // 2), n)


def project(tokens, gains, ir, weights, other_side, before=None, cot=None):
    t, d = tokens.shape
    f, k = weights[0][0].shape
    flat = tuple(weights[0]) + tuple(weights[1])
    n = len(flat)

    def kernel(*refs):
        tok, gain, irr = refs[:3]
        ws = refs[3 : 3 + n]
        rest = refs[3 + n :]
        scale = irr[:, 0:1]
        acc = jnp.zeros((t, k), F32) if before is None else rest[0][...]
        for i, w in enumerate(ws):
            cols = gathered_columns(other_side, i >= n // 2, i % (n // 2), f)
            hidden = (tok[:, cols].astype(F32) * scale * gain[:, cols]).astype(BF16)
            acc += jnp.dot(hidden, w[...], preferred_element_type=F32)
        if before is None:
            rest[0][...] = acc
        else:
            ct, keys, mean = rest[1:]
            keys[...] = acc.astype(BF16)
            row = jnp.sum(acc * ct[...].astype(F32), axis=1, keepdims=True) / d
            mean[...] = jnp.broadcast_to(row, (t, 128))

    ins = (tokens, gains, ir) + flat
    if before is None:
        outs = jax.ShapeDtypeStruct((t, k), F32)
    else:
        ins += (before, cot)
        outs = (jax.ShapeDtypeStruct((t, k), BF16), jax.ShapeDtypeStruct((t, 128), F32))
    return call(kernel, outs, ins, flops=t * d * k, nbytes=t * d * 2 + d * k)


def backward(tokens, gains, ir, mean, cot, own_side, far_side):
    t, d = tokens.shape
    f, k = own_side[0][0].shape
    flat = own_side[0] + own_side[1] + far_side[0] + far_side[1]
    n = len(own_side[0])

    def kernel(*refs):
        tok, gain, irr, mn, ct = refs[:5]
        ws = refs[5:-1]
        out = refs[-1]
        scale = irr[:, 0:1]
        shift = scale * scale * mn[:, 0:1]
        for i, w in enumerate(ws):
            cols = gathered_columns(i >= 2 * n, (i // n) % 2 == 1, i % n, f)
            grad = dot_nt(ct[...], w[...])
            x = tok[:, cols].astype(F32)
            out[:, cols] = (scale * (grad * gain[:, cols]) - x * shift).astype(BF16)

    return call(
        kernel,
        jax.ShapeDtypeStruct((t, d), BF16),
        (tokens, gains, ir, mean, cot) + flat,
        flops=2 * t * d * k,
        nbytes=4 * t * d + 2 * d * k,
    )


def outer_update(average, momentum, outer_params):
    new_momentum = outer_decay * momentum + average
    new_params = outer_params - outer_rate * (average + outer_decay * new_momentum)
    return (new_momentum, new_params)


def replica_sum(delta):
    n_rep = N_X * N_ZL
    x_groups = [[x * N_ZL + z for x in range(N_X)] for z in range(N_ZL)]
    z_groups = [[x * N_ZL + z for z in range(N_ZL)] for x in range(N_X)]
    part = lax.psum_scatter(
        delta, "replica", scatter_dimension=0, tiled=True, axis_index_groups=x_groups
    )
    part = lax.psum(part, "replica", axis_index_groups=z_groups)
    pieces = [part] + [along_x(part, dx) for dx in (1, 2, 3)]
    x = lax.axis_index("replica") // N_ZL
    rows = part.shape[0]
    total = jnp.zeros_like(delta)
    for i, piece in enumerate(pieces):
        total = lax.dynamic_update_slice(total, piece, (((x - i) % N_X) * rows, 0))
    return total


def shards(
    tokens, norm_gain, key_weight, key_cotangent, quantized, scale_exponent, momentum, outer_params
):
    gains = norm_gain
    weight = key_weight[0]

    scales = jnp.exp2(scale_exponent[0].astype(F32))
    frag_rows, frag_cols = quantized.shape[1:]
    blocks = (
        quantized[0].astype(F32).reshape(frag_rows, scales.shape[1], frag_cols // scales.shape[1])
        * scales[..., None]
    )
    delta = blocks.reshape(frag_rows, frag_cols).astype(BF16)
    total = replica_sum(delta).astype(F32)
    new_momentum, new_params = outer_update(total / lax.axis_size("replica"), momentum, outer_params)

    far_weight = to_far(weight)
    own_rows = ring_gather(weight)
    own_swapped = tuple(to_core(v) for v in own_rows)

    partner_far, ir = first_partials(tokens, gains, key_cotangent)
    arrived_far = to_core(partner_far)
    partner_near = partner_partials(tokens, gains, key_cotangent, ir)
    arrived_near = to_core(partner_near)

    packed = own_partials(tokens, gains, key_cotangent, ir, arrived_far, True)
    far_sum = to_far(side_sum(packed[4], *ring_terms(*packed[:4])))

    far_rows = ring_gather(far_weight)
    far_swapped = tuple(to_core(v) for v in far_rows)

    packed = own_partials(tokens, gains, key_cotangent, ir, arrived_near, False)
    terms = ring_terms(*packed[:4])

    near_keys = project(tokens, gains, ir, (own_rows, own_swapped), False)
    keys, mean = project(
        tokens, gains, ir, (far_rows, far_swapped), True, near_keys, key_cotangent
    )
    token_grad = backward(
        tokens, gains, ir, mean, key_cotangent, (own_rows, own_swapped), (far_rows, far_swapped)
    )
    weight_grad, gain_grad = final_sum(packed[4], *terms, far_sum, weight, gains)
    return (keys, token_grad, weight_grad[None], gain_grad, new_momentum, new_params)


def solution(mesh):
    return jax.shard_map(
        shards,
        mesh=mesh,
        in_specs=(
            P(("replica", "dp"), None),
            P("replica", None),
            P("replica", "dp", None),
            P(("replica", "dp"), None),
            P("replica", "dp", None),
            P("replica", "dp", None),
            P("dp", None),
            P("dp", None),
        ),
        out_specs=(
            P(("replica", "dp"), None),
            P(("replica", "dp"), None),
            P("replica", "dp", None),
            P("replica", "dp"),
            P("dp", None),
            P("dp", None),
        ),
        check_vma=False,
    )
```

time: 384 us -> 207 us (0.54)
  waiting for transfers between devices: 231 us -> 86.9 us
  blocking collectives: 88.1 us -> 0 us
  starting transfers between devices: 0.12 us -> 52.7 us
  Pallas kernels: 0 us -> 37.6 us
  matrix products: 28 us -> 0 us
  other arithmetic: 12.2 us -> 4.1 us
  local copies, waits for them, and re-layouts: 3.19 us -> 9.21 us
    psum x1, waiting for transfers between devices: 231 us -> 45.6 us  [replica_sum(): part = lax.psum(part, 'replica', axis_index_groups=z_groups)]
    unnamed x1 -> x0, blocking collectives: 88.1 us -> none
    ppermute x0 -> x33, starting transfers between devices: none -> 52.6 us  [the longest x12 20 us: to_core(): return lax.ppermute(v, 'dp', dp_moves(dc=1))]
    ppermute x0 -> x33, waiting for transfers between devices: none -> 41.3 us  [the longest x8 16.1 us: to_down(): return lax.ppermute(v, 'dp', dp_moves(dy=-1))]
    pallas_call x0 -> x9, Pallas kernels: none -> 37.6 us  [call(): pl.pallas_call(kernel, out_shape=outs, compiler_params=pltpu.CompilerPara...]
    dot_general x3 -> x0, matrix products: 28 us -> none  [the longest x1 12 us: shards(): lax.dot_general(key_cotangent, lax.all_gather(weight_rows, 'dp', axis=0,...]
    unnamed x16 -> x56, local copies, waits for them, and re-layouts: 1.85 us -> 8.3 us
  transfers between devices with their start and end apart: 3 -> 35, of which waited for: 1 -> 11; matrix products, arithmetic and copies ran while one was open for 10% -> 2% of each run, Pallas kernels for 0% -> 15%
where the time goes in v1:
time: 207 us; the launch traced here: 205 us
  waiting for transfers between devices  86.9 us (42%)
  starting transfers between devices  52.7 us (25%)
  Pallas kernels  37.6 us (18%)
  between operations  14.6 us (7%)
  local copies, waits for them, and re-layouts  9.21 us (4%)
  other arithmetic  4.1 us (2%)
    psum x1, waiting for transfers between devices, replica_sum(): part = lax.psum(part, 'replica', axis_index_groups=z_groups)  45.6 us
    pallas_call x9, Pallas kernels, call(): pl.pallas_call(kernel, out_shape=outs, compiler_params=pltpu.CompilerPara...  37.6 us
    ppermute x12, starting transfers between devices, to_core(): return lax.ppermute(v, 'dp', dp_moves(dc=1))  20 us
    ppermute x8, waiting for transfers between devices, to_down(): return lax.ppermute(v, 'dp', dp_moves(dy=-1))  16.1 us
    ppermute x8, starting transfers between devices, to_down(): return lax.ppermute(v, 'dp', dp_moves(dy=-1))  13.4 us
    ppermute x8, waiting for transfers between devices, to_up(): return lax.ppermute(v, 'dp', dp_moves(dy=1))  11.9 us
    ppermute x2, waiting for transfers between devices, to_far(): return lax.ppermute(v, 'dp', dp_moves(dz=1))  11.1 us
    ppermute x2, starting transfers between devices, to_far(): return lax.ppermute(v, 'dp', dp_moves(dz=1))  9.33 us
  transfers between devices with their start and end apart: 35, of which 11 were waited for; matrix products, arithmetic and copies ran while one was open for 2% of the time, Pallas kernels for 15%

profile of v1, /device:TPU:1, one launch (start us, length us, event | category | flops | bytes accessed | tf_op | source)
XLA Modules:
  0.0 205.1 jit_solution(855644023511904544)
XLA Ops:
  8.9 6.0 %shard_map.127 = (bf16[2048,512]{1,0:T(8,128)(2,1)}, f32[256,128]{1,0:T(8,128)S(1)}) custom-call(bf16[256,8192]{1,0:T(8,128)(2,1)} %tok.7, f32[1,8192]{1,0:T(1,128)S(1)} %copy-done.6, bf16[256,512]{1,0:T(8,128)(2,1)S(1)} %copy-done), custom_call_target="tpu_custom_call" | custom-call | flops 536870912 | bytes 6291456 | tf_op jit(solution)/shard_map/pallas_call | solution.py:65
  15.0 3.2 %collective-permute-start.24 = (bf16[2048,512]{1,0:T(8,128)(2,1)}, bf16[2048,512]{1,0:T(8,128)(2,1)}, u32[]{:S(2)}, u32[]{:S(2)}) collective-permute-start(bf16[2048,512]{1,0:T(8,128)(2,1)} %get-tuple-element.30), channel_id=1, source_target_pairs={{0,1},{1,0},{2,3},{3,2},{4,5},{5,4},{6,7},{7,6},{8,9},{9,8},{10,11... | collective-permute-start | bytes 6291464 | tf_op jit(solution)/shard_map/ppermute | solution.py:44
  18.2 6.5 %collective-permute-start = (bf16[512,512]{1,0:T(8,128)(2,1)S(1)}, bf16[512,512]{1,0:T(8,128)(2,1)}, u32[]{:S(2)}, u32[]{:S(2)}) collective-permute-start(bf16[512,512]{1,0:T(8,128)(2,1)S(1)} %bitcast.12), channel_id=1, source_target_pairs={{0,8},{1,9},{2,10},{3,11},{4,12},{5,13},{6,14},{7,15},{8,0},{9,1},... | collective-permute-start | bytes 1572872 | tf_op jit(solution)/shard_map/ppermute | solution.py:40
  26.1 4.4 %shard_map.131 = bf16[2048,512]{1,0:T(8,128)(2,1)} custom-call(bf16[256,8192]{1,0:T(8,128)(2,1)} %tok.7, f32[1,8192]{1,0:T(1,128)S(1)} %copy-done.6, bf16[256,512]{1,0:T(8,128)(2,1)S(1)} %copy-done, f32[256,128]{1,0:T(8,128)S(1)} %get-tuple-element.22.refs_2_.irr), custom_call_target="tpu_custom_call" | custom-call | flops 536870912 | bytes 3145728 | tf_op jit(solution)/shard_map/pallas_call | solution.py:65
  34.4 2.3 %fusion = bf16[512,512]{1,0:T(8,128)(2,1)} fusion(f32[64,8,4,128]{3,2,1,0:T(4,128)S(1)} %bitcast.18, s32[1,512,512]{2,1,0:T(8,128)} %param.12), kind=kLoop, calls=%fused_computation.1 | loop fusion | flops 786432 | bytes 2621440 | tf_op jit(solution)/shard_map/convert_element_type | solution.py:366
  36.8 2.2 %collective-permute-done.refs_3_.refs_15_ = bf16[512,512]{1,0:T(8,128)(2,1)} collective-permute-done((bf16[512,512]{1,0:T(8,128)(2,1)S(1)}, bf16[512,512]{1,0:T(8,128)(2,1)}, u32[]{:S(2)}, u32[]{:S(2)}) %collective-permute-start) | collective-permute-done | bytes 524320 | tf_op jit(solution)/shard_map/ppermute | solution.py:40
  42.4 4.8 %collective-permute-done.12.refs_6_.refs_8_ = bf16[256,512]{1,0:T(8,128)(2,1)S(1)} collective-permute-done((bf16[256,512]{1,0:T(8,128)(2,1)S(1)}, bf16[256,512]{1,0:T(8,128)(2,1)S(1)}, u32[]{:S(2)}, u32[]{:S(2)}) %collective-permute-start.12) | collective-permute-done | bytes 262176 | tf_op jit(solution)/shard_map/ppermute | solution.py:32
  47.2 6.1 %collective-permute-done.13.refs_7_.refs_9_ = bf16[256,512]{1,0:T(8,128)(2,1)} collective-permute-done((bf16[256,512]{1,0:T(8,128)(2,1)S(1)}, bf16[256,512]{1,0:T(8,128)(2,1)}, u32[]{:S(2)}, u32[]{:S(2)}) %collective-permute-start.13) | collective-permute-done | bytes 262176 | tf_op jit(solution)/shard_map/ppermute | solution.py:36
  53.3 2.6 %collective-permute-start.2 = (bf16[512,512]{1,0:T(8,128)(2,1)}, bf16[512,512]{1,0:T(8,128)(2,1)S(1)}, u32[]{:S(2)}, u32[]{:S(2)}) collective-permute-start(bf16[512,512]{1,0:T(8,128)(2,1)} %collective-permute-done.refs_3_.refs_15_), channel_id=1, source_target_pairs={{0,6},{1,7},{2,0},{3,1},{4,2},{5,3},{6,4},{7,5},{8,14},{9,15},{10,... | collective-permute-start | bytes 1572872 | tf_op jit(solution)/shard_map/ppermute | solution.py:36
  56.8 3.3 %collective-permute-start.17 = (bf16[256,512]{1,0:T(8,128)(2,1)S(1)}, bf16[256,512]{1,0:T(8,128)(2,1)}, u32[]{:S(2)}, u32[]{:S(2)}) collective-permute-start(bf16[256,512]{1,0:T(8,128)(2,1)S(1)} %collective-permute-done.12.refs_6_.refs_8_), channel_id=1, source_target_pairs={{0,1},{1,0},{2,3},{3,2},{4,5},{5,4},{6,7},{7,6},{8,9},{9,8},{10,11... | collective-permute-start | bytes 786440 | tf_op jit(solution)/shard_map/ppermute | solution.py:44
  60.3 3.9 %shard_map.133 = (bf16[512,512]{1,0:T(8,128)(2,1)S(1)}, bf16[512,512]{1,0:T(8,128)(2,1)S(1)}, bf16[256,512]{1,0:T(8,128)(2,1)S(1)}, bf16[256,512]{1,0:T(8,128)(2,1)S(1)}, bf16[512,512]{1,0:T(8,128)(2,1)S(1)}) custom-call(bf16[256,8192]{1,0:T(8,128)(2,1)} %tok.7, f32[1,8192]{1,0:T(1,128)S(1)} %copy-done.7, bf16[256,512]{1,0:T(8,128)(2,1)S(1)} %copy-done.1, ...), custom_call_target="tpu_custom_call" | custom-call | flops 536870912 | bytes 5242880 | tf_op jit(solution)/shard_map/pallas_call | solution.py:65
  68.0 45.6 %all-reduce.2.cloned.1.call-done = bf16[128,512]{1,0:T(8,128)(2,1)} async-done(((bf16[128,512]{1,0:T(8,128)(2,1)}), bf16[128,512]{1,0:T(8,128)(2,1)}) %all-reduce.2.cloned.1.call-update) | async-done | bytes 131088 | tf_op jit(solution)/shard_map/psum | solution.py:344
  117.1 4.0 %shard_map.128.refs_13_ = f32[256,512]{1,0:T(8,128)S(1)} custom-call(bf16[256,8192]{1,0:T(8,128)(2,1)} %tok.7, f32[1,8192]{1,0:T(1,128)S(1)} %copy-done.7, f32[256,128]{1,0:T(8,128)S(1)} %get-tuple-element.22.refs_2_.irr, bf16[512,512]{1,0:T(8,128)(2,1)S(1)} %bitcast.15, bf16[512,512]{1,0:T(8,128)(2,1)S(1)} %collective-permute-done.10.refs_4_.refs_6_, ...), custom_call_target="tpu_custom_call" | custom-call | flops 1073741824 | bytes 8388608 | tf_op jit(solution)/shard_map/pallas_call | solution.py:65
  121.1 3.4 %collective-permute-start.5 = (bf16[512,512]{1,0:T(8,128)(2,1)}, bf16[512,512]{1,0:T(8,128)(2,1)S(1)}, u32[]{:S(2)}, u32[]{:S(2)}) collective-permute-start(bf16[512,512]{1,0:T(8,128)(2,1)} %collective-permute-done.refs_3_.refs_15_), channel_id=1, source_target_pairs={{0,1},{1,0},{2,3},{3,2},{4,5},{5,4},{6,7},{7,6},{8,9},{9,8},{10,11... | collective-permute-start | bytes 1572872 | tf_op jit(solution)/shard_map/ppermute | solution.py:44
  124.6 2.5 %collective-permute-start.31 = (bf16[128,512]{1,0:T(8,128)(2,1)S(1)}, bf16[128,512]{1,0:T(8,128)(2,1)S(1)}, u32[]{:S(2)}, u32[]{:S(2)}) collective-permute-start(bf16[128,512]{1,0:T(8,128)(2,1)S(1)} %copy-done.26), channel_id=1, source_target_pairs={{0,128},{16,144},{32,160},{48,176},{64,192},{80,208},{96,224},{112... | collective-permute-start | bytes 393224 | tf_op jit(solution)/shard_map/ppermute | solution.py:49
  128.4 2.2 %collective-permute-done.31 = bf16[128,512]{1,0:T(8,128)(2,1)S(1)} collective-permute-done((bf16[128,512]{1,0:T(8,128)(2,1)S(1)}, bf16[128,512]{1,0:T(8,128)(2,1)S(1)}, u32[]{:S(2)}, u32[]{:S(2)}) %collective-permute-start.31) | collective-permute-done | bytes 131104 | tf_op jit(solution)/shard_map/ppermute | solution.py:49
  132.2 4.0 %shard_map.132 = (bf16[512,512]{1,0:T(8,128)(2,1)S(1)}, bf16[512,512]{1,0:T(8,128)(2,1)S(1)}, bf16[256,512]{1,0:T(8,128)(2,1)S(1)}, bf16[256,512]{1,0:T(8,128)(2,1)S(1)}, bf16[512,512]{1,0:T(8,128)(2,1)S(1)}) custom-call(bf16[256,8192]{1,0:T(8,128)(2,1)} %tok.7, f32[1,8192]{1,0:T(1,128)S(1)} %copy-done.7, bf16[256,512]{1,0:T(8,128)(2,1)S(1)} %copy-done.1, ...), custom_call_target="tpu_custom_call" | custom-call | flops 536870912 | bytes 5242880 | tf_op jit(solution)/shard_map/pallas_call | solution.py:65
  137.6 1.6 collective-permute-start.4
  139.2 3.4 %collective-permute-done.26.fu = bf16[512,512]{1,0:T(8,128)(2,1)S(1)} collective-permute-done((bf16[512,512]{1,0:T(8,128)(2,1)S(1)}, bf16[512,512]{1,0:T(8,128)(2,1)S(1)}, u32[]{:S(2)}, u32[]{:S(2)}) %collective-permute-start.26) | collective-permute-done | bytes 524320 | tf_op jit(solution)/shard_map/ppermute | solution.py:36
  142.6 4.4 %collective-permute-start.6 = (bf16[512,512]{1,0:T(8,128)(2,1)S(1)}, bf16[512,512]{1,0:T(8,128)(2,1)S(1)}, u32[]{:S(2)}, u32[]{:S(2)}) collective-permute-start(bf16[512,512]{1,0:T(8,128)(2,1)S(1)} %collective-permute-done.1.refs_4_.refs_16_), channel_id=1, source_target_pairs={{0,1},{1,0},{2,3},{3,2},{4,5},{5,4},{6,7},{7,6},{8,9},{9,8},{10,11... | collective-permute-start | bytes 1572872 | tf_op jit(solution)/shard_map/ppermute | solution.py:44
  147.1 2.7 %collective-permute-start.21 = (bf16[512,512]{1,0:T(8,128)(2,1)S(1)}, bf16[512,512]{1,0:T(8,128)(2,1)S(1)}, u32[]{:S(2)}, u32[]{:S(2)}) collective-permute-start(bf16[512,512]{1,0:T(8,128)(2,1)S(1)} %get-tuple-element.27), channel_id=1, source_target_pairs={{0,6},{1,7},{2,0},{3,1},{4,2},{5,3},{6,4},{7,5},{8,14},{9,15},{10,... | collective-permute-start | bytes 1572872 | tf_op jit(solution)/shard_map/ppermute | solution.py:36
  149.9 1.7 collective-permute-done.20.fd
  152.6 1.7 multiply_subtract_fusion
  154.2 3.8 %collective-permute-done.27.ld = bf16[256,512]{1,0:T(8,128)(2,1)S(1)} collective-permute-done((bf16[256,512]{1,0:T(8,128)(2,1)S(1)}, bf16[256,512]{1,0:T(8,128)(2,1)S(1)}, u32[]{:S(2)}, u32[]{:S(2)}) %collective-permute-start.27) | collective-permute-done | bytes 262176 | tf_op jit(solution)/shard_map/ppermute | solution.py:32
  158.0 1.8 collective-permute-start.8
  159.8 6.6 %collective-permute-done.28.lu = bf16[256,512]{1,0:T(8,128)(2,1)S(1)} collective-permute-done((bf16[256,512]{1,0:T(8,128)(2,1)S(1)}, bf16[256,512]{1,0:T(8,128)(2,1)S(1)}, u32[]{:S(2)}, u32[]{:S(2)}) %collective-permute-start.28) | collective-permute-done | bytes 262176 | tf_op jit(solution)/shard_map/ppermute | solution.py:36
  167.9 2.8 %collective-permute-start.29 = (bf16[512,512]{1,0:T(8,128)(2,1)S(1)}, bf16[512,512]{1,0:T(8,128)(2,1)S(1)}, u32[]{:S(2)}, u32[]{:S(2)}) collective-permute-start(bf16[512,512]{1,0:T(8,128)(2,1)S(1)} %shard_map.134), channel_id=1, source_target_pairs={{0,8},{1,9},{2,10},{3,11},{4,12},{5,13},{6,14},{7,15},{8,0},{9,1},... | collective-permute-start | bytes 1572872 | tf_op jit(solution)/shard_map/ppermute | solution.py:40
  171.9 2.5 %collective-permute-start.23 = (bf16[256,512]{1,0:T(8,128)(2,1)S(1)}, bf16[256,512]{1,0:T(8,128)(2,1)S(1)}, u32[]{:S(2)}, u32[]{:S(2)}) collective-permute-start(bf16[256,512]{1,0:T(8,128)(2,1)S(1)} %slice_add_fusion.2), channel_id=1, source_target_pairs={{0,6},{1,7},{2,0},{3,1},{4,2},{5,3},{6,4},{7,5},{8,14},{9,15},{10,... | collective-permute-start | bytes 786440 | tf_op jit(solution)/shard_map/ppermute | solution.py:36
  174.5 4.9 %shard_map.129 = (bf16[256,512]{1,0:T(8,128)(2,1)}, f32[256,128]{1,0:T(8,128)S(1)}) custom-call(bf16[256,8192]{1,0:T(8,128)(2,1)} %tok.7, f32[1,8192]{1,0:T(1,128)S(1)} %copy-done.7, f32[256,128]{1,0:T(8,128)S(1)} %get-tuple-element.22.refs_2_.irr, bf16[512,512]{1,0:T(8,128)(2,1)} %collective-permute-done.refs_3_.refs_15_, ...), custom_call_target="tpu_custom_call" | custom-call | flops 1073741824 | bytes 8388608 | tf_op jit(solution)/shard_map/pallas_call | solution.py:65
  179.3 8.4 %shard_map.130 = bf16[256,8192]{1,0:T(8,128)(2,1)} custom-call(bf16[256,8192]{1,0:T(8,128)(2,1)} %tok.7, f32[1,8192]{1,0:T(1,128)S(1)} %copy-done.7, f32[256,128]{1,0:T(8,128)S(1)} %get-tuple-element.22.refs_2_.irr, f32[256,128]{1,0:T(8,128)S(1)} %get-tuple-element.24.refs_3_, bf16[256,512]{1,0:T(8,128)(2,1)S(1)} %copy-done.1, ...), custom_call_target="tpu_custom_call" | custom-call | flops 2147483648 | bytes 16777216 | tf_op jit(solution)/shard_map/pallas_call | solution.py:65
  187.8 8.8 %collective-permute-done.29.fr = bf16[512,512]{1,0:T(8,128)(2,1)S(1)} collective-permute-done((bf16[512,512]{1,0:T(8,128)(2,1)S(1)}, bf16[512,512]{1,0:T(8,128)(2,1)S(1)}, u32[]{:S(2)}, u32[]{:S(2)}) %collective-permute-start.29) | collective-permute-done | bytes 524320 | tf_op jit(solution)/shard_map/ppermute | solution.py:40
  196.6 1.7 shard_map.135
  (123 shorter events, 26.5 us)
Async XLA Ops:
  7.2 52.9 %reduce-scatter.2.cloned.1.call-start = ((), (), s32[]{:S(2)}) async-start(), calls=%async_computation.1 | async-start | bytes 655360 | tf_op jit(solution)/shard_map/reduce_scatter | solution.py:341
  15.0 45.1 %collective-permute-start.24 = (bf16[2048,512]{1,0:T(8,128)(2,1)}, bf16[2048,512]{1,0:T(8,128)(2,1)}, u32[]{:S(2)}, u32[]{:S(2)}) collective-permute-start(bf16[2048,512]{1,0:T(8,128)(2,1)} %get-tuple-element.30), channel_id=1, source_target_pairs={{0,1},{1,0},{2,3},{3,2},{4,5},{5,4},{6,7},{7,6},{8,9},{9,8},{10,11... | collective-permute-start | bytes 6291464 | tf_op jit(solution)/shard_map/ppermute | solution.py:44
  18.2 14.9 %collective-permute-start.10 = (bf16[512,512]{1,0:T(8,128)(2,1)S(1)}, bf16[512,512]{1,0:T(8,128)(2,1)S(1)}, u32[]{:S(2)}, u32[]{:S(2)}) collective-permute-start(bf16[512,512]{1,0:T(8,128)(2,1)S(1)} %bitcast.11), channel_id=1, source_target_pairs={{0,2},{1,3},{2,4},{3,5},{4,6},{5,7},{6,0},{7,1},{8,10},{9,11},{10,... | collective-permute-start | bytes 1572872 | tf_op jit(solution)/shard_map/ppermute | solution.py:32
  18.2 20.8 %collective-permute-start = (bf16[512,512]{1,0:T(8,128)(2,1)S(1)}, bf16[512,512]{1,0:T(8,128)(2,1)}, u32[]{:S(2)}, u32[]{:S(2)}) collective-permute-start(bf16[512,512]{1,0:T(8,128)(2,1)S(1)} %bitcast.12), channel_id=1, source_target_pairs={{0,8},{1,9},{2,10},{3,11},{4,12},{5,13},{6,14},{7,15},{8,0},{9,1},... | collective-permute-start | bytes 1572872 | tf_op jit(solution)/shard_map/ppermute | solution.py:40
  24.7 15.6 %collective-permute-start.11 = (bf16[512,512]{1,0:T(8,128)(2,1)S(1)}, bf16[512,512]{1,0:T(8,128)(2,1)S(1)}, u32[]{:S(2)}, u32[]{:S(2)}) collective-permute-start(bf16[512,512]{1,0:T(8,128)(2,1)S(1)} %bitcast.13), channel_id=1, source_target_pairs={{0,6},{1,7},{2,0},{3,1},{4,2},{5,3},{6,4},{7,5},{8,14},{9,15},{10,... | collective-permute-start | bytes 1572872 | tf_op jit(solution)/shard_map/ppermute | solution.py:36
  30.5 101.6 %collective-permute-start.19 = (bf16[2048,512]{1,0:T(8,128)(2,1)}, bf16[2048,512]{1,0:T(8,128)(2,1)}, u32[]{:S(2)}, u32[]{:S(2)}) collective-permute-start(bf16[2048,512]{1,0:T(8,128)(2,1)} %shard_map.131), channel_id=1, source_target_pairs={{0,1},{1,0},{2,3},{3,2},{4,5},{5,4},{6,7},{7,6},{8,9},{9,8},{10,11... | collective-permute-start | bytes 6291464 | tf_op jit(solution)/shard_map/ppermute | solution.py:44
  33.1 8.4 %collective-permute-start.14 = (bf16[512,512]{1,0:T(8,128)(2,1)S(1)}, bf16[512,512]{1,0:T(8,128)(2,1)S(1)}, u32[]{:S(2)}, u32[]{:S(2)}) collective-permute-start(bf16[512,512]{1,0:T(8,128)(2,1)S(1)} %bitcast.14), channel_id=1, source_target_pairs={{0,1},{1,0},{2,3},{3,2},{4,5},{5,4},{6,7},{7,6},{8,9},{9,8},{10,11... | collective-permute-start | bytes 1572872 | tf_op jit(solution)/shard_map/ppermute | solution.py:44
  36.7 76.9 %all-reduce.2.cloned.1.call-start = ((), (), s32[]{:S(2)}) async-start(), calls=%async_computation.2 | async-start | bytes 262144 | tf_op jit(solution)/shard_map/psum | solution.py:344
  39.0 8.1 %collective-permute-start.12 = (bf16[256,512]{1,0:T(8,128)(2,1)S(1)}, bf16[256,512]{1,0:T(8,128)(2,1)S(1)}, u32[]{:S(2)}, u32[]{:S(2)}) collective-permute-start(bf16[256,512]{1,0:T(8,128)(2,1)S(1)} %slice.34), channel_id=1, source_target_pairs={{0,2},{1,3},{2,4},{3,5},{4,6},{5,7},{6,0},{7,1},{8,10},{9,11},{10,... | collective-permute-start | bytes 786440 | tf_op jit(solution)/shard_map/ppermute | solution.py:32
  40.3 13.0 %collective-permute-start.15 = (bf16[512,512]{1,0:T(8,128)(2,1)S(1)}, bf16[512,512]{1,0:T(8,128)(2,1)}, u32[]{:S(2)}, u32[]{:S(2)}) collective-permute-start(bf16[512,512]{1,0:T(8,128)(2,1)S(1)} %collective-permute-done.10.refs_4_.refs_6_), channel_id=1, source_target_pairs={{0,1},{1,0},{2,3},{3,2},{4,5},{5,4},{6,7},{7,6},{8,9},{9,8},{10,11... | collective-permute-start | bytes 1572872 | tf_op jit(solution)/shard_map/ppermute | solution.py:44
  42.3 13.6 %collective-permute-start.16 = (bf16[512,512]{1,0:T(8,128)(2,1)S(1)}, bf16[512,512]{1,0:T(8,128)(2,1)S(1)}, u32[]{:S(2)}, u32[]{:S(2)}) collective-permute-start(bf16[512,512]{1,0:T(8,128)(2,1)S(1)} %collective-permute-done.11.refs_5_.refs_7_), channel_id=1, source_target_pairs={{0,1},{1,0},{2,3},{3,2},{4,5},{5,4},{6,7},{7,6},{8,9},{9,8},{10,11... | collective-permute-start | bytes 1572872 | tf_op jit(solution)/shard_map/ppermute | solution.py:44
  53.3 67.8 %collective-permute-start.1 = (bf16[512,512]{1,0:T(8,128)(2,1)}, bf16[512,512]{1,0:T(8,128)(2,1)S(1)}, u32[]{:S(2)}, u32[]{:S(2)}) collective-permute-start(bf16[512,512]{1,0:T(8,128)(2,1)} %collective-permute-done.refs_3_.refs_15_), channel_id=1, source_target_pairs={{0,2},{1,3},{2,4},{3,5},{4,6},{5,7},{6,0},{7,1},{8,10},{9,11},{10,... | collective-permute-start | bytes 1572872 | tf_op jit(solution)/shard_map/ppermute | solution.py:32
  53.3 71.2 %collective-permute-start.2 = (bf16[512,512]{1,0:T(8,128)(2,1)}, bf16[512,512]{1,0:T(8,128)(2,1)S(1)}, u32[]{:S(2)}, u32[]{:S(2)}) collective-permute-start(bf16[512,512]{1,0:T(8,128)(2,1)} %collective-permute-done.refs_3_.refs_15_), channel_id=1, source_target_pairs={{0,6},{1,7},{2,0},{3,1},{4,2},{5,3},{6,4},{7,5},{8,14},{9,15},{10,... | collective-permute-start | bytes 1572872 | tf_op jit(solution)/shard_map/ppermute | solution.py:36
  56.8 11.2 %collective-permute-start.17 = (bf16[256,512]{1,0:T(8,128)(2,1)S(1)}, bf16[256,512]{1,0:T(8,128)(2,1)}, u32[]{:S(2)}, u32[]{:S(2)}) collective-permute-start(bf16[256,512]{1,0:T(8,128)(2,1)S(1)} %collective-permute-done.12.refs_6_.refs_8_), channel_id=1, source_target_pairs={{0,1},{1,0},{2,3},{3,2},{4,5},{5,4},{6,7},{7,6},{8,9},{9,8},{10,11... | collective-permute-start | bytes 786440 | tf_op jit(solution)/shard_map/ppermute | solution.py:44
  60.1 54.7 %collective-permute-start.18 = (bf16[256,512]{1,0:T(8,128)(2,1)}, bf16[256,512]{1,0:T(8,128)(2,1)}, u32[]{:S(2)}, u32[]{:S(2)}) collective-permute-start(bf16[256,512]{1,0:T(8,128)(2,1)} %collective-permute-done.13.refs_7_.refs_9_), channel_id=1, source_target_pairs={{0,1},{1,0},{2,3},{3,2},{4,5},{5,4},{6,7},{7,6},{8,9},{9,8},{10,11... | collective-permute-start | bytes 786440 | tf_op jit(solution)/shard_map/ppermute | solution.py:44
  113.6 13.5 %collective-permute-start.30 = (bf16[128,512]{1,0:T(8,128)(2,1)}, bf16[128,512]{1,0:T(8,128)(2,1)S(1)}, u32[]{:S(2)}, u32[]{:S(2)}) collective-permute-start(bf16[128,512]{1,0:T(8,128)(2,1)} %all-reduce.2.cloned.1.call-done), channel_id=1, source_target_pairs={{0,64},{16,80},{32,96},{48,112},{64,128},{80,144},{96,160},{112,17... | collective-permute-start | bytes 393224 | tf_op jit(solution)/shard_map/ppermute | solution.py:49
  114.8 22.7 %collective-permute-start.25 = (bf16[512,512]{1,0:T(8,128)(2,1)}, bf16[512,512]{1,0:T(8,128)(2,1)S(1)}, u32[]{:S(2)}, u32[]{:S(2)}) collective-permute-start(bf16[512,512]{1,0:T(8,128)(2,1)} %copy-done.20), channel_id=1, source_target_pairs={{0,2},{1,3},{2,4},{3,5},{4,6},{5,7},{6,0},{7,1},{8,10},{9,11},{10,... | collective-permute-start | bytes 1572872 | tf_op jit(solution)/shard_map/ppermute | solution.py:32
  121.1 25.9 %collective-permute-start.5 = (bf16[512,512]{1,0:T(8,128)(2,1)}, bf16[512,512]{1,0:T(8,128)(2,1)S(1)}, u32[]{:S(2)}, u32[]{:S(2)}) collective-permute-start(bf16[512,512]{1,0:T(8,128)(2,1)} %collective-permute-done.refs_3_.refs_15_), channel_id=1, source_target_pairs={{0,1},{1,0},{2,3},{3,2},{4,5},{5,4},{6,7},{7,6},{8,9},{9,8},{10,11... | collective-permute-start | bytes 1572872 | tf_op jit(solution)/shard_map/ppermute | solution.py:44
  127.2 9.1 %collective-permute-start.32 = (bf16[128,512]{1,0:T(8,128)(2,1)S(1)}, bf16[128,512]{1,0:T(8,128)(2,1)S(1)}, u32[]{:S(2)}, u32[]{:S(2)}) collective-permute-start(bf16[128,512]{1,0:T(8,128)(2,1)S(1)} %copy-done.26), channel_id=1, source_target_pairs={{0,192},{16,208},{32,224},{48,240},{64,0},{80,16},{96,32},{112,48}... | collective-permute-start | bytes 393224 | tf_op jit(solution)/shard_map/ppermute | solution.py:49
  130.6 11.9 %collective-permute-start.26 = (bf16[512,512]{1,0:T(8,128)(2,1)S(1)}, bf16[512,512]{1,0:T(8,128)(2,1)S(1)}, u32[]{:S(2)}, u32[]{:S(2)}) collective-permute-start(bf16[512,512]{1,0:T(8,128)(2,1)S(1)} %copy-done.19), channel_id=1, source_target_pairs={{0,6},{1,7},{2,0},{3,1},{4,2},{5,3},{6,4},{7,5},{8,14},{9,15},{10,... | collective-permute-start | bytes 1572872 | tf_op jit(solution)/shard_map/ppermute | solution.py:36
  132.1 15.0 %collective-permute-start.3 = (bf16[256,512]{1,0:T(8,128)(2,1)S(1)}, bf16[256,512]{1,0:T(8,128)(2,1)S(1)}, u32[]{:S(2)}, u32[]{:S(2)}) collective-permute-start(bf16[256,512]{1,0:T(8,128)(2,1)S(1)} %slice.32), channel_id=1, source_target_pairs={{0,2},{1,3},{2,4},{3,5},{4,6},{5,7},{6,0},{7,1},{8,10},{9,11},{10,... | collective-permute-start | bytes 786440 | tf_op jit(solution)/shard_map/ppermute | solution.py:32
  136.3 15.3 %collective-permute-start.20 = (bf16[512,512]{1,0:T(8,128)(2,1)S(1)}, bf16[512,512]{1,0:T(8,128)(2,1)S(1)}, u32[]{:S(2)}, u32[]{:S(2)}) collective-permute-start(bf16[512,512]{1,0:T(8,128)(2,1)S(1)} %get-tuple-element.26), channel_id=1, source_target_pairs={{0,2},{1,3},{2,4},{3,5},{4,6},{5,7},{6,0},{7,1},{8,10},{9,11},{10,... | collective-permute-start | bytes 1572872 | tf_op jit(solution)/shard_map/ppermute | solution.py:32
  137.6 12.3 %collective-permute-start.4 = (bf16[256,512]{1,0:T(8,128)(2,1)S(1)}, bf16[256,512]{1,0:T(8,128)(2,1)S(1)}, u32[]{:S(2)}, u32[]{:S(2)}) collective-permute-start(bf16[256,512]{1,0:T(8,128)(2,1)S(1)} %slice.33), channel_id=1, source_target_pairs={{0,6},{1,7},{2,0},{3,1},{4,2},{5,3},{6,4},{7,5},{8,14},{9,15},{10,... | collective-permute-start | bytes 786440 | tf_op jit(solution)/shard_map/ppermute | solution.py:36
  142.6 28.2 %collective-permute-start.6 = (bf16[512,512]{1,0:T(8,128)(2,1)S(1)}, bf16[512,512]{1,0:T(8,128)(2,1)S(1)}, u32[]{:S(2)}, u32[]{:S(2)}) collective-permute-start(bf16[512,512]{1,0:T(8,128)(2,1)S(1)} %collective-permute-done.1.refs_4_.refs_16_), channel_id=1, source_target_pairs={{0,1},{1,0},{2,3},{3,2},{4,5},{5,4},{6,7},{7,6},{8,9},{9,8},{10,11... | collective-permute-start | bytes 1572872 | tf_op jit(solution)/shard_map/ppermute | solution.py:44
  147.0 24.9 %collective-permute-start.7 = (bf16[512,512]{1,0:T(8,128)(2,1)S(1)}, bf16[512,512]{1,0:T(8,128)(2,1)S(1)}, u32[]{:S(2)}, u32[]{:S(2)}) collective-permute-start(bf16[512,512]{1,0:T(8,128)(2,1)S(1)} %collective-permute-done.2.refs_5_.refs_17_), channel_id=1, source_target_pairs={{0,1},{1,0},{2,3},{3,2},{4,5},{5,4},{6,7},{7,6},{8,9},{9,8},{10,11... | collective-permute-start | bytes 1572872 | tf_op jit(solution)/shard_map/ppermute | solution.py:44
  147.1 20.7 %collective-permute-start.21 = (bf16[512,512]{1,0:T(8,128)(2,1)S(1)}, bf16[512,512]{1,0:T(8,128)(2,1)S(1)}, u32[]{:S(2)}, u32[]{:S(2)}) collective-permute-start(bf16[512,512]{1,0:T(8,128)(2,1)S(1)} %get-tuple-element.27), channel_id=1, source_target_pairs={{0,6},{1,7},{2,0},{3,1},{4,2},{5,3},{6,4},{7,5},{8,14},{9,15},{10,... | collective-permute-start | bytes 1572872 | tf_op jit(solution)/shard_map/ppermute | solution.py:36
  149.9 8.1 %collective-permute-start.27 = (bf16[256,512]{1,0:T(8,128)(2,1)S(1)}, bf16[256,512]{1,0:T(8,128)(2,1)S(1)}, u32[]{:S(2)}, u32[]{:S(2)}) collective-permute-start(bf16[256,512]{1,0:T(8,128)(2,1)S(1)} %slice_add_fusion.1), channel_id=1, source_target_pairs={{0,2},{1,3},{2,4},{3,5},{4,6},{5,7},{6,0},{7,1},{8,10},{9,11},{10,... | collective-permute-start | bytes 786440 | tf_op jit(solution)/shard_map/ppermute | solution.py:32
  151.6 14.9 %collective-permute-start.28 = (bf16[256,512]{1,0:T(8,128)(2,1)S(1)}, bf16[256,512]{1,0:T(8,128)(2,1)S(1)}, u32[]{:S(2)}, u32[]{:S(2)}) collective-permute-start(bf16[256,512]{1,0:T(8,128)(2,1)S(1)} %slice_add_fusion), channel_id=1, source_target_pairs={{0,6},{1,7},{2,0},{3,1},{4,2},{5,3},{6,4},{7,5},{8,14},{9,15},{10,... | collective-permute-start | bytes 786440 | tf_op jit(solution)/shard_map/ppermute | solution.py:36
  158.0 16.4 %collective-permute-start.8 = (bf16[256,512]{1,0:T(8,128)(2,1)S(1)}, bf16[256,512]{1,0:T(8,128)(2,1)S(1)}, u32[]{:S(2)}, u32[]{:S(2)}) collective-permute-start(bf16[256,512]{1,0:T(8,128)(2,1)S(1)} %collective-permute-done.3.refs_6_.refs_18_), channel_id=1, source_target_pairs={{0,1},{1,0},{2,3},{3,2},{4,5},{5,4},{6,7},{7,6},{8,9},{9,8},{10,11... | collective-permute-start | bytes 786440 | tf_op jit(solution)/shard_map/ppermute | solution.py:44
  167.9 28.7 %collective-permute-start.29 = (bf16[512,512]{1,0:T(8,128)(2,1)S(1)}, bf16[512,512]{1,0:T(8,128)(2,1)S(1)}, u32[]{:S(2)}, u32[]{:S(2)}) collective-permute-start(bf16[512,512]{1,0:T(8,128)(2,1)S(1)} %shard_map.134), channel_id=1, source_target_pairs={{0,8},{1,9},{2,10},{3,11},{4,12},{5,13},{6,14},{7,15},{8,0},{9,1},... | collective-permute-start | bytes 1572872 | tf_op jit(solution)/shard_map/ppermute | solution.py:40
  170.8 17.0 %collective-permute-start.22 = (bf16[256,512]{1,0:T(8,128)(2,1)S(1)}, bf16[256,512]{1,0:T(8,128)(2,1)S(1)}, u32[]{:S(2)}, u32[]{:S(2)}) collective-permute-start(bf16[256,512]{1,0:T(8,128)(2,1)S(1)} %slice_add_fusion.3), channel_id=1, source_target_pairs={{0,2},{1,3},{2,4},{3,5},{4,6},{5,7},{6,0},{7,1},{8,10},{9,11},{10,... | collective-permute-start | bytes 786440 | tf_op jit(solution)/shard_map/ppermute | solution.py:32
  171.9 15.9 %collective-permute-start.23 = (bf16[256,512]{1,0:T(8,128)(2,1)S(1)}, bf16[256,512]{1,0:T(8,128)(2,1)S(1)}, u32[]{:S(2)}, u32[]{:S(2)}) collective-permute-start(bf16[256,512]{1,0:T(8,128)(2,1)S(1)} %slice_add_fusion.2), channel_id=1, source_target_pairs={{0,6},{1,7},{2,0},{3,1},{4,2},{5,3},{6,4},{7,5},{8,14},{9,15},{10,... | collective-permute-start | bytes 786440 | tf_op jit(solution)/shard_map/ppermute | solution.py:36
  (31 other events, 406.7 us)
Sparse Core Ops, SparseCore 0:
  36.8 21.7 reduce-scatter.1
  61.2 52.3 all-reduce.1

commit v2 on v0

v2 whole, which is shorter than its diff:
```python
import jax
import jax.numpy as jnp
from jax import lax
from jax.experimental import pallas as pl
from jax.experimental.pallas import tpu as pltpu
from jax.sharding import PartitionSpec as P

epsilon = 1e-05
outer_decay = 0.9
outer_rate = 0.7

F32 = jnp.float32
BF16 = jnp.bfloat16
N_Y, N_ZH, N_CORE = 4, 2, 2
N_CHIP = N_Y * N_ZH
N_X, N_ZL = 4, 4
WEIGHT = 1e10
VMEM_LIMIT = 40 * 1024 * 1024


def dp_moves(dy=0, dz=0, dc=0):
    pairs = []
    for zh in range(N_ZH):
        for y in range(N_Y):
            for c in range(N_CORE):
                to = (((zh + dz) % N_ZH) * N_Y + (y + dy) % N_Y) * N_CORE + (c + dc) % N_CORE
                pairs.append(((zh * N_Y + y) * N_CORE + c, to))
    return pairs


def to_up(v):
    return lax.ppermute(v, "dp", dp_moves(dy=1))


def to_down(v):
    return lax.ppermute(v, "dp", dp_moves(dy=-1))


def to_far(v):
    return lax.ppermute(v, "dp", dp_moves(dz=1))


def to_core(v):
    return lax.ppermute(v, "dp", dp_moves(dc=1))


def swap_x(v, bit):
    return lax.ppermute(
        v, "replica", [(x * N_ZL + z, (x ^ bit) * N_ZL + z) for x in range(N_X) for z in range(N_ZL)]
    )


def swap_z(v, bit):
    return lax.ppermute(
        v, "replica", [(x * N_ZL + z, x * N_ZL + (z ^ bit)) for x in range(N_X) for z in range(N_ZL)]
    )


def core():
    return lax.rem(lax.axis_index("dp"), N_CORE)


def chip(side, dy):
    mine = lax.div(lax.axis_index("dp"), N_CORE)
    zh = lax.rem(lax.div(mine, N_Y) + side, N_ZH)
    return zh * N_Y + lax.rem(lax.rem(mine, N_Y) + dy, N_Y)


def place(side, dy):
    return chip(side, dy) * N_CORE + core()


def call(kernel, outs, ins, cost=1.0, vmem=VMEM_LIMIT, **kw):
    return pl.pallas_call(
        kernel,
        out_shape=outs,
        compiler_params=pltpu.CompilerParams(vmem_limit_bytes=vmem),
        cost_estimate=pl.CostEstimate(
            flops=int(cost * WEIGHT), bytes_accessed=0, transcendentals=0
        ),
        **kw,
    )(*ins)


HBM = pl.BlockSpec(memory_space=pltpu.HBM)
INSIDE = pl.BlockSpec(memory_space=pltpu.VMEM)


def full(shape):
    return pl.BlockSpec(shape, lambda j: (0,) * len(shape))


def block(index, size):
    return pl.ds(pl.multiple_of(index * size, size), size)


def dot_nt(a, b):
    return lax.dot_general(a, b, (((1,), (1,)), ((), ())), preferred_element_type=F32)


def dot(a, b):
    return jnp.dot(a, b, preferred_element_type=F32)


def identity(n):
    r = lax.broadcasted_iota(jnp.int32, (n, n), 0)
    c = lax.broadcasted_iota(jnp.int32, (n, n), 1)
    return jnp.where(r == c, 1.0, 0.0).astype(BF16)


def start_all(copies):
    for copy in copies:
        copy.start()
    return copies


ORDER = (2, 3, 1, 0)


def split_tokens(tokens, cot):
    t, d = tokens.shape
    f = cot.shape[1]
    steps = d // (2 * f)

    def kernel(tok, ct, sent, extra, ir_out, held, sems, out_sems):
        arrivals = start_all(
            [
                pltpu.make_async_copy(
                    tok.at[:, 2 * f * i : 2 * f * (i + 1)],
                    held.at[:, 2 * f * i : 2 * f * (i + 1)],
                    sems.at[i],
                )
                for i in range(steps)
            ]
        )
        away = 1 - core()
        leaving = []
        acc = jnp.zeros((t, 128), F32)
        for i in range(steps):
            arrivals[i].wait()
            copy = pltpu.make_async_copy(
                held.at[:, block(2 * i + away, f)],
                sent.at[:, i * f : (i + 1) * f],
                out_sems.at[i],
            )
            copy.start()
            leaving.append(copy)
            for n in range(2 * f * i, 2 * f * (i + 1), 128):
                v = held[:, n : n + 128].astype(F32)
                acc += v * v
        mean = jnp.sum(acc, axis=1, keepdims=True) / d
        ir = lax.rsqrt(jnp.broadcast_to(mean, (t, 128)) + epsilon)
        ir_out[...] = ir
        high = ir.astype(BF16).astype(F32)
        middle = (ir - high).astype(BF16).astype(F32)
        low = ir - high - middle
        lane = lax.broadcasted_iota(jnp.int32, (t, 128), 1)
        terms = jnp.where(lane == 0, high, jnp.where(lane == 1, middle, low))
        extra[:, :f] = ct[...]
        extra[:, f:] = terms.astype(BF16)
        for copy in leaving:
            copy.wait()

    return call(
        kernel,
        (
            jax.ShapeDtypeStruct((t, d // 2), BF16),
            jax.ShapeDtypeStruct((t, f + 128), BF16),
            jax.ShapeDtypeStruct((t, 128), F32),
        ),
        (tokens, cot),
        vmem=60 * 1024 * 1024,
        cost=3.2,
        in_specs=[HBM, INSIDE],
        out_specs=(HBM, INSIDE, INSIDE),
        scratch_shapes=[
            pltpu.VMEM((t, d), BF16),
            pltpu.SemaphoreType.DMA((steps,)),
            pltpu.SemaphoreType.DMA((steps,)),
        ],
    )


def partner_scale(extra, f):
    return sum(extra[:, f + i : f + i + 1].astype(F32) for i in range(3))


def partials(tokens, gains, cot, ir, other, extra, side):
    t, d = tokens.shape
    f = k = cot.shape[1]

    def kernel(tok, oth, gain, ct, irr, ext, *refs):
        hid_out, outs = refs[0], refs[1:5]
        xs, ys, hid, grads, cot_t, in_sems, out_sems = refs[5:]
        arrivals = []
        for i, dy in enumerate(ORDER):
            arrivals += start_all(
                [
                    pltpu.make_async_copy(
                        tok.at[:, block(place(side, dy), f)], xs.at[i], in_sems.at[0, i]
                    ),
                    pltpu.make_async_copy(
                        oth.at[:, block(chip(side, dy), f)], ys.at[i], in_sems.at[1, i]
                    ),
                ]
            )
        eye = identity(k)
        cot_t[:, :t] = dot_nt(eye, ct[...]).astype(BF16)
        cot_t[:, t:] = dot_nt(eye, ext[:, :k]).astype(BF16)
        own_scale = irr[:, 0:1]
        other_scale = partner_scale(ext, f)
        leaving = []
        for i, dy in enumerate(ORDER):
            g = gain[:, block(place(side, dy), f)]
            arrivals[2 * i].wait()
            arrivals[2 * i + 1].wait()
            cols = slice(i * f, (i + 1) * f)
            hid[:t, cols] = (xs[i].astype(F32) * own_scale * g).astype(BF16)
            hid[t:, cols] = (ys[i].astype(F32) * other_scale * g).astype(BF16)
            grads[i] = dot(cot_t[...], hid[:, cols]).astype(BF16)
            leaving += start_all(
                [
                    pltpu.make_async_copy(grads.at[i], outs[i], out_sems.at[0, i]),
                    pltpu.make_async_copy(hid.at[:, cols], hid_out.at[:, cols], out_sems.at[1, i]),
                ]
            )
        for copy in leaving:
            copy.wait()

    shape = jax.ShapeDtypeStruct((k, f), BF16)
    return call(
        kernel,
        (jax.ShapeDtypeStruct((2 * t, N_Y * f), BF16),) + (shape,) * 4,
        (tokens, other, gains, cot, ir, extra),
        cost=3.4,
        in_specs=[HBM, HBM] + [INSIDE] * 4,
        out_specs=(HBM,) * 5,
        scratch_shapes=[
            pltpu.VMEM((N_Y, t, f), BF16),
            pltpu.VMEM((N_Y, t, f), BF16),
            pltpu.VMEM((2 * t, N_Y * f), BF16),
            pltpu.VMEM((N_Y, k, f), BF16),
            pltpu.VMEM((k, 2 * t), BF16),
            pltpu.SemaphoreType.DMA((2, N_Y)),
            pltpu.SemaphoreType.DMA((2, N_Y)),
        ],
    )


def side_sum(own, from_down, from_up):
    def kernel(o, a, b, out):
        out[...] = (o[...].astype(F32) + a[...].astype(F32) + b[...].astype(F32)).astype(BF16)

    return call(kernel, jax.ShapeDtypeStruct(own.shape, BF16), (own, from_down, from_up), cost=1.0)


def final_sum(own, from_down, from_up, far, weight, gains):
    k, f = own.shape

    def kernel(o, a, b, fr, w, gain, out, gain_out):
        eye = identity(k)
        weight_t = dot_nt(eye, w[...])
        total = (o[...].astype(F32) + a[...].astype(F32)) + (b[...].astype(F32) + fr[...].astype(F32))
        out[...] = dot_nt(eye, total.astype(BF16)).astype(BF16)
        sums = jnp.sum(total * weight_t, axis=0, keepdims=True)
        gain_out[...] = (sums / gain[:, block(lax.axis_index("dp"), f)]).astype(BF16)

    return call(
        kernel,
        (jax.ShapeDtypeStruct((f, k), BF16), jax.ShapeDtypeStruct((1, f), BF16)),
        (own, from_down, from_up, far, weight, gains),
        cost=2.9,
    )


def project(hidden, weights, before=None, cot=None, extra=None):
    f, k = weights[0].shape
    t = hidden.shape[0] // 2
    last = before is not None

    def kernel(*refs):
        hid, ws = refs[0], refs[1:5]
        held, hs, sems = refs[-3:]
        arrivals = []
        for i in range(N_Y):
            arrivals += start_all(
                [
                    pltpu.make_async_copy(ws[i], held.at[i], sems.at[0, i]),
                    pltpu.make_async_copy(hid.at[:, i * f : (i + 1) * f], hs.at[i], sems.at[1, i]),
                ]
            )
        total = refs[5][...] if last else jnp.zeros((2 * t, k), F32)
        for i in range(N_Y):
            arrivals[2 * i].wait()
            arrivals[2 * i + 1].wait()
            total += dot(hs[i], held[i])
        if not last:
            refs[5][...] = total
            return
        ct, ext, mine, sent = refs[6:10]
        own = jnp.sum(total[:t] * ct[...].astype(F32), axis=1, keepdims=True)
        others = jnp.sum(total[t:] * ext[:, :k].astype(F32), axis=1, keepdims=True)
        lane = lax.broadcasted_iota(jnp.int32, (t, 128), 1)
        mine[:, :k] = total[:t]
        mine[:, k:] = jnp.where(lane == 0, own, others)
        sent[:, :k] = total[t:]
        sent[:, k:] = jnp.where(lane == 0, others, own)

    ins = (hidden,) + tuple(weights)
    specs = [HBM] * 5
    if last:
        ins += (before, cot, extra)
        specs += [INSIDE] * 3
        outs = (jax.ShapeDtypeStruct((t, k + 128), F32),) * 2
        out_specs = (INSIDE,) * 2
    else:
        outs = jax.ShapeDtypeStruct((2 * t, k), F32)
        out_specs = INSIDE
    return call(
        kernel,
        outs,
        ins,
        cost=2.5,
        in_specs=specs,
        out_specs=out_specs,
        scratch_shapes=[
            pltpu.VMEM((N_Y, f, k), BF16),
            pltpu.VMEM((N_Y, 2 * t, f), BF16),
            pltpu.SemaphoreType.DMA((2, N_Y)),
        ],
    )


def blocks_of_chip():
    return [(side, dy) for side in range(N_ZH) for dy in ORDER]


def backward_scratch(t, f, k):
    return [
        pltpu.VMEM((N_CHIP, f, k), BF16),
        pltpu.VMEM((N_CHIP, t, f), BF16),
        pltpu.VMEM((N_CHIP, t, f), BF16),
        pltpu.SemaphoreType.DMA((2, N_CHIP)),
        pltpu.SemaphoreType.DMA((N_CHIP,)),
    ]


def token_gradient(x_from, ws, out_to, gain, ct, scale, mean, scratch):
    held, xs, results, sems, out_sems = scratch
    arrivals = []
    for i, w in enumerate(ws):
        arrivals += start_all(
            [
                pltpu.make_async_copy(w, held.at[i], sems.at[0, i]),
                pltpu.make_async_copy(x_from(i), xs.at[i], sems.at[1, i]),
            ]
        )
    shift = scale * scale * mean
    leaving = []
    for i, (side, dy) in enumerate(blocks_of_chip()):
        arrivals[2 * i].wait()
        arrivals[2 * i + 1].wait()
        g = gain[:, block(place(side, dy), held.shape[1])]
        grad = dot_nt(ct, held[i])
        results[i] = (scale * (grad * g) - xs[i].astype(F32) * shift).astype(BF16)
        leaving += start_all([pltpu.make_async_copy(results.at[i], out_to(i), out_sems.at[i])])
    for copy in leaving:
        copy.wait()


def backward_other(other, extra, gains, mine, arrived, weights):
    t = other.shape[0]
    f = k = extra.shape[1] - 128
    d = gains.shape[1]
    where = blocks_of_chip()

    def kernel(*refs):
        oth, gain, ext, mn, arr = refs[:5]
        ws = refs[5:13]
        out, keys, mean = refs[13:16]
        keys[...] = (mn[:, :k] + arr[:, :k]).astype(BF16)
        means = (mn[:, k:] + arr[:, k:]) / d
        mean[...] = means
        token_gradient(
            lambda i: oth.at[:, block(chip(*where[i]), f)],
            ws,
            lambda i: out.at[:, i * f : (i + 1) * f],
            gain,
            ext[:, :k],
            partner_scale(ext, f),
            means[:, 1:2],
            refs[16:],
        )

    return call(
        kernel,
        (
            jax.ShapeDtypeStruct((t, d // 2), BF16),
            jax.ShapeDtypeStruct((t, k), BF16),
            jax.ShapeDtypeStruct((t, 128), F32),
        ),
        (other, gains, extra, mine, arrived) + tuple(weights),
        cost=5.5,
        in_specs=[HBM] + [INSIDE] * 4 + [HBM] * 8,
        out_specs=(HBM, INSIDE, INSIDE),
        scratch_shapes=backward_scratch(t, f, k),
    )


def backward_own(tokens, gains, ir, cot, mean, weights):
    t, d = tokens.shape
    f = k = cot.shape[1]
    where = blocks_of_chip()

    def kernel(*refs):
        tok, gain, irr, ct, mn = refs[:5]
        ws = refs[5:13]
        out = refs[13]
        token_gradient(
            lambda i: tok.at[:, block(place(*where[i]), f)],
            ws,
            lambda i: out.at[:, block(place(*where[i]), f)],
            gain,
            ct[...],
            irr[:, 0:1],
            mn[:, 0:1],
            refs[14:],
        )

    return call(
        kernel,
        jax.ShapeDtypeStruct((t, d), BF16),
        (tokens, gains, ir, cot, mean) + tuple(weights),
        cost=4.7,
        in_specs=[HBM] + [INSIDE] * 4 + [HBM] * 8,
        out_specs=HBM,
        scratch_shapes=backward_scratch(t, f, k),
    )


def fill_in(token_grad, arrived):
    t = arrived.shape[0]
    f = arrived.shape[1] // N_CHIP
    where = blocks_of_chip()

    def kernel(_, arr, out, held, sems):
        away = 1 - core()
        arrivals = start_all(
            [
                pltpu.make_async_copy(arr.at[:, i * f : (i + 1) * f], held.at[i], sems.at[0, i])
                for i in range(N_CHIP)
            ]
        )
        leaving = []
        for i in range(N_CHIP):
            arrivals[i].wait()
            to = out.at[:, block(chip(*where[i]) * N_CORE + away, f)]
            leaving += start_all([pltpu.make_async_copy(held.at[i], to, sems.at[1, i])])
        for copy in leaving:
            copy.wait()

    return call(
        kernel,
        jax.ShapeDtypeStruct(token_grad.shape, token_grad.dtype),
        (token_grad, arrived),
        cost=1.4,
        in_specs=[HBM, HBM],
        out_specs=HBM,
        input_output_aliases={0: 0},
        scratch_shapes=[
            pltpu.VMEM((N_CHIP, t, f), BF16),
            pltpu.SemaphoreType.DMA((2, N_CHIP)),
        ],
    )


def x_bit(bit):
    return lax.rem(lax.div(lax.axis_index("replica"), N_ZL * bit), 2)


def scaled_halves(quantized, exponents):
    n, cols = quantized.shape
    h = n // 2
    nb = exponents.shape[1]
    width = cols // nb

    def kernel(q, e, keep, send):
        for out, half in ((keep, x_bit(1)), (send, 1 - x_bit(1))):
            rows = pl.ds(pl.multiple_of(half * h, h), h)
            scale = jnp.exp2(e[rows, :].astype(F32))
            for b in range(nb):
                lanes = slice(b * width, (b + 1) * width)
                out[:, lanes] = (q[rows, lanes].astype(F32) * scale[:, b : b + 1]).astype(BF16)

    return call(
        kernel,
        (jax.ShapeDtypeStruct((h, cols), BF16),) * 2,
        (quantized, exponents),
    )


def outer_update(average, momentum, outer_params):
    new_momentum = outer_decay * momentum + average
    new_params = outer_params - outer_rate * (average + outer_decay * new_momentum)
    return (new_momentum, new_params)


def outer_step(half, other, momentum, outer_params):
    n, cols = momentum.shape
    h = n // 2

    def kernel(a, b, m, p, new_m, new_p):
        j = pl.program_id(0)

        def update(total):
            average = total[...].astype(F32) / (N_X * N_ZL)
            new_m[...], new_p[...] = outer_update(average, m[...], p[...])

        pl.when(j == 0)(lambda: update(a))
        pl.when(j == 1)(lambda: update(b))

    def half_of(j):
        return (lax.rem(x_bit(1) + j, 2), 0)

    spec = pl.BlockSpec((h, cols), half_of)
    return call(
        kernel,
        (jax.ShapeDtypeStruct((n, cols), F32),) * 2,
        (half, other, momentum, outer_params),
        cost=2.0,
        grid=(2,),
        in_specs=[full((h, cols)), full((h, cols)), spec, spec],
        out_specs=(spec, spec),
    )


def after(values, *events):
    held = lax.optimization_barrier(tuple(values) + events)
    return held[: len(values)]


def shards(
    tokens, norm_gain, key_weight, key_cotangent, quantized, scale_exponent, momentum, outer_params
):
    gains = norm_gain
    cot = key_cotangent
    weight = key_weight[0]

    n_down = to_up(weight)
    n_up = to_down(weight)
    far_weight = to_far(weight)

    sent, extra_sent, ir = split_tokens(tokens, cot)
    other = to_core(sent)
    extra = to_core(extra_sent)

    n_down, n_up, quant, exponents = after((n_down, n_up, quantized[0], scale_exponent[0]), ir)
    keep, send = scaled_halves(quant, exponents)
    x1 = swap_x(send, 1)
    n_opposite = to_up(n_down)

    other, extra = after((other, extra), keep)
    hidden_far, f_opposite, f_minus, f_plus, f_own = partials(
        tokens, gains, cot, ir, other, extra, 1
    )
    f_step = to_down(f_opposite)
    f_from_down = to_up(f_plus)

    other, extra = after((other, extra), f_own)
    hidden_near, g_opposite, g_minus, g_plus, g_own = partials(
        tokens, gains, cot, ir, other, extra, 0
    )
    keep, x1 = after((keep, x1), g_own)
    half = keep + x1
    q = half.shape[0] // 2
    mine = x_bit(2) * q
    part = lax.dynamic_slice_in_dim(half, mine, q)
    x2 = swap_x(lax.dynamic_slice_in_dim(half, q - mine, q), 2)

    near_rows = (n_opposite, n_down, n_up, weight)
    *near_rows, hidden_near = after((*near_rows, hidden_near), part)
    near_keys = project(hidden_near, near_rows)

    f_minus, f_step, near_keys = after((f_minus, f_step), near_keys) + (near_keys,)
    f_minus = f_minus + f_step
    f_from_up = to_down(f_minus)
    part, x2 = after((part, x2), f_minus)
    part = part + x2
    z1 = swap_z(part, 1)

    (far_weight,) = after((far_weight,), part)
    a_down = to_up(far_weight)
    a_up = to_down(far_weight)
    part, z1 = after((part, z1), far_weight)
    part = part + z1
    z2 = swap_z(part, 2)

    f_own, f_from_down, f_from_up = after((f_own, f_from_down, f_from_up), part)
    f_total = side_sum(f_own, f_from_down, f_from_up)
    far_sum = to_far(f_total)
    (a_down,) = after((a_down,), f_total)
    a_opposite = to_up(a_down)
    part, z2 = after((part, z2), a_down)
    part = part + z2
    x3 = swap_x(part, 2)

    g_opposite, a_up = after((g_opposite, a_up), part)
    g_step = to_down(g_opposite)
    part, x3 = after((part, x3), a_up)
    pair = jnp.concatenate([part, x3])
    half = jnp.where(x_bit(2) == 0, pair, jnp.roll(pair, q, axis=0))
    x4 = swap_x(half, 1)
    g_plus, a_opposite = after((g_plus, a_opposite), half)
    g_from_down = to_up(g_plus)

    far_rows = (a_opposite, a_down, a_up, far_weight)
    keys_mine, keys_sent = project(hidden_far, far_rows, near_keys, cot, extra)
    arrived = to_core(keys_sent)
    g_minus, g_step = after((g_minus, g_step), keys_sent)
    g_minus = g_minus + g_step
    g_from_up = to_down(g_minus)
    half, x4 = after((half, x4), g_minus)
    new_momentum, new_params = outer_step(half, x4, momentum, outer_params)
    arrived, keys_mine = after((arrived, keys_mine), new_params)
    rows = tuple(near_rows) + tuple(far_rows)
    grad_sent, keys, mean = backward_other(other, extra, gains, keys_mine, arrived, rows)
    grad_arrived = to_core(grad_sent)
    (mean,) = after((mean,), grad_sent)
    token_grad = backward_own(tokens, gains, ir, cot, mean, rows)
    token_grad = fill_in(token_grad, grad_arrived)
    g_from_up, far_sum, token_grad = after((g_from_up, far_sum), token_grad) + (token_grad,)
    weight_grad, gain_grad = final_sum(g_own, g_from_down, g_from_up, far_sum, weight, gains)
    return (keys, token_grad, weight_grad[None], gain_grad, new_momentum, new_params)


def solution(mesh):
    return jax.shard_map(
        shards,
        mesh=mesh,
        in_specs=(
            P(("replica", "dp"), None),
            P("replica", None),
            P("replica", "dp", None),
            P(("replica", "dp"), None),
            P("replica", "dp", None),
            P("replica", "dp", None),
            P("dp", None),
            P("dp", None),
        ),
        out_specs=(
            P(("replica", "dp"), None),
            P(("replica", "dp"), None),
            P("replica", "dp", None),
            P("replica", "dp"),
            P("dp", None),
            P("dp", None),
        ),
        check_vma=False,
    )
```

time: 384 us -> 130 us (0.34); the launches traced: 379 us -> 129 us
  waiting for transfers between devices: 231 us -> 24.4 us
  blocking collectives: 88.1 us -> 0 us
  starting transfers between devices: 0.12 us -> 60 us
  Pallas kernels: 0 us -> 33.1 us
  matrix products: 28 us -> 0 us
  between operations: 16.2 us -> 1.01 us
  other arithmetic: 12.2 us -> 2.25 us
  local copies, waits for them, and re-layouts: 3.19 us -> 8.68 us
    psum x1 -> x0, waiting for transfers between devices: 231 us -> none  [shards(): total = lax.psum(delta.astype(jnp.bfloat16), 'replica').astype(jnp.float32)]
    unnamed x1 -> x0, blocking collectives: 88.1 us -> none
    ppermute x0 -> x24, starting transfers between devices: none -> 60 us  [the longest x4 24.1 us: to_core(): return lax.ppermute(v, 'dp', dp_moves(dc=1))]
    pallas_call x0 -> x12, Pallas kernels: none -> 33.1 us  [call(): pl.pallas_call(kernel, out_shape=outs, compiler_params=pltpu.CompilerPara...]
    dot_general x3 -> x0, matrix products: 28 us -> none  [the longest x1 12 us: shards(): lax.dot_general(key_cotangent, lax.all_gather(weight_rows, 'dp', axis=0,...]
    ppermute x0 -> x24, waiting for transfers between devices: none -> 24.4 us  [the longest x6 10.2 us: to_up(): return lax.ppermute(v, 'dp', dp_moves(dy=1))]
    unnamed x16 -> x51, local copies, waits for them, and re-layouts: 1.85 us -> 8.65 us
    convert_element_type x2 -> x0, other arithmetic: 5.61 us -> none  [the longest x1 3.33 us: shards(): token_grad.astype(jnp.bfloat16)]
  transfers between devices with their start and end apart: 3 -> 24, of which waited for: 1 -> 8; matrix products, arithmetic and copies ran while one was open for 10% -> 2% of each run, Pallas kernels for 0% -> 20%
where the time goes in v2:
time: 130 us; the launch traced here: 129 us
  starting transfers between devices  60 us (46%)
  Pallas kernels  33.1 us (25%)
  waiting for transfers between devices  24.4 us (19%)
  local copies, waits for them, and re-layouts  8.68 us (7%)
  other arithmetic  2.25 us (2%)
    pallas_call x12, Pallas kernels, call(): pl.pallas_call(kernel, out_shape=outs, compiler_params=pltpu.CompilerPara...  33.1 us
    ppermute x4, starting transfers between devices, to_core(): return lax.ppermute(v, 'dp', dp_moves(dc=1))  24.1 us
    ppermute x2, starting transfers between devices, to_far(): return lax.ppermute(v, 'dp', dp_moves(dz=1))  11.8 us
    ppermute x6, waiting for transfers between devices, to_up(): return lax.ppermute(v, 'dp', dp_moves(dy=1))  10.2 us
    ppermute x6, starting transfers between devices, to_down(): return lax.ppermute(v, 'dp', dp_moves(dy=-1))  9.3 us
    unnamed x51, local copies, waits for them, and re-layouts  8.65 us
    ppermute x4, starting transfers between devices, swap_x(): lax.ppermute(v, 'replica', [(x * N_ZL + z, (x ^ bit) * N_ZL + z) for x in...  6.75 us
    ppermute x6, waiting for transfers between devices, to_down(): return lax.ppermute(v, 'dp', dp_moves(dy=-1))  6.38 us
  transfers between devices with their start and end apart: 24, of which 8 were waited for; matrix products, arithmetic and copies ran while one was open for 2% of the time, Pallas kernels for 20%

profile of v2, /device:TPU:1, one launch (start us, length us, event | category | flops | bytes accessed | tf_op | source)
XLA Modules:
  0.0 129.5 jit_solution(10738726236004836698)
XLA Ops:
  0.7 5.1 %shard_map.127 = (bf16[256,4096]{1,0:T(8,128)(2,1)}, bf16[256,640]{1,0:T(8,128)(2,1)}, f32[256,128]{1,0:T(8,128)}) custom-call(bf16[256,8192]{1,0:T(8,128)(2,1)} %refs_0_.1, bf16[256,512]{1,0:T(8,128)(2,1)} %refs_3_.1), custom_call_target="tpu_custom_call" | custom-call | flops 32000000000 | tf_op jit(solution)/shard_map/pallas_call | solution.py:74
  5.7 3.3 %collective-permute-start = (bf16[256,4096]{1,0:T(8,128)(2,1)}, bf16[256,4096]{1,0:T(8,128)(2,1)S(1)}, u32[]{:S(2)}, u32[]{:S(2)}) collective-permute-start(bf16[256,4096]{1,0:T(8,128)(2,1)} %get-tuple-element.73), channel_id=1, source_target_pairs={{0,1},{1,0},{2,3},{3,2},{4,5},{5,4},{6,7},{7,6},{8,9},{9,8},{10,11... | collective-permute-start | bytes 6291464 | tf_op jit(solution)/shard_map/ppermute | solution.py:44
  10.6 6.4 %collective-permute-start.4 = (bf16[512,512]{1,0:T(8,128)(2,1)S(1)}, bf16[512,512]{1,0:T(8,128)(2,1)}, u32[]{:S(2)}, u32[]{:S(2)}) collective-permute-start(bf16[512,512]{1,0:T(8,128)(2,1)S(1)} %bitcast.8), channel_id=1, source_target_pairs={{0,8},{1,9},{2,10},{3,11},{4,12},{5,13},{6,14},{7,15},{8,0},{9,1},... | collective-permute-start | bytes 1572872 | tf_op jit(solution)/shard_map/ppermute | solution.py:40
  17.8 4.9 %collective-permute-done.3.refs_3_.refs_7_ = bf16[512,512]{1,0:T(8,128)(2,1)} collective-permute-done((bf16[512,512]{1,0:T(8,128)(2,1)S(1)}, bf16[512,512]{1,0:T(8,128)(2,1)}, u32[]{:S(2)}, u32[]{:S(2)}) %collective-permute-start.3) | collective-permute-done | bytes 524320 | tf_op jit(solution)/shard_map/ppermute | solution.py:36
  22.7 1.9 %collective-permute-done.2.refs_2_.refs_6_ = bf16[512,512]{1,0:T(8,128)(2,1)} collective-permute-done((bf16[512,512]{1,0:T(8,128)(2,1)S(1)}, bf16[512,512]{1,0:T(8,128)(2,1)}, u32[]{:S(2)}, u32[]{:S(2)}) %collective-permute-start.2) | collective-permute-done | bytes 524320 | tf_op jit(solution)/shard_map/ppermute | solution.py:32
  28.0 3.5 %shard_map.129 = (bf16[512,2048]{1,0:T(8,128)(2,1)S(1)}, bf16[512,512]{1,0:T(8,128)(2,1)S(1)}, bf16[512,512]{1,0:T(8,128)(2,1)S(1)}, bf16[512,512]{1,0:T(8,128)(2,1)S(1)}, bf16[512,512]{1,0:T(8,128)(2,1)S(1)}) custom-call(bf16[256,8192]{1,0:T(8,128)(2,1)S(1)} %copy-done, bf16[256,4096]{1,0:T(8,128)(2,1)S(1)} %collective-permute-done.oth.refs_0_, ...), custom_call_target="tpu_custom_call" | custom-call | flops 33999998976 | tf_op jit(solution)/shard_map/pallas_call | solution.py:74
  31.5 1.3 %copy-done.16 = bf16[512,2048]{1,0:T(8,128)(2,1)} copy-done((bf16[512,2048]{1,0:T(8,128)(2,1)}, bf16[512,2048]{1,0:T(8,128)(2,1)S(1)}, u32[]{:S(2)}) %copy-start.16) | copy-done | bytes 2097176
  32.9 2.2 %collective-permute-start.7 = (bf16[512,512]{1,0:T(8,128)(2,1)S(1)}, bf16[512,512]{1,0:T(8,128)(2,1)S(1)}, u32[]{:S(2)}, u32[]{:S(2)}) collective-permute-start(bf16[512,512]{1,0:T(8,128)(2,1)S(1)} %get-tuple-element.91), channel_id=1, source_target_pairs={{0,6},{1,7},{2,0},{3,1},{4,2},{5,3},{6,4},{7,5},{8,14},{9,15},{10,... | collective-permute-start | bytes 1572872 | tf_op jit(solution)/shard_map/ppermute | solution.py:36
  35.0 3.5 %shard_map.130 = (bf16[512,2048]{1,0:T(8,128)(2,1)S(1)}, bf16[512,512]{1,0:T(8,128)(2,1)S(1)}, bf16[512,512]{1,0:T(8,128)(2,1)S(1)}, bf16[512,512]{1,0:T(8,128)(2,1)S(1)}, bf16[512,512]{1,0:T(8,128)(2,1)S(1)}) custom-call(bf16[256,8192]{1,0:T(8,128)(2,1)S(1)} %copy-done, bf16[256,4096]{1,0:T(8,128)(2,1)S(1)} %collective-permute-done.oth.refs_0_, ...), custom_call_target="tpu_custom_call" | custom-call | flops 33999998976 | tf_op jit(solution)/shard_map/pallas_call | solution.py:74
  39.5 1.4 %collective-permute-done.8.refs_1_.refs_5_ = bf16[512,512]{1,0:T(8,128)(2,1)S(1)} collective-permute-done((bf16[512,512]{1,0:T(8,128)(2,1)}, bf16[512,512]{1,0:T(8,128)(2,1)S(1)}, u32[]{:S(2)}, u32[]{:S(2)}) %collective-permute-start.8) | collective-permute-done | bytes 524320 | tf_op jit(solution)/shard_map/ppermute | solution.py:32
  40.8 2.7 %shard_map.131.refs_5_ = f32[512,512]{1,0:T(8,128)S(1)} custom-call(bf16[512,2048]{1,0:T(8,128)(2,1)S(1)} %get-tuple-element.95.refs_0_, bf16[512,512]{1,0:T(8,128)(2,1)S(1)} %collective-permute-done.8.refs_1_.refs_5_, bf16[512,512]{1,0:T(8,128)(2,1)} %collective-permute-done.2.refs_2_.refs_6_, bf16[512,512]{1,0:T(8,128)(2,1)} %collective-permute-done.3.refs_3_.refs_7_, ...), custom_call_target="tpu_custom_call" | custom-call | flops 24999999488 | tf_op jit(solution)/shard_map/pallas_call | solution.py:74
  43.6 1.5 %collective-permute-done.7 = bf16[512,512]{1,0:T(8,128)(2,1)S(1)} collective-permute-done((bf16[512,512]{1,0:T(8,128)(2,1)S(1)}, bf16[512,512]{1,0:T(8,128)(2,1)S(1)}, u32[]{:S(2)}, u32[]{:S(2)}) %collective-permute-start.7) | collective-permute-done | bytes 524320 | tf_op jit(solution)/shard_map/ppermute | solution.py:36
  45.2 2.9 %collective-permute-start.11 = (bf16[512,512]{1,0:T(8,128)(2,1)S(1)}, bf16[512,512]{1,0:T(8,128)(2,1)S(1)}, u32[]{:S(2)}, u32[]{:S(2)}) collective-permute-start(bf16[512,512]{1,0:T(8,128)(2,1)S(1)} %add.28), channel_id=1, source_target_pairs={{0,6},{1,7},{2,0},{3,1},{4,2},{5,3},{6,4},{7,5},{8,14},{9,15},{10,... | collective-permute-start | bytes 1572872 | tf_op jit(solution)/shard_map/ppermute | solution.py:36
  48.1 2.5 %collective-permute-start.6 = (bf16[128,512]{1,0:T(8,128)(2,1)S(1)}, bf16[128,512]{1,0:T(8,128)(2,1)S(1)}, u32[]{:S(2)}, u32[]{:S(2)}) collective-permute-start(bf16[128,512]{1,0:T(8,128)(2,1)S(1)} %get-tuple-element.140), channel_id=1, source_target_pairs={{0,128},{16,144},{32,160},{48,176},{64,192},{80,208},{96,224},{112... | collective-permute-start | bytes 393224 | tf_op jit(solution)/shard_map/ppermute | solution.py:48
  50.6 2.9 %collective-permute-done.6 = bf16[128,512]{1,0:T(8,128)(2,1)S(1)} collective-permute-done((bf16[128,512]{1,0:T(8,128)(2,1)S(1)}, bf16[128,512]{1,0:T(8,128)(2,1)S(1)}, u32[]{:S(2)}, u32[]{:S(2)}) %collective-permute-start.6) | collective-permute-done | bytes 131104 | tf_op jit(solution)/shard_map/ppermute | solution.py:48
  53.5 1.7 %collective-permute-start.12 = (bf16[128,512]{1,0:T(8,128)(2,1)S(1)}, bf16[128,512]{1,0:T(8,128)(2,1)S(1)}, u32[]{:S(2)}, u32[]{:S(2)}) collective-permute-start(bf16[128,512]{1,0:T(8,128)(2,1)S(1)} %add.29), channel_id=1, source_target_pairs={{0,16},{16,0},{32,48},{48,32},{64,80},{80,64},{96,112},{112,96},{1... | collective-permute-start | bytes 393224 | tf_op jit(solution)/shard_map/ppermute | solution.py:54
  55.3 1.4 %collective-permute-start.9 = (bf16[512,512]{1,0:T(8,128)(2,1)}, bf16[512,512]{1,0:T(8,128)(2,1)}, u32[]{:S(2)}, u32[]{:S(2)}) collective-permute-start(bf16[512,512]{1,0:T(8,128)(2,1)} %collective-permute-done.4.refs_4_.refs_12_), channel_id=1, source_target_pairs={{0,2},{1,3},{2,4},{3,5},{4,6},{5,7},{6,0},{7,1},{8,10},{9,11},{10,... | collective-permute-start | bytes 1572872 | tf_op jit(solution)/shard_map/ppermute | solution.py:32
  58.9 6.9 %collective-permute-done.9.refs_2_.refs_10_ = bf16[512,512]{1,0:T(8,128)(2,1)} collective-permute-done((bf16[512,512]{1,0:T(8,128)(2,1)}, bf16[512,512]{1,0:T(8,128)(2,1)}, u32[]{:S(2)}, u32[]{:S(2)}) %collective-permute-start.9) | collective-permute-done | bytes 524320 | tf_op jit(solution)/shard_map/ppermute | solution.py:32
  65.9 3.0 %collective-permute-start.14 = (bf16[128,512]{1,0:T(8,128)(2,1)S(1)}, bf16[128,512]{1,0:T(8,128)(2,1)S(1)}, u32[]{:S(2)}, u32[]{:S(2)}) collective-permute-start(bf16[128,512]{1,0:T(8,128)(2,1)S(1)} %add.30), channel_id=1, source_target_pairs={{0,32},{16,48},{32,0},{48,16},{64,96},{80,112},{96,64},{112,80},{1... | collective-permute-start | bytes 393224 | tf_op jit(solution)/shard_map/ppermute | solution.py:54
  68.9 3.8 %collective-permute-done.14 = bf16[128,512]{1,0:T(8,128)(2,1)S(1)} collective-permute-done((bf16[128,512]{1,0:T(8,128)(2,1)S(1)}, bf16[128,512]{1,0:T(8,128)(2,1)S(1)}, u32[]{:S(2)}, u32[]{:S(2)}) %collective-permute-start.14) | collective-permute-done | bytes 131104 | tf_op jit(solution)/shard_map/ppermute | solution.py:54
  73.3 2.9 %collective-permute-start.15 = (bf16[128,512]{1,0:T(8,128)(2,1)}, bf16[128,512]{1,0:T(8,128)(2,1)}, u32[]{:S(2)}, u32[]{:S(2)}) collective-permute-start(bf16[128,512]{1,0:T(8,128)(2,1)} %add.31), channel_id=1, source_target_pairs={{0,128},{16,144},{32,160},{48,176},{64,192},{80,208},{96,224},{112... | collective-permute-start | bytes 393224 | tf_op jit(solution)/shard_map/ppermute | solution.py:48
  76.2 5.4 %collective-permute-start.23 = (bf16[512,512]{1,0:T(8,128)(2,1)}, bf16[512,512]{1,0:T(8,128)(2,1)}, u32[]{:S(2)}, u32[]{:S(2)}) collective-permute-start(bf16[512,512]{1,0:T(8,128)(2,1)} %copy-done.11), channel_id=1, source_target_pairs={{0,8},{1,9},{2,10},{3,11},{4,12},{5,13},{6,14},{7,15},{8,0},{9,1},... | collective-permute-start | bytes 1572872 | tf_op jit(solution)/shard_map/ppermute | solution.py:40
  81.6 3.0 %collective-permute-start.19 = (bf16[512,512]{1,0:T(8,128)(2,1)}, bf16[512,512]{1,0:T(8,128)(2,1)S(1)}, u32[]{:S(2)}, u32[]{:S(2)}) collective-permute-start(bf16[512,512]{1,0:T(8,128)(2,1)} %copy-done.10), channel_id=1, source_target_pairs={{0,6},{1,7},{2,0},{3,1},{4,2},{5,3},{6,4},{7,5},{8,14},{9,15},{10,... | collective-permute-start | bytes 1572872 | tf_op jit(solution)/shard_map/ppermute | solution.py:36
  86.9 1.6 %copy-done.17 = bf16[512,2048]{1,0:T(8,128)(2,1)S(1)} copy-done((bf16[512,2048]{1,0:T(8,128)(2,1)S(1)}, bf16[512,2048]{1,0:T(8,128)(2,1)}, u32[]{:S(2)}) %copy-start.17) | copy-done | bytes 2097176
  89.7 2.8 %shard_map.133 = (f32[256,640]{1,0:T(8,128)S(1)}, f32[256,640]{1,0:T(8,128)S(1)}) custom-call(bf16[512,2048]{1,0:T(8,128)(2,1)S(1)} %copy-done.17, bf16[512,512]{1,0:T(8,128)(2,1)} %collective-permute-done.13.refs_1_.refs_9_, bf16[512,512]{1,0:T(8,128)(2,1)} %collective-permute-done.9.refs_2_.refs_10_, ...), custom_call_target="tpu_custom_call" | custom-call | flops 24999999488 | tf_op jit(solution)/shard_map/pallas_call | solution.py:74
  92.5 19.2 %collective-permute-start.17 = (f32[256,640]{1,0:T(8,128)S(1)}, f32[256,640]{1,0:T(8,128)S(1)}, u32[]{:S(2)}, u32[]{:S(2)}) collective-permute-start(f32[256,640]{1,0:T(8,128)S(1)} %get-tuple-element.119), channel_id=1, source_target_pairs={{0,1},{1,0},{2,3},{3,2},{4,5},{5,4},{6,7},{7,6},{8,9},{9,8},{10,11... | collective-permute-start | bytes 1966088 | tf_op jit(solution)/shard_map/ppermute | solution.py:44
  111.9 1.4 %collective-permute-start.21 = (bf16[512,512]{1,0:T(8,128)(2,1)S(1)}, bf16[512,512]{1,0:T(8,128)(2,1)S(1)}, u32[]{:S(2)}, u32[]{:S(2)}) collective-permute-start(bf16[512,512]{1,0:T(8,128)(2,1)S(1)} %copy-done.9), channel_id=1, source_target_pairs={{0,2},{1,3},{2,4},{3,5},{4,6},{5,7},{6,0},{7,1},{8,10},{9,11},{10,... | collective-permute-start | bytes 1572872 | tf_op jit(solution)/shard_map/ppermute | solution.py:32
  113.4 1.5 %shard_map.134 = (f32[512,512]{1,0:T(8,128)}, f32[512,512]{1,0:T(8,128)}) custom-call(bf16[256,512]{1,0:T(8,128)(2,1)S(1)} %maximum_select_fusion.a, bf16[256,512]{1,0:T(8,128)(2,1)S(1)} %collective-permute-done.18.b, f32[512,512]{1,0:T(8,128)S(1)} %copy-done.3, f32[512,512]{1,0:T(8,128)S(1)} %copy-done.4), custom_call_target="tpu_custom_call" | custom-call | flops 20000000000 | tf_op jit(solution)/shard_map/pallas_call | solution.py:74
  114.9 4.8 %shard_map.135 = (bf16[256,4096]{1,0:T(8,128)(2,1)S(1)}, bf16[256,512]{1,0:T(8,128)(2,1)}, f32[256,128]{1,0:T(8,128)S(1)}) custom-call(bf16[256,4096]{1,0:T(8,128)(2,1)S(1)} %collective-permute-done.oth.refs_0_, f32[1,8192]{1,0:T(1,128)S(1)} %copy-done.15, bf16[256,640]{1,0:T(8,128)(2,1)S(1)} %collective-permute-done.1.ext.refs_7_.refs_2_, ...), custom_call_target="tpu_custom_call" | custom-call | flops 54999998464 | tf_op jit(solution)/shard_map/pallas_call | solution.py:74
  120.7 4.5 %shard_map.136._ = bf16[256,8192]{1,0:T(8,128)(2,1)} custom-call(bf16[256,8192]{1,0:T(8,128)(2,1)S(1)} %copy-done.1, f32[1,8192]{1,0:T(1,128)S(1)} %copy-done.15, f32[256,128]{1,0:T(8,128)S(1)} %copy-done.23, bf16[256,512]{1,0:T(8,128)(2,1)S(1)} %copy-done.14, f32[256,128]{1,0:T(8,128)S(1)} %get-tuple-element.133.refs_4_, bf16[512,512]{1,0:T(8,128)(2,1)S(1)} %copy-done.7, ...), custom_call_target="tpu_custom_call" | custom-call | flops 46999998464 | tf_op jit(solution)/shard_map/pallas_call | solution.py:74
  125.2 1.6 %shard_map.137 = bf16[256,8192]{1,0:T(8,128)(2,1)} custom-call(bf16[256,8192]{1,0:T(8,128)(2,1)} %shard_map.136._, bf16[256,4096]{1,0:T(8,128)(2,1)S(1)} %collective-permute-done.20.arr), custom_call_target="tpu_custom_call", output_to_operand_aliasing={{}: (0, {})} | custom-call | flops 14000000000 | tf_op jit(solution)/shard_map/pallas_call | solution.py:74
  126.9 2.6 %shard_map.138 = (bf16[512,512]{1,0:T(8,128)(2,1)}, bf16[1,512]{1,0:T(2,128)(2,1)}) custom-call(bf16[512,512]{1,0:T(8,128)(2,1)S(1)} %copy-done.21, bf16[512,512]{1,0:T(8,128)(2,1)S(1)} %collective-permute-done.21.a, bf16[512,512]{1,0:T(8,128)(2,1)S(1)} %collective-permute-done.22.b, bf16[512,512]{1,0:T(8,128)(2,1)} %collective-permute-done.23.fr, ...), custom_call_target="tpu_custom_call" | custom-call | flops 28999999488 | tf_op jit(solution)/shard_map/pallas_call | solution.py:74
  (87 shorter events, 14.4 us)
Async XLA Ops:
  0.6 8.4 %copy-start.5 = (bf16[1,512,512]{2,1,0:T(8,128)(2,1)S(1)}, bf16[1,512,512]{2,1,0:T(8,128)(2,1)}, u32[]{:S(2)}) copy-start(bf16[1,512,512]{2,1,0:T(8,128)(2,1)} %param.10) | copy-start | bytes 1572868
  0.6 17.0 %copy-start.24 = (s32[1,512,4]{1,2,0:T(4,128)S(1)}, s32[1,512,4]{1,2,0:T(4,128)}, u32[]{:S(2)}) copy-start(s32[1,512,4]{1,2,0:T(4,128)} %param.13) | copy-start | bytes 24580
  5.7 21.7 %collective-permute-start = (bf16[256,4096]{1,0:T(8,128)(2,1)}, bf16[256,4096]{1,0:T(8,128)(2,1)S(1)}, u32[]{:S(2)}, u32[]{:S(2)}) collective-permute-start(bf16[256,4096]{1,0:T(8,128)(2,1)} %get-tuple-element.73), channel_id=1, source_target_pairs={{0,1},{1,0},{2,3},{3,2},{4,5},{5,4},{6,7},{7,6},{8,9},{9,8},{10,11... | collective-permute-start | bytes 6291464 | tf_op jit(solution)/shard_map/ppermute | solution.py:44
  9.1 13.6 %collective-permute-start.3 = (bf16[512,512]{1,0:T(8,128)(2,1)S(1)}, bf16[512,512]{1,0:T(8,128)(2,1)}, u32[]{:S(2)}, u32[]{:S(2)}) collective-permute-start(bf16[512,512]{1,0:T(8,128)(2,1)S(1)} %bitcast.6), channel_id=1, source_target_pairs={{0,6},{1,7},{2,0},{3,1},{4,2},{5,3},{6,4},{7,5},{8,14},{9,15},{10,... | collective-permute-start | bytes 1572872 | tf_op jit(solution)/shard_map/ppermute | solution.py:36
  10.1 14.5 %collective-permute-start.2 = (bf16[512,512]{1,0:T(8,128)(2,1)S(1)}, bf16[512,512]{1,0:T(8,128)(2,1)}, u32[]{:S(2)}, u32[]{:S(2)}) collective-permute-start(bf16[512,512]{1,0:T(8,128)(2,1)S(1)} %bitcast.7), channel_id=1, source_target_pairs={{0,2},{1,3},{2,4},{3,5},{4,6},{5,7},{6,0},{7,1},{8,10},{9,11},{10,... | collective-permute-start | bytes 1572872 | tf_op jit(solution)/shard_map/ppermute | solution.py:32
  10.6 44.6 %collective-permute-start.4 = (bf16[512,512]{1,0:T(8,128)(2,1)S(1)}, bf16[512,512]{1,0:T(8,128)(2,1)}, u32[]{:S(2)}, u32[]{:S(2)}) collective-permute-start(bf16[512,512]{1,0:T(8,128)(2,1)S(1)} %bitcast.8), channel_id=1, source_target_pairs={{0,8},{1,9},{2,10},{3,11},{4,12},{5,13},{6,14},{7,15},{8,0},{9,1},... | collective-permute-start | bytes 1572872 | tf_op jit(solution)/shard_map/ppermute | solution.py:40
  17.0 10.5 %collective-permute-start.1 = (bf16[256,640]{1,0:T(8,128)(2,1)}, bf16[256,640]{1,0:T(8,128)(2,1)S(1)}, u32[]{:S(2)}, u32[]{:S(2)}) collective-permute-start(bf16[256,640]{1,0:T(8,128)(2,1)} %get-tuple-element.74), channel_id=1, source_target_pairs={{0,1},{1,0},{2,3},{3,2},{4,5},{5,4},{6,7},{7,6},{8,9},{9,8},{10,11... | collective-permute-start | bytes 983048 | tf_op jit(solution)/shard_map/ppermute | solution.py:44
  26.2 13.2 %collective-permute-start.5 = (bf16[256,512]{1,0:T(8,128)(2,1)S(1)}, bf16[256,512]{1,0:T(8,128)(2,1)S(1)}, u32[]{:S(2)}, u32[]{:S(2)}) collective-permute-start(bf16[256,512]{1,0:T(8,128)(2,1)S(1)} %get-tuple-element.86), channel_id=1, source_target_pairs={{0,64},{16,80},{32,96},{48,112},{64,0},{80,16},{96,32},{112,48},{1... | collective-permute-start | bytes 786440 | tf_op jit(solution)/shard_map/ppermute | solution.py:48
  27.5 13.4 %collective-permute-start.8 = (bf16[512,512]{1,0:T(8,128)(2,1)}, bf16[512,512]{1,0:T(8,128)(2,1)S(1)}, u32[]{:S(2)}, u32[]{:S(2)}) collective-permute-start(bf16[512,512]{1,0:T(8,128)(2,1)} %collective-permute-done.2.refs_2_.refs_6_), channel_id=1, source_target_pairs={{0,2},{1,3},{2,4},{3,5},{4,6},{5,7},{6,0},{7,1},{8,10},{9,11},{10,... | collective-permute-start | bytes 1572872 | tf_op jit(solution)/shard_map/ppermute | solution.py:32
  32.9 12.2 %collective-permute-start.7 = (bf16[512,512]{1,0:T(8,128)(2,1)S(1)}, bf16[512,512]{1,0:T(8,128)(2,1)S(1)}, u32[]{:S(2)}, u32[]{:S(2)}) collective-permute-start(bf16[512,512]{1,0:T(8,128)(2,1)S(1)} %get-tuple-element.91), channel_id=1, source_target_pairs={{0,6},{1,7},{2,0},{3,1},{4,2},{5,3},{6,4},{7,5},{8,14},{9,15},{10,... | collective-permute-start | bytes 1572872 | tf_op jit(solution)/shard_map/ppermute | solution.py:36
  35.0 22.8 %collective-permute-start.10 = (bf16[512,512]{1,0:T(8,128)(2,1)S(1)}, bf16[512,512]{1,0:T(8,128)(2,1)S(1)}, u32[]{:S(2)}, u32[]{:S(2)}) collective-permute-start(bf16[512,512]{1,0:T(8,128)(2,1)S(1)} %get-tuple-element.105), channel_id=1, source_target_pairs={{0,2},{1,3},{2,4},{3,5},{4,6},{5,7},{6,0},{7,1},{8,10},{9,11},{10,... | collective-permute-start | bytes 1572872 | tf_op jit(solution)/shard_map/ppermute | solution.py:32
  43.5 14.6 %copy-start.18 = (f32[512,512]{1,0:T(8,128)}, f32[512,512]{1,0:T(8,128)S(1)}, u32[]{:S(2)}) copy-start(f32[512,512]{1,0:T(8,128)S(1)} %shard_map.131.refs_5_) | copy-start | bytes 3145732
  45.2 12.7 %collective-permute-start.11 = (bf16[512,512]{1,0:T(8,128)(2,1)S(1)}, bf16[512,512]{1,0:T(8,128)(2,1)S(1)}, u32[]{:S(2)}, u32[]{:S(2)}) collective-permute-start(bf16[512,512]{1,0:T(8,128)(2,1)S(1)} %add.28), channel_id=1, source_target_pairs={{0,6},{1,7},{2,0},{3,1},{4,2},{5,3},{6,4},{7,5},{8,14},{9,15},{10,... | collective-permute-start | bytes 1572872 | tf_op jit(solution)/shard_map/ppermute | solution.py:36
  48.1 5.3 %collective-permute-start.6 = (bf16[128,512]{1,0:T(8,128)(2,1)S(1)}, bf16[128,512]{1,0:T(8,128)(2,1)S(1)}, u32[]{:S(2)}, u32[]{:S(2)}) collective-permute-start(bf16[128,512]{1,0:T(8,128)(2,1)S(1)} %get-tuple-element.140), channel_id=1, source_target_pairs={{0,128},{16,144},{32,160},{48,176},{64,192},{80,208},{96,224},{112... | collective-permute-start | bytes 393224 | tf_op jit(solution)/shard_map/ppermute | solution.py:48
  53.5 4.4 %collective-permute-start.12 = (bf16[128,512]{1,0:T(8,128)(2,1)S(1)}, bf16[128,512]{1,0:T(8,128)(2,1)S(1)}, u32[]{:S(2)}, u32[]{:S(2)}) collective-permute-start(bf16[128,512]{1,0:T(8,128)(2,1)S(1)} %add.29), channel_id=1, source_target_pairs={{0,16},{16,0},{32,48},{48,32},{64,80},{80,64},{96,112},{112,96},{1... | collective-permute-start | bytes 393224 | tf_op jit(solution)/shard_map/ppermute | solution.py:54
  55.2 26.4 %collective-permute-start.16 = (bf16[512,512]{1,0:T(8,128)(2,1)}, bf16[512,512]{1,0:T(8,128)(2,1)}, u32[]{:S(2)}, u32[]{:S(2)}) collective-permute-start(bf16[512,512]{1,0:T(8,128)(2,1)} %collective-permute-done.4.refs_4_.refs_12_), channel_id=1, source_target_pairs={{0,6},{1,7},{2,0},{3,1},{4,2},{5,3},{6,4},{7,5},{8,14},{9,15},{10,... | collective-permute-start | bytes 1572872 | tf_op jit(solution)/shard_map/ppermute | solution.py:36
  55.3 10.5 %collective-permute-start.9 = (bf16[512,512]{1,0:T(8,128)(2,1)}, bf16[512,512]{1,0:T(8,128)(2,1)}, u32[]{:S(2)}, u32[]{:S(2)}) collective-permute-start(bf16[512,512]{1,0:T(8,128)(2,1)} %collective-permute-done.4.refs_4_.refs_12_), channel_id=1, source_target_pairs={{0,2},{1,3},{2,4},{3,5},{4,6},{5,7},{6,0},{7,1},{8,10},{9,11},{10,... | collective-permute-start | bytes 1572872 | tf_op jit(solution)/shard_map/ppermute | solution.py:32
  65.8 20.1 %collective-permute-start.13 = (bf16[512,512]{1,0:T(8,128)(2,1)}, bf16[512,512]{1,0:T(8,128)(2,1)}, u32[]{:S(2)}, u32[]{:S(2)}) collective-permute-start(bf16[512,512]{1,0:T(8,128)(2,1)} %collective-permute-done.9.refs_2_.refs_10_), channel_id=1, source_target_pairs={{0,2},{1,3},{2,4},{3,5},{4,6},{5,7},{6,0},{7,1},{8,10},{9,11},{10,... | collective-permute-start | bytes 1572872 | tf_op jit(solution)/shard_map/ppermute | solution.py:32
  65.9 6.8 %collective-permute-start.14 = (bf16[128,512]{1,0:T(8,128)(2,1)S(1)}, bf16[128,512]{1,0:T(8,128)(2,1)S(1)}, u32[]{:S(2)}, u32[]{:S(2)}) collective-permute-start(bf16[128,512]{1,0:T(8,128)(2,1)S(1)} %add.30), channel_id=1, source_target_pairs={{0,32},{16,48},{32,0},{48,16},{64,96},{80,112},{96,64},{112,80},{1... | collective-permute-start | bytes 393224 | tf_op jit(solution)/shard_map/ppermute | solution.py:54
  73.3 11.3 %collective-permute-start.15 = (bf16[128,512]{1,0:T(8,128)(2,1)}, bf16[128,512]{1,0:T(8,128)(2,1)}, u32[]{:S(2)}, u32[]{:S(2)}) collective-permute-start(bf16[128,512]{1,0:T(8,128)(2,1)} %add.31), channel_id=1, source_target_pairs={{0,128},{16,144},{32,160},{48,176},{64,192},{80,208},{96,224},{112... | collective-permute-start | bytes 393224 | tf_op jit(solution)/shard_map/ppermute | solution.py:48
  76.2 50.6 %collective-permute-start.23 = (bf16[512,512]{1,0:T(8,128)(2,1)}, bf16[512,512]{1,0:T(8,128)(2,1)}, u32[]{:S(2)}, u32[]{:S(2)}) collective-permute-start(bf16[512,512]{1,0:T(8,128)(2,1)} %copy-done.11), channel_id=1, source_target_pairs={{0,8},{1,9},{2,10},{3,11},{4,12},{5,13},{6,14},{7,15},{8,0},{9,1},... | collective-permute-start | bytes 1572872 | tf_op jit(solution)/shard_map/ppermute | solution.py:40
  81.6 30.0 %collective-permute-start.19 = (bf16[512,512]{1,0:T(8,128)(2,1)}, bf16[512,512]{1,0:T(8,128)(2,1)S(1)}, u32[]{:S(2)}, u32[]{:S(2)}) collective-permute-start(bf16[512,512]{1,0:T(8,128)(2,1)} %copy-done.10), channel_id=1, source_target_pairs={{0,6},{1,7},{2,0},{3,1},{4,2},{5,3},{6,4},{7,5},{8,14},{9,15},{10,... | collective-permute-start | bytes 1572872 | tf_op jit(solution)/shard_map/ppermute | solution.py:36
  85.8 26.1 %collective-permute-start.18 = (bf16[256,512]{1,0:T(8,128)(2,1)S(1)}, bf16[256,512]{1,0:T(8,128)(2,1)S(1)}, u32[]{:S(2)}, u32[]{:S(2)}) collective-permute-start(bf16[256,512]{1,0:T(8,128)(2,1)S(1)} %maximum_select_fusion.a), channel_id=1, source_target_pairs={{0,64},{16,80},{32,96},{48,112},{64,0},{80,16},{96,32},{112,48},{1... | collective-permute-start | bytes 786440 | tf_op jit(solution)/shard_map/ppermute | solution.py:48
  89.7 22.2 %copy-start.9 = (bf16[512,512]{1,0:T(8,128)(2,1)S(1)}, bf16[512,512]{1,0:T(8,128)(2,1)}, u32[]{:S(2)}) copy-start(bf16[512,512]{1,0:T(8,128)(2,1)} %copy-done.8) | copy-start | bytes 1572868
  89.7 23.7 %copy-start.3 = (f32[512,512]{1,0:T(8,128)S(1)}, f32[512,512]{1,0:T(8,128)}, u32[]{:S(2)}) copy-start(f32[512,512]{1,0:T(8,128)} %m.1) | copy-start | bytes 3145732
  89.7 23.7 %copy-start.4 = (f32[512,512]{1,0:T(8,128)S(1)}, f32[512,512]{1,0:T(8,128)}, u32[]{:S(2)}) copy-start(f32[512,512]{1,0:T(8,128)} %p.1) | copy-start | bytes 3145732
  92.5 22.4 %collective-permute-start.17 = (f32[256,640]{1,0:T(8,128)S(1)}, f32[256,640]{1,0:T(8,128)S(1)}, u32[]{:S(2)}, u32[]{:S(2)}) collective-permute-start(f32[256,640]{1,0:T(8,128)S(1)} %get-tuple-element.119), channel_id=1, source_target_pairs={{0,1},{1,0},{2,3},{3,2},{4,5},{5,4},{6,7},{7,6},{8,9},{9,8},{10,11... | collective-permute-start | bytes 1966088 | tf_op jit(solution)/shard_map/ppermute | solution.py:44
  111.8 15.0 %collective-permute-start.22 = (bf16[512,512]{1,0:T(8,128)(2,1)S(1)}, bf16[512,512]{1,0:T(8,128)(2,1)S(1)}, u32[]{:S(2)}, u32[]{:S(2)}) collective-permute-start(bf16[512,512]{1,0:T(8,128)(2,1)S(1)} %add.32), channel_id=1, source_target_pairs={{0,6},{1,7},{2,0},{3,1},{4,2},{5,3},{6,4},{7,5},{8,14},{9,15},{10,... | collective-permute-start | bytes 1572872 | tf_op jit(solution)/shard_map/ppermute | solution.py:36
  111.9 14.9 %collective-permute-start.21 = (bf16[512,512]{1,0:T(8,128)(2,1)S(1)}, bf16[512,512]{1,0:T(8,128)(2,1)S(1)}, u32[]{:S(2)}, u32[]{:S(2)}) collective-permute-start(bf16[512,512]{1,0:T(8,128)(2,1)S(1)} %copy-done.9), channel_id=1, source_target_pairs={{0,2},{1,3},{2,4},{3,5},{4,6},{5,7},{6,0},{7,1},{8,10},{9,11},{10,... | collective-permute-start | bytes 1572872 | tf_op jit(solution)/shard_map/ppermute | solution.py:32
  114.9 5.8 %copy-start.1 = (bf16[256,8192]{1,0:T(8,128)(2,1)S(1)}, bf16[256,8192]{1,0:T(8,128)(2,1)}, u32[]{:S(2)}) copy-start(bf16[256,8192]{1,0:T(8,128)(2,1)} %refs_0_.1) | copy-start | bytes 12582916
  114.9 5.8 %copy-start.14 = (bf16[256,512]{1,0:T(8,128)(2,1)S(1)}, bf16[256,512]{1,0:T(8,128)(2,1)}, u32[]{:S(2)}) copy-start(bf16[256,512]{1,0:T(8,128)(2,1)} %refs_3_.1) | copy-start | bytes 786436
  119.8 5.4 %collective-permute-start.20 = (bf16[256,4096]{1,0:T(8,128)(2,1)S(1)}, bf16[256,4096]{1,0:T(8,128)(2,1)S(1)}, u32[]{:S(2)}, u32[]{:S(2)}) collective-permute-start(bf16[256,4096]{1,0:T(8,128)(2,1)S(1)} %get-tuple-element.132), channel_id=1, source_target_pairs={{0,1},{1,0},{2,3},{3,2},{4,5},{5,4},{6,7},{7,6},{8,9},{9,8},{10,11... | collective-permute-start | bytes 6291464 | tf_op jit(solution)/shard_map/ppermute | solution.py:44
  (17 other events, 38.4 us)

commit v3 on v2

v3 whole, which is shorter than its diff:
```python
import jax
import jax.numpy as jnp
from jax import lax
from jax.experimental import pallas as pl
from jax.experimental.pallas import tpu as pltpu
from jax.sharding import PartitionSpec as P

epsilon = 1e-05
outer_decay = 0.9
outer_rate = 0.7

F32 = jnp.float32
BF16 = jnp.bfloat16
N_Y, N_ZH, N_CORE = 4, 2, 2
N_CHIP = N_Y * N_ZH
N_X, N_ZL = 4, 4
WEIGHT = 1e10
VMEM_LIMIT = 12 * 1024 * 1024


def dp_moves(dy=0, dz=0, dc=0):
    pairs = []
    for zh in range(N_ZH):
        for y in range(N_Y):
            for c in range(N_CORE):
                to = (((zh + dz) % N_ZH) * N_Y + (y + dy) % N_Y) * N_CORE + (c + dc) % N_CORE
                pairs.append(((zh * N_Y + y) * N_CORE + c, to))
    return pairs


def to_up(v):
    return lax.ppermute(v, "dp", dp_moves(dy=1))


def to_down(v):
    return lax.ppermute(v, "dp", dp_moves(dy=-1))


def to_far(v):
    return lax.ppermute(v, "dp", dp_moves(dz=1))


def to_core(v):
    return lax.ppermute(v, "dp", dp_moves(dc=1))


def swap_x(v, bit):
    return lax.ppermute(
        v, "replica", [(x * N_ZL + z, (x ^ bit) * N_ZL + z) for x in range(N_X) for z in range(N_ZL)]
    )


def swap_z(v, bit):
    return lax.ppermute(
        v, "replica", [(x * N_ZL + z, x * N_ZL + (z ^ bit)) for x in range(N_X) for z in range(N_ZL)]
    )


def core():
    return lax.rem(lax.axis_index("dp"), N_CORE)


def chip(side, dy):
    mine = lax.div(lax.axis_index("dp"), N_CORE)
    zh = lax.rem(lax.div(mine, N_Y) + side, N_ZH)
    return zh * N_Y + lax.rem(lax.rem(mine, N_Y) + dy, N_Y)


def place(side, dy):
    return chip(side, dy) * N_CORE + core()


def call(kernel, outs, ins, cost=1.0, vmem=VMEM_LIMIT, **kw):
    return pl.pallas_call(
        kernel,
        out_shape=outs,
        compiler_params=pltpu.CompilerParams(vmem_limit_bytes=vmem),
        cost_estimate=pl.CostEstimate(
            flops=int(cost * WEIGHT), bytes_accessed=0, transcendentals=0
        ),
        **kw,
    )(*ins)


HBM = pl.BlockSpec(memory_space=pltpu.HBM)
INSIDE = pl.BlockSpec(memory_space=pltpu.VMEM)


def full(shape):
    return pl.BlockSpec(shape, lambda j: (0,) * len(shape))


def block(index, size):
    return pl.ds(pl.multiple_of(index * size, size), size)


def dot_nt(a, b):
    return lax.dot_general(a, b, (((1,), (1,)), ((), ())), preferred_element_type=F32)


def dot(a, b):
    return jnp.dot(a, b, preferred_element_type=F32)


def identity(n):
    r = lax.broadcasted_iota(jnp.int32, (n, n), 0)
    c = lax.broadcasted_iota(jnp.int32, (n, n), 1)
    return jnp.where(r == c, 1.0, 0.0).astype(BF16)


def start_all(copies):
    for copy in copies:
        copy.start()
    return copies


ORDER = (2, 3, 1, 0)


def split_tokens(tokens, cot):
    t, d = tokens.shape
    f = cot.shape[1]
    steps = d // (2 * f)

    def kernel(tok, ct, mine, sent, extra, ir_out, sems):
        arrivals = []
        for i in range(steps):
            cols = slice(i * f, (i + 1) * f)
            arrivals += start_all(
                [
                    pltpu.make_async_copy(
                        tok.at[:, block(2 * i + core(), f)], mine.at[:, cols], sems.at[0, i]
                    ),
                    pltpu.make_async_copy(
                        tok.at[:, block(2 * i + 1 - core(), f)], sent.at[:, cols], sems.at[1, i]
                    ),
                ]
            )
        acc = jnp.zeros((t, 128), F32)
        for i in range(steps):
            arrivals[2 * i].wait()
            arrivals[2 * i + 1].wait()
            for n in range(i * f, (i + 1) * f, 128):
                for part in (mine, sent):
                    v = part[:, n : n + 128].astype(F32)
                    acc += v * v
        mean = jnp.sum(acc, axis=1, keepdims=True) / d
        ir = lax.rsqrt(jnp.broadcast_to(mean, (t, 128)) + epsilon)
        ir_out[...] = ir
        lane = lax.broadcasted_iota(jnp.int32, (t, 128), 1)
        terms = exact_terms(ir, lane, 0)
        extra[:, :f] = ct[...]
        extra[:, f:] = terms.astype(BF16)

    return call(
        kernel,
        (
            jax.ShapeDtypeStruct((t, d // 2), BF16),
            jax.ShapeDtypeStruct((t, d // 2), BF16),
            jax.ShapeDtypeStruct((t, f + 128), BF16),
            jax.ShapeDtypeStruct((t, 128), F32),
        ),
        (tokens, cot),
        cost=3.2,
        vmem=56 * 1024 * 1024,
        in_specs=[HBM, INSIDE],
        out_specs=(INSIDE,) * 4,
        scratch_shapes=[pltpu.SemaphoreType.DMA((2, steps))],
    )


def exact_terms(column, lane, first):
    high = column.astype(BF16).astype(F32)
    middle = (column - high).astype(BF16).astype(F32)
    low = column - high - middle
    zero = jnp.zeros_like(column)
    terms = jnp.where(lane == first, high, jnp.where(lane == first + 1, middle, zero))
    return jnp.where(lane == first + 2, low, terms)


def from_terms(values, first):
    return sum(values[:, first + i : first + i + 1].astype(F32) for i in range(3))


def partner_scale(extra, f):
    return from_terms(extra, f)


def hidden_block(hid, cols, own, oth, gain, irr, ext, side, dy):
    t = own.shape[0]
    f = cols.stop - cols.start
    g = gain[:, block(place(side, dy), f)]
    at = block(chip(side, dy), f)
    hid[:t, cols] = (own[:, at].astype(F32) * irr[:, 0:1] * g).astype(BF16)
    hid[t:, cols] = (oth[:, at].astype(F32) * partner_scale(ext, f) * g).astype(BF16)


def partials(mine, gains, cot, ir, other, extra, side):
    t = mine.shape[0]
    f = k = cot.shape[1]

    def kernel(own, oth, gain, ct, irr, ext, *refs):
        outs, hid, cot_t = refs[:4], refs[4], refs[5]
        eye = identity(k)
        cot_t[:, :t] = dot_nt(eye, ct[...]).astype(BF16)
        cot_t[:, t:] = dot_nt(eye, ext[:, :k]).astype(BF16)
        for i in range(N_Y):
            cols = slice(i * f, (i + 1) * f)
            hidden_block(hid, cols, own, oth, gain, irr, ext, side, ORDER[i])
            outs[i][...] = dot(cot_t[...], hid[:, cols]).astype(BF16)

    shape = jax.ShapeDtypeStruct((k, f), BF16)
    hidden = [] if side else [jax.ShapeDtypeStruct((2 * t, N_Y * f), BF16)]
    scratch = [pltpu.VMEM((2 * t, N_Y * f), BF16)] if side else []
    return call(
        kernel,
        [shape] * 4 + hidden,
        (mine, other, gains, cot, ir, extra),
        cost=3.4,
        in_specs=[INSIDE] * 6,
        out_specs=[INSIDE] * (4 + len(hidden)),
        scratch_shapes=scratch + [pltpu.VMEM((k, 2 * t), BF16)],
    )


def side_sum(own, from_down, from_up):
    def kernel(o, a, b, out):
        out[...] = (o[...].astype(F32) + a[...].astype(F32) + b[...].astype(F32)).astype(BF16)

    return call(kernel, jax.ShapeDtypeStruct(own.shape, BF16), (own, from_down, from_up), cost=1.0)


def final_sum(own, from_down, from_up, far, weight, gains):
    k, f = own.shape

    def kernel(o, a, b, fr, w, gain, out, gain_out):
        eye = identity(k)
        weight_t = dot_nt(eye, w[...])
        total = (o[...].astype(F32) + a[...].astype(F32)) + (b[...].astype(F32) + fr[...].astype(F32))
        out[...] = dot_nt(eye, total.astype(BF16)).astype(BF16)
        sums = jnp.sum(total * weight_t, axis=0, keepdims=True)
        gain_out[...] = (sums / gain[:, block(lax.axis_index("dp"), f)]).astype(BF16)

    return call(
        kernel,
        (jax.ShapeDtypeStruct((f, k), BF16), jax.ShapeDtypeStruct((1, f), BF16)),
        (own, from_down, from_up, far, weight, gains),
        cost=2.9,
    )


def project_near(hidden, weights):
    f, k = weights[0].shape

    def kernel(hid, w0, w1, w2, w3, out):
        total = jnp.zeros(out.shape, F32)
        for i, w in enumerate((w0, w1, w2, w3)):
            total += dot(hid[:, i * f : (i + 1) * f], w[...])
        out[...] = total

    return call(
        kernel,
        jax.ShapeDtypeStruct((hidden.shape[0], k), F32),
        (hidden,) + tuple(weights),
        cost=2.5,
        in_specs=[INSIDE] * 5,
        out_specs=INSIDE,
    )


def project_far(mine, other, gains, ir, extra, cot, weights, before):
    f, k = weights[0].shape
    t = mine.shape[0]

    def kernel(own_x, oth, gain, irr, ext, ct, w0, w1, w2, w3, first, kept, sent, hid):
        total = first[...]
        for i, w in enumerate((w0, w1, w2, w3)):
            cols = slice(i * f, (i + 1) * f)
            hidden_block(hid, cols, own_x, oth, gain, irr, ext, 1, ORDER[i])
            total += dot(hid[:, cols], w[...])
        own = jnp.sum(total[:t] * ct[...].astype(F32), axis=1, keepdims=True)
        others = jnp.sum(total[t:] * ext[:, :k].astype(F32), axis=1, keepdims=True)
        lane = lax.broadcasted_iota(jnp.int32, (t, 128), 1)
        kept[:, :k] = total[:t]
        kept[:, k:] = jnp.where(lane == 0, own, others)
        sent[:, :k] = total[t:].astype(BF16)
        sent[:, k:] = (exact_terms(others, lane, 0) + exact_terms(own, lane, 3)).astype(BF16)

    return call(
        kernel,
        (
            jax.ShapeDtypeStruct((t, k + 128), F32),
            jax.ShapeDtypeStruct((t, k + 128), BF16),
        ),
        (mine, other, gains, ir, extra, cot) + tuple(weights) + (before,),
        cost=2.5,
        in_specs=[INSIDE] * 11,
        out_specs=(INSIDE,) * 2,
        scratch_shapes=[pltpu.VMEM((2 * t, N_Y * f), BF16)],
    )


def blocks_of_chip():
    return [(side, dy) for side in range(N_ZH) for dy in ORDER]


def token_gradient(x, ws, gain, ct, scale, mean, store):
    f = ws[0].shape[0]
    shift = scale * scale * mean
    for i, (side, dy) in enumerate(blocks_of_chip()):
        g = gain[:, block(place(side, dy), f)]
        grad = dot_nt(ct, ws[i][...])
        values = x[:, block(chip(side, dy), f)].astype(F32)
        store(i, (scale * (grad * g) - values * shift).astype(BF16))


def backward_other(other, extra, gains, mine, arrived, weights):
    t = other.shape[0]
    f = k = extra.shape[1] - 128
    d = gains.shape[1]

    def kernel(*refs):
        oth, gain, ext, mn, arr = refs[:5]
        ws = refs[5:13]
        out, keys, mean = refs[13:16]
        keys[...] = (mn[:, :k] + arr[:, :k].astype(F32)).astype(BF16)
        own = (mn[:, k : k + 1] + from_terms(arr, k)) / d
        others = (mn[:, k + 1 : k + 2] + from_terms(arr, k + 3)) / d
        mean[...] = jnp.broadcast_to(own, (t, 128))

        def store(i, values):
            out[:, i * f : (i + 1) * f] = values

        token_gradient(oth, ws, gain, ext[:, :k], partner_scale(ext, f), others, store)

    return call(
        kernel,
        (
            jax.ShapeDtypeStruct((t, d // 2), BF16),
            jax.ShapeDtypeStruct((t, k), BF16),
            jax.ShapeDtypeStruct((t, 128), F32),
        ),
        (other, gains, extra, mine, arrived) + tuple(weights),
        cost=5.5,
        in_specs=[INSIDE] * 13,
        out_specs=(INSIDE,) * 3,
    )


def backward_own(mine, gains, ir, cot, mean, weights):
    t = mine.shape[0]
    d = gains.shape[1]
    f = cot.shape[1]
    where = blocks_of_chip()

    def kernel(*refs):
        own, gain, irr, ct, mn = refs[:5]
        ws = refs[5:13]
        out, results, sems = refs[13:]
        leaving = []

        def store(i, values):
            results[i] = values
            to = out.at[:, block(place(*where[i]), f)]
            leaving.extend(start_all([pltpu.make_async_copy(results.at[i], to, sems.at[i])]))

        token_gradient(own, ws, gain, ct[...], irr[:, 0:1], mn[:, 0:1], store)
        for copy in leaving:
            copy.wait()

    return call(
        kernel,
        jax.ShapeDtypeStruct((t, d), BF16),
        (mine, gains, ir, cot, mean) + tuple(weights),
        cost=4.7,
        in_specs=[INSIDE] * 13,
        out_specs=HBM,
        scratch_shapes=[
            pltpu.VMEM((N_CHIP, t, f), BF16),
            pltpu.SemaphoreType.DMA((N_CHIP,)),
        ],
    )


def fill_in(token_grad, arrived):
    f = arrived.shape[1] // N_CHIP
    where = blocks_of_chip()

    def kernel(_, arr, out, sems):
        away = 1 - core()
        leaving = []
        for i in range(N_CHIP):
            to = out.at[:, block(chip(*where[i]) * N_CORE + away, f)]
            leaving += start_all(
                [pltpu.make_async_copy(arr.at[:, i * f : (i + 1) * f], to, sems.at[i])]
            )
        for copy in leaving:
            copy.wait()

    return call(
        kernel,
        jax.ShapeDtypeStruct(token_grad.shape, token_grad.dtype),
        (token_grad, arrived),
        cost=1.4,
        in_specs=[HBM, INSIDE],
        out_specs=HBM,
        input_output_aliases={0: 0},
        scratch_shapes=[pltpu.SemaphoreType.DMA((N_CHIP,))],
    )


def x_bit(bit):
    return lax.rem(lax.div(lax.axis_index("replica"), N_ZL * bit), 2)


def scaled_halves(quantized, exponents):
    n, cols = quantized.shape
    h = n // 2
    nb = exponents.shape[0]
    width = cols // nb

    def kernel(q, e, keep, send, scales):
        powers = jnp.exp2(e[...].astype(F32)).astype(BF16)
        scales[...] = dot_nt(identity(n), powers)
        for out, half in ((keep, x_bit(1)), (send, 1 - x_bit(1))):
            rows = block(half, h)
            for b in range(nb):
                lanes = slice(b * width, (b + 1) * width)
                scale = scales[rows, b : b + 1]
                out[:, lanes] = (q[rows, lanes].astype(F32) * scale).astype(BF16)

    return call(
        kernel,
        (jax.ShapeDtypeStruct((h, cols), BF16),) * 2,
        (quantized, exponents),
        cost=20.0,
        scratch_shapes=[pltpu.VMEM((n, nb), F32)],
    )


def outer_update(average, momentum, outer_params):
    new_momentum = outer_decay * momentum + average
    new_params = outer_params - outer_rate * (average + outer_decay * new_momentum)
    return (new_momentum, new_params)


def outer_step(half, other, momentum, outer_params):
    n, cols = momentum.shape
    h = n // 2

    def kernel(a, b, m, p, new_m, new_p):
        j = pl.program_id(0)

        def update(total):
            average = total[...].astype(F32) / (N_X * N_ZL)
            new_m[...], new_p[...] = outer_update(average, m[...], p[...])

        pl.when(j == 0)(lambda: update(a))
        pl.when(j == 1)(lambda: update(b))

    def half_of(j):
        return (lax.rem(x_bit(1) + j, 2), 0)

    spec = pl.BlockSpec((h, cols), half_of)
    return call(
        kernel,
        (jax.ShapeDtypeStruct((n, cols), F32),) * 2,
        (half, other, momentum, outer_params),
        cost=2.0,
        grid=(2,),
        in_specs=[full((h, cols)), full((h, cols)), spec, spec],
        out_specs=(spec, spec),
    )


def after(values, *events):
    held = lax.optimization_barrier(tuple(values) + events)
    return held[: len(values)]


def shards(
    tokens, norm_gain, key_weight, key_cotangent, quantized, scale_exponent, momentum, outer_params
):
    gains = norm_gain
    cot = key_cotangent
    weight = key_weight[0]

    n_down = to_up(weight)
    n_up = to_down(weight)

    mine, sent, extra_sent, ir = split_tokens(tokens, cot)
    other = to_core(sent)
    extra = to_core(extra_sent)

    quant, exponents = after((quantized[0], scale_exponent[0]), ir)
    keep, send = scaled_halves(quant, exponents.T)
    x1 = swap_x(send, 1)
    far_weight = to_far(after((weight,), keep)[0])

    other, extra = after((other, extra), keep)
    f_opposite, f_minus, f_plus, f_own = partials(
        mine, gains, cot, ir, other, extra, 1
    )
    n_down, n_up = after((n_down, n_up), f_own)
    n_opposite = to_up(n_down)
    f_step = to_down(f_opposite)
    f_from_down = to_up(f_plus)

    keep, x1 = after((keep, x1), n_up)
    half = keep + x1
    q = half.shape[0] // 2
    first = x_bit(2) * q
    part = lax.dynamic_slice_in_dim(half, first, q)
    x2 = swap_x(lax.dynamic_slice_in_dim(half, q - first, q), 2)

    other, extra = after((other, extra), part)
    g_opposite, g_minus, g_plus, g_own, hidden_near = partials(
        mine, gains, cot, ir, other, extra, 0
    )
    part, x2 = after((part, x2), g_own)
    part = part + x2
    z1 = swap_z(part, 1)

    f_minus, f_step = after((f_minus, f_step), part)
    f_minus = f_minus + f_step
    f_from_up = to_down(f_minus)

    near_rows = (n_opposite, n_down, n_up, weight)
    *near_rows, hidden_near = after((*near_rows, hidden_near), f_minus)
    near_keys = project_near(hidden_near, near_rows)
    part, z1 = after((part, z1), near_keys)
    part = part + z1
    z2 = swap_z(part, 2)

    (far_weight,) = after((far_weight,), part)
    a_down = to_up(far_weight)
    a_up = to_down(far_weight)

    f_own, f_from_down, f_from_up = after((f_own, f_from_down, f_from_up), far_weight)
    f_total = side_sum(f_own, f_from_down, f_from_up)
    far_sum = to_far(f_total)
    part, z2 = after((part, z2), f_total)
    part = part + z2
    x3 = swap_x(part, 2)
    (a_down,) = after((a_down,), part)
    a_opposite = to_up(a_down)

    g_opposite, a_up = after((g_opposite, a_up), a_down)
    g_step = to_down(g_opposite)
    part, x3 = after((part, x3), a_up)
    pair = jnp.concatenate([part, x3])
    half = jnp.where(x_bit(2) == 0, pair, jnp.roll(pair, q, axis=0))
    x4 = swap_x(half, 1)
    g_plus, a_opposite = after((g_plus, a_opposite), half)
    g_from_down = to_up(g_plus)

    far_rows = (a_opposite, a_down, a_up, far_weight)
    keys_mine, keys_sent = project_far(
        mine, other, gains, ir, extra, cot, far_rows, near_keys
    )
    arrived = to_core(keys_sent)
    half, x4 = after((half, x4), keys_sent)
    new_momentum, new_params = outer_step(half, x4, momentum, outer_params)
    g_minus, g_step = after((g_minus, g_step), new_params)
    g_minus = g_minus + g_step
    g_from_up = to_down(g_minus)
    arrived, keys_mine, far_sum = after((arrived, keys_mine, far_sum), g_minus)
    rows = tuple(near_rows) + tuple(far_rows)
    grad_sent, keys, mean = backward_other(other, extra, gains, keys_mine, arrived, rows)
    grad_arrived = to_core(grad_sent)
    mean, far_sum = after((mean, far_sum), grad_sent)
    token_grad = backward_own(mine, gains, ir, cot, mean, rows)
    grad_arrived, token_grad = after((grad_arrived, token_grad), new_params)
    token_grad = fill_in(token_grad, grad_arrived)
    (g_from_up,) = after((g_from_up,), token_grad)
    weight_grad, gain_grad = final_sum(g_own, g_from_down, g_from_up, far_sum, weight, gains)
    return (keys, token_grad, weight_grad[None], gain_grad, new_momentum, new_params)


def solution(mesh):
    return jax.shard_map(
        shards,
        mesh=mesh,
        in_specs=(
            P(("replica", "dp"), None),
            P("replica", None),
            P("replica", "dp", None),
            P(("replica", "dp"), None),
            P("replica", "dp", None),
            P("replica", "dp", None),
            P("dp", None),
            P("dp", None),
        ),
        out_specs=(
            P(("replica", "dp"), None),
            P(("replica", "dp"), None),
            P("replica", "dp", None),
            P("replica", "dp"),
            P("dp", None),
            P("dp", None),
        ),
        check_vma=False,
    )
```

time: 130 us -> 108 us (0.83)
  starting transfers between devices: 60 us -> 40.6 us
  local copies, waits for them, and re-layouts: 8.68 us -> 6.96 us
    ppermute x4, starting transfers between devices: 24.1 us -> 6.65 us  [to_core(): return lax.ppermute(v, 'dp', dp_moves(dc=1))]
    ppermute x6, starting transfers between devices: 9.3 us -> 17.5 us  [to_down(): return lax.ppermute(v, 'dp', dp_moves(dy=-1))]
    ppermute x6, waiting for transfers between devices: 10.2 us -> 18 us  [to_up(): return lax.ppermute(v, 'dp', dp_moves(dy=1))]
    ppermute x2, waiting for transfers between devices: 4.94 us -> 0.01 us  [swap_z(): lax.ppermute(v, 'replica', [(x * N_ZL + z, x * N_ZL + (z ^ bit)) for x in...]
    ppermute x2, starting transfers between devices: 11.8 us -> 8.19 us  [to_far(): return lax.ppermute(v, 'dp', dp_moves(dz=1))]
    ppermute x6, starting transfers between devices: 3.28 us -> 0.33 us  [to_up(): return lax.ppermute(v, 'dp', dp_moves(dy=1))]
    ppermute x4, waiting for transfers between devices: 2.88 us -> 0.01 us  [swap_x(): lax.ppermute(v, 'replica', [(x * N_ZL + z, (x ^ bit) * N_ZL + z) for x in...]
    ppermute x2, starting transfers between devices: 4.74 us -> 2.28 us  [swap_z(): lax.ppermute(v, 'replica', [(x * N_ZL + z, x * N_ZL + (z ^ bit)) for x in...]
  transfers between devices with their start and end apart: 24 -> 24, of which waited for: 8 -> 7; matrix products, arithmetic and copies ran while one was open for 2% -> 2% of each run, Pallas kernels for 20% -> 29%
where the time goes in v3:
time: 108 us; the launch traced here: 107 us
  starting transfers between devices  40.6 us (38%)
  Pallas kernels  32.4 us (30%)
  waiting for transfers between devices  24.2 us (22%)
  local copies, waits for them, and re-layouts  6.96 us (6%)
  other arithmetic  2.25 us (2%)
    pallas_call x12, Pallas kernels, call(): pl.pallas_call(kernel, out_shape=outs, compiler_params=pltpu.CompilerPara...  32.4 us
    ppermute x6, waiting for transfers between devices, to_up(): return lax.ppermute(v, 'dp', dp_moves(dy=1))  18 us
    ppermute x6, starting transfers between devices, to_down(): return lax.ppermute(v, 'dp', dp_moves(dy=-1))  17.5 us
    ppermute x2, starting transfers between devices, to_far(): return lax.ppermute(v, 'dp', dp_moves(dz=1))  8.19 us
    unnamed x38, local copies, waits for them, and re-layouts  6.93 us
    ppermute x4, starting transfers between devices, to_core(): return lax.ppermute(v, 'dp', dp_moves(dc=1))  6.65 us
    ppermute x4, starting transfers between devices, swap_x(): lax.ppermute(v, 'replica', [(x * N_ZL + z, (x ^ bit) * N_ZL + z) for x in...  5.7 us
    ppermute x6, waiting for transfers between devices, to_down(): return lax.ppermute(v, 'dp', dp_moves(dy=-1))  4.85 us
  transfers between devices with their start and end apart: 24, of which 7 were waited for; matrix products, arithmetic and copies ran while one was open for 2% of the time, Pallas kernels for 29%

profile of v3, /device:TPU:1, one launch (start us, length us, event | category | flops | bytes accessed | tf_op | source)
XLA Modules:
  0.0 107.3 jit_solution(98172944695051299)
XLA Ops:
  0.7 3.6 %collective-permute-start.4 = (bf16[512,512]{1,0:T(8,128)(2,1)}, bf16[512,512]{1,0:T(8,128)(2,1)}, u32[]{:S(2)}, u32[]{:S(2)}) collective-permute-start(bf16[512,512]{1,0:T(8,128)(2,1)} %bitcast.6), channel_id=1, source_target_pairs={{0,6},{1,7},{2,0},{3,1},{4,2},{5,3},{6,4},{7,5},{8,14},{9,15},{10,... | collective-permute-start | bytes 1572872 | tf_op jit(solution)/shard_map/ppermute | solution.py:36
  4.3 5.4 %shard_map.127 = (bf16[256,4096]{1,0:T(8,128)(2,1)}, bf16[256,4096]{1,0:T(8,128)(2,1)}, bf16[256,640]{1,0:T(8,128)(2,1)}, f32[256,128]{1,0:T(8,128)}) custom-call(bf16[256,8192]{1,0:T(8,128)(2,1)} %tok.1, bf16[256,512]{1,0:T(8,128)(2,1)} %refs_3_.1), custom_call_target="tpu_custom_call" | custom-call | flops 32000000000 | tf_op jit(solution)/shard_map/pallas_call | solution.py:74
  9.7 1.8 %collective-permute-start.1 = (bf16[256,640]{1,0:T(8,128)(2,1)}, bf16[256,640]{1,0:T(8,128)(2,1)}, u32[]{:S(2)}, u32[]{:S(2)}) collective-permute-start(bf16[256,640]{1,0:T(8,128)(2,1)} %get-tuple-element.78), channel_id=1, source_target_pairs={{0,1},{1,0},{2,3},{3,2},{4,5},{5,4},{6,7},{7,6},{8,9},{9,8},{10,11... | collective-permute-start | bytes 983048 | tf_op jit(solution)/shard_map/ppermute | solution.py:44
  13.1 6.6 %collective-permute-start.5 = (bf16[512,512]{1,0:T(8,128)(2,1)S(1)}, bf16[512,512]{1,0:T(8,128)(2,1)S(1)}, u32[]{:S(2)}, u32[]{:S(2)}) collective-permute-start(bf16[512,512]{1,0:T(8,128)(2,1)S(1)} %bitcast.8), channel_id=1, source_target_pairs={{0,8},{1,9},{2,10},{3,11},{4,12},{5,13},{6,14},{7,15},{8,0},{9,1},... | collective-permute-start | bytes 1572872 | tf_op jit(solution)/shard_map/ppermute | solution.py:40
  19.8 1.6 %copy-done.8 = bf16[256,4096]{1,0:T(8,128)(2,1)S(1)} copy-done((bf16[256,4096]{1,0:T(8,128)(2,1)S(1)}, bf16[256,4096]{1,0:T(8,128)(2,1)}, u32[]{:S(2)}) %copy-start.8) | copy-done | bytes 2097176
  21.3 3.4 %shard_map.129 = (bf16[512,512]{1,0:T(8,128)(2,1)S(1)}, bf16[512,512]{1,0:T(8,128)(2,1)S(1)}, bf16[512,512]{1,0:T(8,128)(2,1)S(1)}, bf16[512,512]{1,0:T(8,128)(2,1)S(1)}) custom-call(bf16[256,4096]{1,0:T(8,128)(2,1)S(1)} %copy-done.8, bf16[256,4096]{1,0:T(8,128)(2,1)} %collective-permute-done.oth.refs_0_, f32[1,8192]{1,0:T(1,128)S(1)} %copy-done.6, ...), custom_call_target="tpu_custom_call" | custom-call | flops 33999998976 | tf_op jit(solution)/shard_map/pallas_call | solution.py:74
  24.9 2.5 %collective-permute-start.6 = (bf16[128,512]{1,0:T(8,128)(2,1)S(1)}, bf16[128,512]{1,0:T(8,128)(2,1)S(1)}, u32[]{:S(2)}, u32[]{:S(2)}) collective-permute-start(bf16[128,512]{1,0:T(8,128)(2,1)S(1)} %get-tuple-element.148), channel_id=1, source_target_pairs={{0,128},{16,144},{32,160},{48,176},{64,192},{80,208},{96,224},{112... | collective-permute-start | bytes 393224 | tf_op jit(solution)/shard_map/ppermute | solution.py:48
  27.8 2.6 %collective-permute-start.9 = (bf16[512,512]{1,0:T(8,128)(2,1)S(1)}, bf16[512,512]{1,0:T(8,128)(2,1)S(1)}, u32[]{:S(2)}, u32[]{:S(2)}) collective-permute-start(bf16[512,512]{1,0:T(8,128)(2,1)S(1)} %get-tuple-element.101), channel_id=1, source_target_pairs={{0,6},{1,7},{2,0},{3,1},{4,2},{5,3},{6,4},{7,5},{8,14},{9,15},{10,... | collective-permute-start | bytes 1572872 | tf_op jit(solution)/shard_map/ppermute | solution.py:36
  30.4 3.5 %shard_map.130 = (bf16[512,512]{1,0:T(8,128)(2,1)S(1)}, bf16[512,512]{1,0:T(8,128)(2,1)S(1)}, bf16[512,512]{1,0:T(8,128)(2,1)S(1)}, bf16[512,512]{1,0:T(8,128)(2,1)S(1)}, bf16[512,2048]{1,0:T(8,128)(2,1)S(1)}) custom-call(bf16[256,4096]{1,0:T(8,128)(2,1)S(1)} %copy-done.8, bf16[256,4096]{1,0:T(8,128)(2,1)} %collective-permute-done.oth.refs_0_, ...), custom_call_target="tpu_custom_call" | custom-call | flops 33999998976 | tf_op jit(solution)/shard_map/pallas_call | solution.py:74
  35.7 4.6 %collective-permute-done.9 = bf16[512,512]{1,0:T(8,128)(2,1)S(1)} collective-permute-done((bf16[512,512]{1,0:T(8,128)(2,1)S(1)}, bf16[512,512]{1,0:T(8,128)(2,1)S(1)}, u32[]{:S(2)}, u32[]{:S(2)}) %collective-permute-start.9) | collective-permute-done | bytes 524320 | tf_op jit(solution)/shard_map/ppermute | solution.py:36
  40.5 3.5 %collective-permute-start.13 = (bf16[512,512]{1,0:T(8,128)(2,1)S(1)}, bf16[512,512]{1,0:T(8,128)(2,1)S(1)}, u32[]{:S(2)}, u32[]{:S(2)}) collective-permute-start(bf16[512,512]{1,0:T(8,128)(2,1)S(1)} %add.29), channel_id=1, source_target_pairs={{0,6},{1,7},{2,0},{3,1},{4,2},{5,3},{6,4},{7,5},{8,14},{9,15},{10,... | collective-permute-start | bytes 1572872 | tf_op jit(solution)/shard_map/ppermute | solution.py:36
  44.0 2.4 %shard_map.131.first = f32[512,512]{1,0:T(8,128)S(1)} custom-call(bf16[512,2048]{1,0:T(8,128)(2,1)S(1)} %get-tuple-element.104.hid, bf16[512,512]{1,0:T(8,128)(2,1)S(1)} %collective-permute-done.8.w0.refs_5_, bf16[512,512]{1,0:T(8,128)(2,1)} %collective-permute-done.3.w1.refs_6_, bf16[512,512]{1,0:T(8,128)(2,1)} %collective-permute-done.4.w2.refs_7_, ...), custom_call_target="tpu_custom_call" | custom-call | flops 24999999488 | tf_op jit(solution)/shard_map/pallas_call | solution.py:74
  46.5 1.3 %collective-permute-start.11 = (bf16[128,512]{1,0:T(8,128)(2,1)S(1)}, bf16[128,512]{1,0:T(8,128)(2,1)S(1)}, u32[]{:S(2)}, u32[]{:S(2)}) collective-permute-start(bf16[128,512]{1,0:T(8,128)(2,1)S(1)} %add.30), channel_id=1, source_target_pairs={{0,32},{16,48},{32,0},{48,16},{64,96},{80,112},{96,64},{112,80},{1... | collective-permute-start | bytes 393224 | tf_op jit(solution)/shard_map/ppermute | solution.py:54
  47.8 2.1 %collective-permute-start.16 = (bf16[512,512]{1,0:T(8,128)(2,1)S(1)}, bf16[512,512]{1,0:T(8,128)(2,1)}, u32[]{:S(2)}, u32[]{:S(2)}) collective-permute-start(bf16[512,512]{1,0:T(8,128)(2,1)S(1)} %collective-permute-done.5.w3.refs_12_), channel_id=1, source_target_pairs={{0,6},{1,7},{2,0},{3,1},{4,2},{5,3},{6,4},{7,5},{8,14},{9,15},{10,... | collective-permute-start | bytes 1572872 | tf_op jit(solution)/shard_map/ppermute | solution.py:36
  49.9 2.9 %collective-permute-done.12.a = bf16[512,512]{1,0:T(8,128)(2,1)S(1)} collective-permute-done((bf16[512,512]{1,0:T(8,128)(2,1)S(1)}, bf16[512,512]{1,0:T(8,128)(2,1)S(1)}, u32[]{:S(2)}, u32[]{:S(2)}) %collective-permute-start.12) | collective-permute-done | bytes 524320 | tf_op jit(solution)/shard_map/ppermute | solution.py:32
  54.7 9.7 %collective-permute-done.10.w1.refs_10_ = bf16[512,512]{1,0:T(8,128)(2,1)} collective-permute-done((bf16[512,512]{1,0:T(8,128)(2,1)S(1)}, bf16[512,512]{1,0:T(8,128)(2,1)}, u32[]{:S(2)}, u32[]{:S(2)}) %collective-permute-start.10) | collective-permute-done | bytes 524320 | tf_op jit(solution)/shard_map/ppermute | solution.py:32
  64.5 1.5 %collective-permute-start.15 = (bf16[128,512]{1,0:T(8,128)(2,1)}, bf16[128,512]{1,0:T(8,128)(2,1)}, u32[]{:S(2)}, u32[]{:S(2)}) collective-permute-start(bf16[128,512]{1,0:T(8,128)(2,1)} %add.31), channel_id=1, source_target_pairs={{0,128},{16,144},{32,160},{48,176},{64,192},{80,208},{96,224},{112... | collective-permute-start | bytes 393224 | tf_op jit(solution)/shard_map/ppermute | solution.py:48
  66.0 1.5 %collective-permute-start.18 = (bf16[512,512]{1,0:T(8,128)(2,1)}, bf16[512,512]{1,0:T(8,128)(2,1)S(1)}, u32[]{:S(2)}, u32[]{:S(2)}) collective-permute-start(bf16[512,512]{1,0:T(8,128)(2,1)} %copy-done.4), channel_id=1, source_target_pairs={{0,8},{1,9},{2,10},{3,11},{4,12},{5,13},{6,14},{7,15},{8,0},{9,1},... | collective-permute-start | bytes 1572872 | tf_op jit(solution)/shard_map/ppermute | solution.py:40
  67.5 2.7 %collective-permute-start.19 = (bf16[512,512]{1,0:T(8,128)(2,1)S(1)}, bf16[512,512]{1,0:T(8,128)(2,1)S(1)}, u32[]{:S(2)}, u32[]{:S(2)}) collective-permute-start(bf16[512,512]{1,0:T(8,128)(2,1)S(1)} %get-tuple-element.127), channel_id=1, source_target_pairs={{0,6},{1,7},{2,0},{3,1},{4,2},{5,3},{6,4},{7,5},{8,14},{9,15},{10,... | collective-permute-start | bytes 1572872 | tf_op jit(solution)/shard_map/ppermute | solution.py:36
  70.2 1.2 %maximum_select_fusion.a = bf16[256,512]{1,0:T(8,128)(2,1)S(1)} fusion(bf16[128,512]{1,0:T(8,128)(2,1)} %collective-permute-done.15, bf16[128,512]{1,0:T(8,128)(2,1)} %add.31, pred[]{:T(512)S(6)} %eq.3), kind=kLoop, calls=%fused_computation | loop fusion | flops 1179648 | bytes 524289 | tf_op jit(solution)/shard_map/jit(_where)/select_n | solution.py:552
  72.5 5.4 %collective-permute-done.14.w0.refs_9_ = bf16[512,512]{1,0:T(8,128)(2,1)} collective-permute-done((bf16[512,512]{1,0:T(8,128)(2,1)}, bf16[512,512]{1,0:T(8,128)(2,1)}, u32[]{:S(2)}, u32[]{:S(2)}) %collective-permute-start.14) | collective-permute-done | bytes 524320 | tf_op jit(solution)/shard_map/ppermute | solution.py:32
  77.8 1.6 %copy-done.9 = bf16[256,4096]{1,0:T(8,128)(2,1)S(1)} copy-done((bf16[256,4096]{1,0:T(8,128)(2,1)S(1)}, bf16[256,4096]{1,0:T(8,128)(2,1)}, u32[]{:S(2)}) %copy-start.9) | copy-done | bytes 2097176
  79.4 1.2 %copy-done.12 = f32[512,512]{1,0:T(8,128)S(1)} copy-done((f32[512,512]{1,0:T(8,128)S(1)}, f32[512,512]{1,0:T(8,128)}, u32[]{:S(2)}) %copy-start.12) | copy-done | bytes 1048600
  81.6 3.7 %shard_map.133 = (f32[256,640]{1,0:T(8,128)S(1)}, bf16[256,640]{1,0:T(8,128)(2,1)S(1)}) custom-call(bf16[256,4096]{1,0:T(8,128)(2,1)S(1)} %copy-done.9, bf16[256,4096]{1,0:T(8,128)(2,1)} %collective-permute-done.oth.refs_0_, f32[1,8192]{1,0:T(1,128)S(1)} %copy-done.6, f32[256,128]{1,0:T(8,128)S(1)} %copy-done.17, ...), custom_call_target="tpu_custom_call" | custom-call | flops 24999999488 | tf_op jit(solution)/shard_map/pallas_call | solution.py:74
  85.3 2.6 %collective-permute-start.17 = (bf16[256,640]{1,0:T(8,128)(2,1)S(1)}, bf16[256,640]{1,0:T(8,128)(2,1)S(1)}, u32[]{:S(2)}, u32[]{:S(2)}) collective-permute-start(bf16[256,640]{1,0:T(8,128)(2,1)S(1)} %get-tuple-element.124), channel_id=1, source_target_pairs={{0,1},{1,0},{2,3},{3,2},{4,5},{5,4},{6,7},{7,6},{8,9},{9,8},{10,11... | collective-permute-start | bytes 983048 | tf_op jit(solution)/shard_map/ppermute | solution.py:44
  87.9 1.6 %shard_map.134 = (f32[512,512]{1,0:T(8,128)}, f32[512,512]{1,0:T(8,128)}) custom-call(bf16[256,512]{1,0:T(8,128)(2,1)S(1)} %maximum_select_fusion.a, bf16[256,512]{1,0:T(8,128)(2,1)S(1)} %collective-permute-done.20.b, f32[512,512]{1,0:T(8,128)S(1)} %copy-done.1, f32[512,512]{1,0:T(8,128)S(1)} %copy-done.2), custom_call_target="tpu_custom_call" | custom-call | flops 20000000000 | tf_op jit(solution)/shard_map/pallas_call | solution.py:74
  89.7 2.9 %collective-permute-start.23 = (bf16[512,512]{1,0:T(8,128)(2,1)S(1)}, bf16[512,512]{1,0:T(8,128)(2,1)S(1)}, u32[]{:S(2)}, u32[]{:S(2)}) collective-permute-start(bf16[512,512]{1,0:T(8,128)(2,1)S(1)} %add.32), channel_id=1, source_target_pairs={{0,6},{1,7},{2,0},{3,1},{4,2},{5,3},{6,4},{7,5},{8,14},{9,15},{10,... | collective-permute-start | bytes 1572872 | tf_op jit(solution)/shard_map/ppermute | solution.py:36
  93.6 4.7 %shard_map.135 = (bf16[256,4096]{1,0:T(8,128)(2,1)S(1)}, bf16[256,512]{1,0:T(8,128)(2,1)}, f32[256,128]{1,0:T(8,128)S(1)}) custom-call(bf16[256,4096]{1,0:T(8,128)(2,1)} %collective-permute-done.oth.refs_0_, f32[1,8192]{1,0:T(1,128)S(1)} %copy-done.6, bf16[256,640]{1,0:T(8,128)(2,1)} %collective-permute-done.1.ext.refs_2_, ...), custom_call_target="tpu_custom_call" | custom-call | flops 54999998464 | tf_op jit(solution)/shard_map/pallas_call | solution.py:74
  98.3 2.2 %collective-permute-start.21 = (bf16[256,4096]{1,0:T(8,128)(2,1)S(1)}, bf16[256,4096]{1,0:T(8,128)(2,1)S(1)}, u32[]{:S(2)}, u32[]{:S(2)}) collective-permute-start(bf16[256,4096]{1,0:T(8,128)(2,1)S(1)} %get-tuple-element.136), channel_id=1, source_target_pairs={{0,1},{1,0},{2,3},{3,2},{4,5},{5,4},{6,7},{7,6},{8,9},{9,8},{10,11... | collective-permute-start | bytes 6291464 | tf_op jit(solution)/shard_map/ppermute | solution.py:44
  100.5 3.8 %shard_map.136._ = bf16[256,8192]{1,0:T(8,128)(2,1)} custom-call(bf16[256,4096]{1,0:T(8,128)(2,1)S(1)} %copy-done.10, f32[1,8192]{1,0:T(1,128)S(1)} %copy-done.6, f32[256,128]{1,0:T(8,128)S(1)} %copy-done.18, bf16[256,512]{1,0:T(8,128)(2,1)S(1)} %copy-done.5, f32[256,128]{1,0:T(8,128)S(1)} %get-tuple-element.139.refs_4_, ...), custom_call_target="tpu_custom_call" | custom-call | flops 46999998464 | tf_op jit(solution)/shard_map/pallas_call | solution.py:74
  104.3 1.4 %shard_map.137 = bf16[256,8192]{1,0:T(8,128)(2,1)} custom-call(bf16[256,8192]{1,0:T(8,128)(2,1)} %shard_map.136._, bf16[256,4096]{1,0:T(8,128)(2,1)S(1)} %collective-permute-done.21.arr), custom_call_target="tpu_custom_call", output_to_operand_aliasing={{}: (0, {})} | custom-call | flops 14000000000 | tf_op jit(solution)/shard_map/pallas_call | solution.py:74
  105.7 1.6 %shard_map.138 = (bf16[512,512]{1,0:T(8,128)(2,1)}, bf16[1,512]{1,0:T(2,128)(2,1)}) custom-call(bf16[512,512]{1,0:T(8,128)(2,1)S(1)} %copy-done.14, bf16[512,512]{1,0:T(8,128)(2,1)S(1)} %collective-permute-done.22.a, bf16[512,512]{1,0:T(8,128)(2,1)S(1)} %collective-permute-done.23.b, bf16[512,512]{1,0:T(8,128)(2,1)S(1)} %collective-permute-done.18.fr, ...), custom_call_target="tpu_custom_call" | custom-call | flops 28999999488 | tf_op jit(solution)/shard_map/pallas_call | solution.py:74
  (74 shorter events, 9.1 us)
Async XLA Ops:
  0.6 11.0 %copy-start = (s32[1,512,512]{2,1,0:T(8,128)S(1)}, s32[1,512,512]{2,1,0:T(8,128)}, u32[]{:S(2)}) copy-start(s32[1,512,512]{2,1,0:T(8,128)} %param.12) | copy-start | bytes 3145732
  0.6 11.0 %copy-start.7 = (s32[1,512,4]{1,2,0:T(4,128)S(1)}, s32[1,512,4]{1,2,0:T(4,128)}, u32[]{:S(2)}) copy-start(s32[1,512,4]{1,2,0:T(4,128)} %param.13) | copy-start | bytes 24580
  0.7 24.1 %collective-permute-start.4 = (bf16[512,512]{1,0:T(8,128)(2,1)}, bf16[512,512]{1,0:T(8,128)(2,1)}, u32[]{:S(2)}, u32[]{:S(2)}) collective-permute-start(bf16[512,512]{1,0:T(8,128)(2,1)} %bitcast.6), channel_id=1, source_target_pairs={{0,6},{1,7},{2,0},{3,1},{4,2},{5,3},{6,4},{7,5},{8,14},{9,15},{10,... | collective-permute-start | bytes 1572872 | tf_op jit(solution)/shard_map/ppermute | solution.py:36
  4.3 20.5 %collective-permute-start.3 = (bf16[512,512]{1,0:T(8,128)(2,1)}, bf16[512,512]{1,0:T(8,128)(2,1)}, u32[]{:S(2)}, u32[]{:S(2)}) collective-permute-start(bf16[512,512]{1,0:T(8,128)(2,1)} %bitcast.7), channel_id=1, source_target_pairs={{0,2},{1,3},{2,4},{3,5},{4,6},{5,7},{6,0},{7,1},{8,10},{9,11},{10,... | collective-permute-start | bytes 1572872 | tf_op jit(solution)/shard_map/ppermute | solution.py:32
  9.7 3.4 %collective-permute-start.1 = (bf16[256,640]{1,0:T(8,128)(2,1)}, bf16[256,640]{1,0:T(8,128)(2,1)}, u32[]{:S(2)}, u32[]{:S(2)}) collective-permute-start(bf16[256,640]{1,0:T(8,128)(2,1)} %get-tuple-element.78), channel_id=1, source_target_pairs={{0,1},{1,0},{2,3},{3,2},{4,5},{5,4},{6,7},{7,6},{8,9},{9,8},{10,11... | collective-permute-start | bytes 983048 | tf_op jit(solution)/shard_map/ppermute | solution.py:44
  11.5 8.2 %collective-permute-start = (bf16[256,4096]{1,0:T(8,128)(2,1)}, bf16[256,4096]{1,0:T(8,128)(2,1)}, u32[]{:S(2)}, u32[]{:S(2)}) collective-permute-start(bf16[256,4096]{1,0:T(8,128)(2,1)} %get-tuple-element.77), channel_id=1, source_target_pairs={{0,1},{1,0},{2,3},{3,2},{4,5},{5,4},{6,7},{7,6},{8,9},{9,8},{10,11... | collective-permute-start | bytes 6291464 | tf_op jit(solution)/shard_map/ppermute | solution.py:44
  11.6 8.1 %copy-start.5 = (bf16[256,512]{1,0:T(8,128)(2,1)S(1)}, bf16[256,512]{1,0:T(8,128)(2,1)}, u32[]{:S(2)}) copy-start(bf16[256,512]{1,0:T(8,128)(2,1)} %refs_3_.1) | copy-start | bytes 786436
  11.6 8.1 %copy-start.6 = (f32[1,8192]{1,0:T(1,128)S(1)}, f32[1,8192]{1,0:T(1,128)}, u32[]{:S(2)}) copy-start(f32[1,8192]{1,0:T(1,128)} %gain.7) | copy-start | bytes 98308
  11.6 8.1 %copy-start.15 = (f32[256,128]{1,0:T(8,128)S(1)}, f32[256,128]{1,0:T(8,128)}, u32[]{:S(2)}) copy-start(f32[256,128]{1,0:T(8,128)} %get-tuple-element.79.irr.refs_2_) | copy-start | bytes 393220
  12.3 12.5 %collective-permute-start.2 = (bf16[256,512]{1,0:T(8,128)(2,1)S(1)}, bf16[256,512]{1,0:T(8,128)(2,1)S(1)}, u32[]{:S(2)}, u32[]{:S(2)}) collective-permute-start(bf16[256,512]{1,0:T(8,128)(2,1)S(1)} %get-tuple-element.85), channel_id=1, source_target_pairs={{0,64},{16,80},{32,96},{48,112},{64,0},{80,16},{96,32},{112,48},{1... | collective-permute-start | bytes 786440 | tf_op jit(solution)/shard_map/ppermute | solution.py:48
  13.1 34.7 %collective-permute-start.5 = (bf16[512,512]{1,0:T(8,128)(2,1)S(1)}, bf16[512,512]{1,0:T(8,128)(2,1)S(1)}, u32[]{:S(2)}, u32[]{:S(2)}) collective-permute-start(bf16[512,512]{1,0:T(8,128)(2,1)S(1)} %bitcast.8), channel_id=1, source_target_pairs={{0,8},{1,9},{2,10},{3,11},{4,12},{5,13},{6,14},{7,15},{8,0},{9,1},... | collective-permute-start | bytes 1572872 | tf_op jit(solution)/shard_map/ppermute | solution.py:40
  21.3 9.1 %copy-start.16 = (f32[256,128]{1,0:T(8,128)S(1)}, f32[256,128]{1,0:T(8,128)}, u32[]{:S(2)}) copy-start(f32[256,128]{1,0:T(8,128)} %get-tuple-element.79.irr.refs_2_) | copy-start | bytes 393220
  24.9 9.8 %collective-permute-start.6 = (bf16[128,512]{1,0:T(8,128)(2,1)S(1)}, bf16[128,512]{1,0:T(8,128)(2,1)S(1)}, u32[]{:S(2)}, u32[]{:S(2)}) collective-permute-start(bf16[128,512]{1,0:T(8,128)(2,1)S(1)} %get-tuple-element.148), channel_id=1, source_target_pairs={{0,128},{16,144},{32,160},{48,176},{64,192},{80,208},{96,224},{112... | collective-permute-start | bytes 393224 | tf_op jit(solution)/shard_map/ppermute | solution.py:48
  27.4 16.6 %collective-permute-start.8 = (bf16[512,512]{1,0:T(8,128)(2,1)}, bf16[512,512]{1,0:T(8,128)(2,1)S(1)}, u32[]{:S(2)}, u32[]{:S(2)}) collective-permute-start(bf16[512,512]{1,0:T(8,128)(2,1)} %collective-permute-done.3.w1.refs_6_), channel_id=1, source_target_pairs={{0,2},{1,3},{2,4},{3,5},{4,6},{5,7},{6,0},{7,1},{8,10},{9,11},{10,... | collective-permute-start | bytes 1572872 | tf_op jit(solution)/shard_map/ppermute | solution.py:32
  27.8 12.6 %collective-permute-start.9 = (bf16[512,512]{1,0:T(8,128)(2,1)S(1)}, bf16[512,512]{1,0:T(8,128)(2,1)S(1)}, u32[]{:S(2)}, u32[]{:S(2)}) collective-permute-start(bf16[512,512]{1,0:T(8,128)(2,1)S(1)} %get-tuple-element.101), channel_id=1, source_target_pairs={{0,6},{1,7},{2,0},{3,1},{4,2},{5,3},{6,4},{7,5},{8,14},{9,15},{10,... | collective-permute-start | bytes 1572872 | tf_op jit(solution)/shard_map/ppermute | solution.py:36
  30.4 22.4 %collective-permute-start.12 = (bf16[512,512]{1,0:T(8,128)(2,1)S(1)}, bf16[512,512]{1,0:T(8,128)(2,1)S(1)}, u32[]{:S(2)}, u32[]{:S(2)}) collective-permute-start(bf16[512,512]{1,0:T(8,128)(2,1)S(1)} %get-tuple-element.112), channel_id=1, source_target_pairs={{0,2},{1,3},{2,4},{3,5},{4,6},{5,7},{6,0},{7,1},{8,10},{9,11},{10,... | collective-permute-start | bytes 1572872 | tf_op jit(solution)/shard_map/ppermute | solution.py:32
  34.7 11.7 %collective-permute-start.7 = (bf16[128,512]{1,0:T(8,128)(2,1)S(1)}, bf16[128,512]{1,0:T(8,128)(2,1)S(1)}, u32[]{:S(2)}, u32[]{:S(2)}) collective-permute-start(bf16[128,512]{1,0:T(8,128)(2,1)S(1)} %add.28), channel_id=1, source_target_pairs={{0,16},{16,0},{32,48},{48,32},{64,80},{80,64},{96,112},{112,96},{1... | collective-permute-start | bytes 393224 | tf_op jit(solution)/shard_map/ppermute | solution.py:54
  40.5 12.5 %collective-permute-start.13 = (bf16[512,512]{1,0:T(8,128)(2,1)S(1)}, bf16[512,512]{1,0:T(8,128)(2,1)S(1)}, u32[]{:S(2)}, u32[]{:S(2)}) collective-permute-start(bf16[512,512]{1,0:T(8,128)(2,1)S(1)} %add.29), channel_id=1, source_target_pairs={{0,6},{1,7},{2,0},{3,1},{4,2},{5,3},{6,4},{7,5},{8,14},{9,15},{10,... | collective-permute-start | bytes 1572872 | tf_op jit(solution)/shard_map/ppermute | solution.py:36
  46.5 7.5 %collective-permute-start.11 = (bf16[128,512]{1,0:T(8,128)(2,1)S(1)}, bf16[128,512]{1,0:T(8,128)(2,1)S(1)}, u32[]{:S(2)}, u32[]{:S(2)}) collective-permute-start(bf16[128,512]{1,0:T(8,128)(2,1)S(1)} %add.30), channel_id=1, source_target_pairs={{0,32},{16,48},{32,0},{48,16},{64,96},{80,112},{96,64},{112,80},{1... | collective-permute-start | bytes 393224 | tf_op jit(solution)/shard_map/ppermute | solution.py:54
  47.8 19.8 %collective-permute-start.16 = (bf16[512,512]{1,0:T(8,128)(2,1)S(1)}, bf16[512,512]{1,0:T(8,128)(2,1)}, u32[]{:S(2)}, u32[]{:S(2)}) collective-permute-start(bf16[512,512]{1,0:T(8,128)(2,1)S(1)} %collective-permute-done.5.w3.refs_12_), channel_id=1, source_target_pairs={{0,6},{1,7},{2,0},{3,1},{4,2},{5,3},{6,4},{7,5},{8,14},{9,15},{10,... | collective-permute-start | bytes 1572872 | tf_op jit(solution)/shard_map/ppermute | solution.py:36
  49.9 14.6 %collective-permute-start.10 = (bf16[512,512]{1,0:T(8,128)(2,1)S(1)}, bf16[512,512]{1,0:T(8,128)(2,1)}, u32[]{:S(2)}, u32[]{:S(2)}) collective-permute-start(bf16[512,512]{1,0:T(8,128)(2,1)S(1)} %collective-permute-done.5.w3.refs_12_), channel_id=1, source_target_pairs={{0,2},{1,3},{2,4},{3,5},{4,6},{5,7},{6,0},{7,1},{8,10},{9,11},{10,... | collective-permute-start | bytes 1572872 | tf_op jit(solution)/shard_map/ppermute | solution.py:32
  64.5 13.4 %collective-permute-start.14 = (bf16[512,512]{1,0:T(8,128)(2,1)}, bf16[512,512]{1,0:T(8,128)(2,1)}, u32[]{:S(2)}, u32[]{:S(2)}) collective-permute-start(bf16[512,512]{1,0:T(8,128)(2,1)} %collective-permute-done.10.w1.refs_10_), channel_id=1, source_target_pairs={{0,2},{1,3},{2,4},{3,5},{4,6},{5,7},{6,0},{7,1},{8,10},{9,11},{10,... | collective-permute-start | bytes 1572872 | tf_op jit(solution)/shard_map/ppermute | solution.py:32
  64.5 5.7 %collective-permute-start.15 = (bf16[128,512]{1,0:T(8,128)(2,1)}, bf16[128,512]{1,0:T(8,128)(2,1)}, u32[]{:S(2)}, u32[]{:S(2)}) collective-permute-start(bf16[128,512]{1,0:T(8,128)(2,1)} %add.31), channel_id=1, source_target_pairs={{0,128},{16,144},{32,160},{48,176},{64,192},{80,208},{96,224},{112... | collective-permute-start | bytes 393224 | tf_op jit(solution)/shard_map/ppermute | solution.py:48
  66.0 27.6 %collective-permute-start.18 = (bf16[512,512]{1,0:T(8,128)(2,1)}, bf16[512,512]{1,0:T(8,128)(2,1)S(1)}, u32[]{:S(2)}, u32[]{:S(2)}) collective-permute-start(bf16[512,512]{1,0:T(8,128)(2,1)} %copy-done.4), channel_id=1, source_target_pairs={{0,8},{1,9},{2,10},{3,11},{4,12},{5,13},{6,14},{7,15},{8,0},{9,1},... | collective-permute-start | bytes 1572872 | tf_op jit(solution)/shard_map/ppermute | solution.py:40
  67.5 22.0 %collective-permute-start.19 = (bf16[512,512]{1,0:T(8,128)(2,1)S(1)}, bf16[512,512]{1,0:T(8,128)(2,1)S(1)}, u32[]{:S(2)}, u32[]{:S(2)}) collective-permute-start(bf16[512,512]{1,0:T(8,128)(2,1)S(1)} %get-tuple-element.127), channel_id=1, source_target_pairs={{0,6},{1,7},{2,0},{3,1},{4,2},{5,3},{6,4},{7,5},{8,14},{9,15},{10,... | collective-permute-start | bytes 1572872 | tf_op jit(solution)/shard_map/ppermute | solution.py:36
  71.4 16.5 %collective-permute-start.20 = (bf16[256,512]{1,0:T(8,128)(2,1)S(1)}, bf16[256,512]{1,0:T(8,128)(2,1)S(1)}, u32[]{:S(2)}, u32[]{:S(2)}) collective-permute-start(bf16[256,512]{1,0:T(8,128)(2,1)S(1)} %maximum_select_fusion.a), channel_id=1, source_target_pairs={{0,64},{16,80},{32,96},{48,112},{64,0},{80,16},{96,32},{112,48},{1... | collective-permute-start | bytes 786440 | tf_op jit(solution)/shard_map/ppermute | solution.py:48
  85.3 8.3 %collective-permute-start.17 = (bf16[256,640]{1,0:T(8,128)(2,1)S(1)}, bf16[256,640]{1,0:T(8,128)(2,1)S(1)}, u32[]{:S(2)}, u32[]{:S(2)}) collective-permute-start(bf16[256,640]{1,0:T(8,128)(2,1)S(1)} %get-tuple-element.124), channel_id=1, source_target_pairs={{0,1},{1,0},{2,3},{3,2},{4,5},{5,4},{6,7},{7,6},{8,9},{9,8},{10,11... | collective-permute-start | bytes 983048 | tf_op jit(solution)/shard_map/ppermute | solution.py:44
  87.9 17.8 %collective-permute-start.22 = (bf16[512,512]{1,0:T(8,128)(2,1)S(1)}, bf16[512,512]{1,0:T(8,128)(2,1)S(1)}, u32[]{:S(2)}, u32[]{:S(2)}) collective-permute-start(bf16[512,512]{1,0:T(8,128)(2,1)S(1)} %get-tuple-element.142), channel_id=1, source_target_pairs={{0,2},{1,3},{2,4},{3,5},{4,6},{5,7},{6,0},{7,1},{8,10},{9,11},{10,... | collective-permute-start | bytes 1572872 | tf_op jit(solution)/shard_map/ppermute | solution.py:32
  89.7 16.1 %collective-permute-start.23 = (bf16[512,512]{1,0:T(8,128)(2,1)S(1)}, bf16[512,512]{1,0:T(8,128)(2,1)S(1)}, u32[]{:S(2)}, u32[]{:S(2)}) collective-permute-start(bf16[512,512]{1,0:T(8,128)(2,1)S(1)} %add.32), channel_id=1, source_target_pairs={{0,6},{1,7},{2,0},{3,1},{4,2},{5,3},{6,4},{7,5},{8,14},{9,15},{10,... | collective-permute-start | bytes 1572872 | tf_op jit(solution)/shard_map/ppermute | solution.py:36
  93.6 6.9 %copy-start.10 = (bf16[256,4096]{1,0:T(8,128)(2,1)S(1)}, bf16[256,4096]{1,0:T(8,128)(2,1)}, u32[]{:S(2)}) copy-start(bf16[256,4096]{1,0:T(8,128)(2,1)} %get-tuple-element.86.own.own_x.refs_0_) | copy-start | bytes 6291460
  93.6 6.9 %copy-start.18 = (f32[256,128]{1,0:T(8,128)S(1)}, f32[256,128]{1,0:T(8,128)}, u32[]{:S(2)}) copy-start(f32[256,128]{1,0:T(8,128)} %get-tuple-element.79.irr.refs_2_) | copy-start | bytes 393220
  98.3 6.0 %collective-permute-start.21 = (bf16[256,4096]{1,0:T(8,128)(2,1)S(1)}, bf16[256,4096]{1,0:T(8,128)(2,1)S(1)}, u32[]{:S(2)}, u32[]{:S(2)}) collective-permute-start(bf16[256,4096]{1,0:T(8,128)(2,1)S(1)} %get-tuple-element.136), channel_id=1, source_target_pairs={{0,1},{1,0},{2,3},{3,2},{4,5},{5,4},{6,7},{7,6},{8,9},{9,8},{10,11... | collective-permute-start | bytes 6291464 | tf_op jit(solution)/shard_map/ppermute | solution.py:44
  (11 other events, 29.3 us)

commit v4 on v3

--- a/solution.py
+++ b/solution.py
@@ -433,7 +433,7 @@
         kernel,
         (jax.ShapeDtypeStruct((h, cols), BF16),) * 2,
         (quantized, exponents),
-        cost=20.0,
+        cost=1.0,
         scratch_shapes=[pltpu.VMEM((n, nb), F32)],
     )
 
@@ -507,11 +507,8 @@
     f_from_down = to_up(f_plus)
 
     keep, x1 = after((keep, x1), n_up)
-    half = keep + x1
-    q = half.shape[0] // 2
-    first = x_bit(2) * q
-    part = lax.dynamic_slice_in_dim(half, first, q)
-    x2 = swap_x(lax.dynamic_slice_in_dim(half, q - first, q), 2)
+    part = keep + x1
+    x2 = swap_x(part, 2)
 
     other, extra = after((other, extra), part)
     g_opposite, g_minus, g_plus, g_own, hidden_near = partials(
@@ -528,30 +525,26 @@
     near_rows = (n_opposite, n_down, n_up, weight)
     *near_rows, hidden_near = after((*near_rows, hidden_near), f_minus)
     near_keys = project_near(hidden_near, near_rows)
-    part, z1 = after((part, z1), near_keys)
+
+    (far_weight,) = after((far_weight,), near_keys)
+    a_down = to_up(far_weight)
+    a_up = to_down(far_weight)
+    part, z1 = after((part, z1), far_weight)
     part = part + z1
     z2 = swap_z(part, 2)
 
-    (far_weight,) = after((far_weight,), part)
-    a_down = to_up(far_weight)
-    a_up = to_down(far_weight)
-
-    f_own, f_from_down, f_from_up = after((f_own, f_from_down, f_from_up), far_weight)
+    f_own, f_from_down, f_from_up = after((f_own, f_from_down, f_from_up), part)
     f_total = side_sum(f_own, f_from_down, f_from_up)
     far_sum = to_far(f_total)
     part, z2 = after((part, z2), f_total)
     part = part + z2
-    x3 = swap_x(part, 2)
+    x3 = swap_x(part, 1)
     (a_down,) = after((a_down,), part)
     a_opposite = to_up(a_down)
 
     g_opposite, a_up = after((g_opposite, a_up), a_down)
     g_step = to_down(g_opposite)
-    part, x3 = after((part, x3), a_up)
-    pair = jnp.concatenate([part, x3])
-    half = jnp.where(x_bit(2) == 0, pair, jnp.roll(pair, q, axis=0))
-    x4 = swap_x(half, 1)
-    g_plus, a_opposite = after((g_plus, a_opposite), half)
+    g_plus, a_opposite = after((g_plus, a_opposite), a_up)
     g_from_down = to_up(g_plus)
 
     far_rows = (a_opposite, a_down, a_up, far_weight)
@@ -559,8 +552,8 @@
         mine, other, gains, ir, extra, cot, far_rows, near_keys
     )
     arrived = to_core(keys_sent)
-    half, x4 = after((half, x4), keys_sent)
-    new_momentum, new_params = outer_step(half, x4, momentum, outer_params)
+    part, x3 = after((part, x3), keys_sent)
+    new_momentum, new_params = outer_step(part, x3, momentum, outer_params)
     g_minus, g_step = after((g_minus, g_step), new_params)
     g_minus = g_minus + g_step
     g_from_up = to_down(g_minus)

time: 108 us -> 104 us (0.963)
  the two profiles are of different devices: /device:TPU:1 before, /device:TPU:9 now
where the time goes in v4:
time: 104 us; the launch traced here: 103 us
  waiting for transfers between devices  41.3 us (40%)
  starting transfers between devices  39.3 us (38%)
  Pallas kernels  21.5 us (21%)
    pallas_call x12, Pallas kernels, call(): pl.pallas_call(kernel, out_shape=outs, compiler_params=pltpu.CompilerPara...  21.5 us
    ppermute x2, waiting for transfers between devices, swap_z(): lax.ppermute(v, 'replica', [(x * N_ZL + z, x * N_ZL + (z ^ bit)) for x in...  15.3 us
    ppermute x6, starting transfers between devices, to_down(): return lax.ppermute(v, 'dp', dp_moves(dy=-1))  13.2 us
    ppermute x2, waiting for transfers between devices, to_far(): return lax.ppermute(v, 'dp', dp_moves(dz=1))  10.2 us
    ppermute x2, starting transfers between devices, to_far(): return lax.ppermute(v, 'dp', dp_moves(dz=1))  9.56 us
    ppermute x6, waiting for transfers between devices, to_up(): return lax.ppermute(v, 'dp', dp_moves(dy=1))  6.38 us
    ppermute x6, waiting for transfers between devices, to_down(): return lax.ppermute(v, 'dp', dp_moves(dy=-1))  6.09 us
    ppermute x4, starting transfers between devices, to_core(): return lax.ppermute(v, 'dp', dp_moves(dc=1))  5.48 us
  transfers between devices with their start and end apart: 23, of which 12 were waited for; matrix products, arithmetic and copies ran while one was open for 1% of the time, Pallas kernels for 14%

profile of v4, /device:TPU:9, one launch (start us, length us, event | category | flops | bytes accessed | tf_op | source)
XLA Modules:
  0.0 103.5 jit_solution(13908830677295348547)
XLA Ops:
  0.7 5.5 %shard_map.127 = (bf16[256,4096]{1,0:T(8,128)(2,1)}, bf16[256,4096]{1,0:T(8,128)(2,1)}, bf16[256,640]{1,0:T(8,128)(2,1)}, f32[256,128]{1,0:T(8,128)}) custom-call(bf16[256,8192]{1,0:T(8,128)(2,1)} %tok.1, bf16[256,512]{1,0:T(8,128)(2,1)} %refs_3_.1), custom_call_target="tpu_custom_call" | custom-call | flops 32000000000 | tf_op jit(solution)/shard_map/pallas_call | solution.py:74
  6.9 1.9 %collective-permute-start.4 = (bf16[512,512]{1,0:T(8,128)(2,1)S(1)}, bf16[512,512]{1,0:T(8,128)(2,1)S(1)}, u32[]{:S(2)}, u32[]{:S(2)}) collective-permute-start(bf16[512,512]{1,0:T(8,128)(2,1)S(1)} %bitcast.6), channel_id=1, source_target_pairs={{0,6},{1,7},{2,0},{3,1},{4,2},{5,3},{6,4},{7,5},{8,14},{9,15},{10,... | collective-permute-start | bytes 1572872 | tf_op jit(solution)/shard_map/ppermute | solution.py:36
  11.4 6.9 %collective-permute-start.5 = (bf16[512,512]{1,0:T(8,128)(2,1)S(1)}, bf16[512,512]{1,0:T(8,128)(2,1)S(1)}, u32[]{:S(2)}, u32[]{:S(2)}) collective-permute-start(bf16[512,512]{1,0:T(8,128)(2,1)S(1)} %bitcast.8), channel_id=1, source_target_pairs={{0,8},{1,9},{2,10},{3,11},{4,12},{5,13},{6,14},{7,15},{8,0},{9,1},... | collective-permute-start | bytes 1572872 | tf_op jit(solution)/shard_map/ppermute | solution.py:40
  18.4 1.8 %shard_map.129 = (bf16[512,512]{1,0:T(8,128)(2,1)S(1)}, bf16[512,512]{1,0:T(8,128)(2,1)S(1)}, bf16[512,512]{1,0:T(8,128)(2,1)S(1)}, bf16[512,512]{1,0:T(8,128)(2,1)S(1)}) custom-call(bf16[256,4096]{1,0:T(8,128)(2,1)S(1)} %copy-done.7, bf16[256,4096]{1,0:T(8,128)(2,1)S(1)} %collective-permute-done.oth.refs_0_, f32[1,8192]{1,0:T(1,128)S(1)} %copy-done.5, ...), custom_call_target="tpu_custom_call" | custom-call | flops 33999998976 | tf_op jit(solution)/shard_map/pallas_call | solution.py:74
  20.4 1.6 %collective-permute-done.3.w1.refs_6_ = bf16[512,512]{1,0:T(8,128)(2,1)S(1)} collective-permute-done((bf16[512,512]{1,0:T(8,128)(2,1)S(1)}, bf16[512,512]{1,0:T(8,128)(2,1)S(1)}, u32[]{:S(2)}, u32[]{:S(2)}) %collective-permute-start.3) | collective-permute-done | bytes 524320 | tf_op jit(solution)/shard_map/ppermute | solution.py:32
  22.1 2.7 %collective-permute-start.8 = (bf16[256,512]{1,0:T(8,128)(2,1)S(1)}, bf16[256,512]{1,0:T(8,128)(2,1)S(1)}, u32[]{:S(2)}, u32[]{:S(2)}) collective-permute-start(bf16[256,512]{1,0:T(8,128)(2,1)S(1)} %add.18), channel_id=1, source_target_pairs={{0,128},{16,144},{32,160},{48,176},{64,192},{80,208},{96,224},{112... | collective-permute-start | bytes 786440 | tf_op jit(solution)/shard_map/ppermute | solution.py:48
  24.8 2.4 %collective-permute-start.7 = (bf16[512,512]{1,0:T(8,128)(2,1)S(1)}, bf16[512,512]{1,0:T(8,128)(2,1)S(1)}, u32[]{:S(2)}, u32[]{:S(2)}) collective-permute-start(bf16[512,512]{1,0:T(8,128)(2,1)S(1)} %get-tuple-element.96), channel_id=1, source_target_pairs={{0,6},{1,7},{2,0},{3,1},{4,2},{5,3},{6,4},{7,5},{8,14},{9,15},{10,... | collective-permute-start | bytes 1572872 | tf_op jit(solution)/shard_map/ppermute | solution.py:36
  27.1 1.9 %shard_map.130 = (bf16[512,512]{1,0:T(8,128)(2,1)S(1)}, bf16[512,512]{1,0:T(8,128)(2,1)S(1)}, bf16[512,512]{1,0:T(8,128)(2,1)S(1)}, bf16[512,512]{1,0:T(8,128)(2,1)S(1)}, bf16[512,2048]{1,0:T(8,128)(2,1)S(1)}) custom-call(bf16[256,4096]{1,0:T(8,128)(2,1)S(1)} %copy-done.7, bf16[256,4096]{1,0:T(8,128)(2,1)S(1)} %collective-permute-done.oth.refs_0_, ...), custom_call_target="tpu_custom_call" | custom-call | flops 33999998976 | tf_op jit(solution)/shard_map/pallas_call | solution.py:74
  29.0 1.2 %collective-permute-done.8 = bf16[256,512]{1,0:T(8,128)(2,1)S(1)} collective-permute-done((bf16[256,512]{1,0:T(8,128)(2,1)S(1)}, bf16[256,512]{1,0:T(8,128)(2,1)S(1)}, u32[]{:S(2)}, u32[]{:S(2)}) %collective-permute-start.8) | collective-permute-done | bytes 262176 | tf_op jit(solution)/shard_map/ppermute | solution.py:48
  30.4 2.1 %collective-permute-start.10 = (bf16[256,512]{1,0:T(8,128)(2,1)S(1)}, bf16[256,512]{1,0:T(8,128)(2,1)S(1)}, u32[]{:S(2)}, u32[]{:S(2)}) collective-permute-start(bf16[256,512]{1,0:T(8,128)(2,1)S(1)} %add.19), channel_id=1, source_target_pairs={{0,16},{16,0},{32,48},{48,32},{64,80},{80,64},{96,112},{112,96},{1... | collective-permute-start | bytes 786440 | tf_op jit(solution)/shard_map/ppermute | solution.py:54
  32.5 5.2 %collective-permute-done.7 = bf16[512,512]{1,0:T(8,128)(2,1)S(1)} collective-permute-done((bf16[512,512]{1,0:T(8,128)(2,1)S(1)}, bf16[512,512]{1,0:T(8,128)(2,1)S(1)}, u32[]{:S(2)}, u32[]{:S(2)}) %collective-permute-start.7) | collective-permute-done | bytes 524320 | tf_op jit(solution)/shard_map/ppermute | solution.py:36
  37.8 1.7 %collective-permute-start.13 = (bf16[512,512]{1,0:T(8,128)(2,1)S(1)}, bf16[512,512]{1,0:T(8,128)(2,1)S(1)}, u32[]{:S(2)}, u32[]{:S(2)}) collective-permute-start(bf16[512,512]{1,0:T(8,128)(2,1)S(1)} %add.20), channel_id=1, source_target_pairs={{0,6},{1,7},{2,0},{3,1},{4,2},{5,3},{6,4},{7,5},{8,14},{9,15},{10,... | collective-permute-start | bytes 1572872 | tf_op jit(solution)/shard_map/ppermute | solution.py:36
  40.7 3.5 %collective-permute-start.15 = (bf16[512,512]{1,0:T(8,128)(2,1)S(1)}, bf16[512,512]{1,0:T(8,128)(2,1)S(1)}, u32[]{:S(2)}, u32[]{:S(2)}) collective-permute-start(bf16[512,512]{1,0:T(8,128)(2,1)S(1)} %collective-permute-done.5.w3.refs_12_), channel_id=1, source_target_pairs={{0,6},{1,7},{2,0},{3,1},{4,2},{5,3},{6,4},{7,5},{8,14},{9,15},{10,... | collective-permute-start | bytes 1572872 | tf_op jit(solution)/shard_map/ppermute | solution.py:36
  44.2 3.3 %collective-permute-done.10 = bf16[256,512]{1,0:T(8,128)(2,1)S(1)} collective-permute-done((bf16[256,512]{1,0:T(8,128)(2,1)S(1)}, bf16[256,512]{1,0:T(8,128)(2,1)S(1)}, u32[]{:S(2)}, u32[]{:S(2)}) %collective-permute-start.10) | collective-permute-done | bytes 262176 | tf_op jit(solution)/shard_map/ppermute | solution.py:54
  49.9 12.0 %collective-permute-done.11 = bf16[256,512]{1,0:T(8,128)(2,1)S(1)} collective-permute-done((bf16[256,512]{1,0:T(8,128)(2,1)S(1)}, bf16[256,512]{1,0:T(8,128)(2,1)S(1)}, u32[]{:S(2)}, u32[]{:S(2)}) %collective-permute-start.11) | collective-permute-done | bytes 262176 | tf_op jit(solution)/shard_map/ppermute | solution.py:54
  62.0 1.4 %collective-permute-start.14 = (bf16[512,512]{1,0:T(8,128)(2,1)S(1)}, bf16[512,512]{1,0:T(8,128)(2,1)S(1)}, u32[]{:S(2)}, u32[]{:S(2)}) collective-permute-start(bf16[512,512]{1,0:T(8,128)(2,1)S(1)} %collective-permute-done.9.w1.refs_10_), channel_id=1, source_target_pairs={{0,2},{1,3},{2,4},{3,5},{4,6},{5,7},{6,0},{7,1},{8,10},{9,11},{10,... | collective-permute-start | bytes 1572872 | tf_op jit(solution)/shard_map/ppermute | solution.py:32
  63.4 1.6 %collective-permute-start.19 = (bf16[256,512]{1,0:T(8,128)(2,1)S(1)}, bf16[256,512]{1,0:T(8,128)(2,1)S(1)}, u32[]{:S(2)}, u32[]{:S(2)}) collective-permute-start(bf16[256,512]{1,0:T(8,128)(2,1)S(1)} %add.22.a), channel_id=1, source_target_pairs={{0,64},{16,80},{32,96},{48,112},{64,0},{80,16},{96,32},{112,48},{1... | collective-permute-start | bytes 786440 | tf_op jit(solution)/shard_map/ppermute | solution.py:48
  64.9 2.6 %collective-permute-start.17 = (bf16[512,512]{1,0:T(8,128)(2,1)S(1)}, bf16[512,512]{1,0:T(8,128)(2,1)S(1)}, u32[]{:S(2)}, u32[]{:S(2)}) collective-permute-start(bf16[512,512]{1,0:T(8,128)(2,1)S(1)} %shard_map.132), channel_id=1, source_target_pairs={{0,8},{1,9},{2,10},{3,11},{4,12},{5,13},{6,14},{7,15},{8,0},{9,1},... | collective-permute-start | bytes 1572872 | tf_op jit(solution)/shard_map/ppermute | solution.py:40
  67.6 2.4 %collective-permute-start.18 = (bf16[512,512]{1,0:T(8,128)(2,1)S(1)}, bf16[512,512]{1,0:T(8,128)(2,1)S(1)}, u32[]{:S(2)}, u32[]{:S(2)}) collective-permute-start(bf16[512,512]{1,0:T(8,128)(2,1)S(1)} %get-tuple-element.123), channel_id=1, source_target_pairs={{0,6},{1,7},{2,0},{3,1},{4,2},{5,3},{6,4},{7,5},{8,14},{9,15},{10,... | collective-permute-start | bytes 1572872 | tf_op jit(solution)/shard_map/ppermute | solution.py:36
  70.0 4.2 %collective-permute-done.14.w0.refs_9_ = bf16[512,512]{1,0:T(8,128)(2,1)S(1)} collective-permute-done((bf16[512,512]{1,0:T(8,128)(2,1)S(1)}, bf16[512,512]{1,0:T(8,128)(2,1)S(1)}, u32[]{:S(2)}, u32[]{:S(2)}) %collective-permute-start.14) | collective-permute-done | bytes 524320 | tf_op jit(solution)/shard_map/ppermute | solution.py:32
  74.2 1.5 %shard_map.133 = (f32[256,640]{1,0:T(8,128)S(1)}, bf16[256,640]{1,0:T(8,128)(2,1)S(1)}) custom-call(bf16[256,4096]{1,0:T(8,128)(2,1)S(1)} %copy-done.7, bf16[256,4096]{1,0:T(8,128)(2,1)S(1)} %collective-permute-done.oth.refs_0_, f32[1,8192]{1,0:T(1,128)S(1)} %copy-done.5, f32[256,128]{1,0:T(8,128)S(1)} %copy-done.8, ...), custom_call_target="tpu_custom_call" | custom-call | flops 24999999488 | tf_op jit(solution)/shard_map/pallas_call | solution.py:74
  75.6 2.3 %collective-permute-start.16 = (bf16[256,640]{1,0:T(8,128)(2,1)S(1)}, bf16[256,640]{1,0:T(8,128)(2,1)S(1)}, u32[]{:S(2)}, u32[]{:S(2)}) collective-permute-start(bf16[256,640]{1,0:T(8,128)(2,1)S(1)} %get-tuple-element.120), channel_id=1, source_target_pairs={{0,1},{1,0},{2,3},{3,2},{4,5},{5,4},{6,7},{7,6},{8,9},{9,8},{10,11... | collective-permute-start | bytes 983048 | tf_op jit(solution)/shard_map/ppermute | solution.py:44
  78.0 1.3 %collective-permute-start.21 = (bf16[512,512]{1,0:T(8,128)(2,1)S(1)}, bf16[512,512]{1,0:T(8,128)(2,1)S(1)}, u32[]{:S(2)}, u32[]{:S(2)}) collective-permute-start(bf16[512,512]{1,0:T(8,128)(2,1)S(1)} %get-tuple-element.138), channel_id=1, source_target_pairs={{0,2},{1,3},{2,4},{3,5},{4,6},{5,7},{6,0},{7,1},{8,10},{9,11},{10,... | collective-permute-start | bytes 1572872 | tf_op jit(solution)/shard_map/ppermute | solution.py:32
  79.3 1.5 %shard_map.134 = (f32[512,512]{1,0:T(8,128)}, f32[512,512]{1,0:T(8,128)}) custom-call(bf16[256,512]{1,0:T(8,128)(2,1)S(1)} %add.22.a, bf16[256,512]{1,0:T(8,128)(2,1)S(1)} %collective-permute-done.19.b, f32[512,512]{1,0:T(8,128)S(1)} %copy-done.1, f32[512,512]{1,0:T(8,128)S(1)} %copy-done.2), custom_call_target="tpu_custom_call" | custom-call | flops 20000000000 | tf_op jit(solution)/shard_map/pallas_call | solution.py:74
  81.0 1.3 %collective-permute-start.22 = (bf16[512,512]{1,0:T(8,128)(2,1)S(1)}, bf16[512,512]{1,0:T(8,128)(2,1)S(1)}, u32[]{:S(2)}, u32[]{:S(2)}) collective-permute-start(bf16[512,512]{1,0:T(8,128)(2,1)S(1)} %add.23), channel_id=1, source_target_pairs={{0,6},{1,7},{2,0},{3,1},{4,2},{5,3},{6,4},{7,5},{8,14},{9,15},{10,... | collective-permute-start | bytes 1572872 | tf_op jit(solution)/shard_map/ppermute | solution.py:36
  82.3 10.2 %collective-permute-done.17.fr = bf16[512,512]{1,0:T(8,128)(2,1)S(1)} collective-permute-done((bf16[512,512]{1,0:T(8,128)(2,1)S(1)}, bf16[512,512]{1,0:T(8,128)(2,1)S(1)}, u32[]{:S(2)}, u32[]{:S(2)}) %collective-permute-start.17) | collective-permute-done | bytes 524320 | tf_op jit(solution)/shard_map/ppermute | solution.py:40
  92.5 2.2 %shard_map.135 = (bf16[256,4096]{1,0:T(8,128)(2,1)S(1)}, bf16[256,512]{1,0:T(8,128)(2,1)}, f32[256,128]{1,0:T(8,128)S(1)}) custom-call(bf16[256,4096]{1,0:T(8,128)(2,1)S(1)} %collective-permute-done.oth.refs_0_, f32[1,8192]{1,0:T(1,128)S(1)} %copy-done.5, bf16[256,640]{1,0:T(8,128)(2,1)S(1)} %collective-permute-done.1.ext.refs_2_, ...), custom_call_target="tpu_custom_call" | custom-call | flops 54999998464 | tf_op jit(solution)/shard_map/pallas_call | solution.py:74
  94.7 2.0 %collective-permute-start.20 = (bf16[256,4096]{1,0:T(8,128)(2,1)S(1)}, bf16[256,4096]{1,0:T(8,128)(2,1)S(1)}, u32[]{:S(2)}, u32[]{:S(2)}) collective-permute-start(bf16[256,4096]{1,0:T(8,128)(2,1)S(1)} %get-tuple-element.132), channel_id=1, source_target_pairs={{0,1},{1,0},{2,3},{3,2},{4,5},{5,4},{6,7},{7,6},{8,9},{9,8},{10,11... | collective-permute-start | bytes 6291464 | tf_op jit(solution)/shard_map/ppermute | solution.py:44
  96.7 2.1 %shard_map.136._ = bf16[256,8192]{1,0:T(8,128)(2,1)} custom-call(bf16[256,4096]{1,0:T(8,128)(2,1)S(1)} %copy-done.7, f32[1,8192]{1,0:T(1,128)S(1)} %copy-done.5, f32[256,128]{1,0:T(8,128)S(1)} %copy-done.8, bf16[256,512]{1,0:T(8,128)(2,1)S(1)} %copy-done.4, f32[256,128]{1,0:T(8,128)S(1)} %get-tuple-element.135.refs_4_, ...), custom_call_target="tpu_custom_call" | custom-call | flops 46999998464 | tf_op jit(solution)/shard_map/pallas_call | solution.py:74
  98.8 1.7 %collective-permute-done.20.arr = bf16[256,4096]{1,0:T(8,128)(2,1)S(1)} collective-permute-done((bf16[256,4096]{1,0:T(8,128)(2,1)S(1)}, bf16[256,4096]{1,0:T(8,128)(2,1)S(1)}, u32[]{:S(2)}, u32[]{:S(2)}) %collective-permute-start.20) | collective-permute-done | bytes 2097184 | tf_op jit(solution)/shard_map/ppermute | solution.py:44
  100.5 1.4 %shard_map.137 = bf16[256,8192]{1,0:T(8,128)(2,1)} custom-call(bf16[256,8192]{1,0:T(8,128)(2,1)} %shard_map.136._, bf16[256,4096]{1,0:T(8,128)(2,1)S(1)} %collective-permute-done.20.arr), custom_call_target="tpu_custom_call", output_to_operand_aliasing={{}: (0, {})} | custom-call | flops 14000000000 | tf_op jit(solution)/shard_map/pallas_call | solution.py:74
  101.9 1.6 %shard_map.138 = (bf16[512,512]{1,0:T(8,128)(2,1)}, bf16[1,512]{1,0:T(2,128)(2,1)}) custom-call(bf16[512,512]{1,0:T(8,128)(2,1)S(1)} %get-tuple-element.97.o, bf16[512,512]{1,0:T(8,128)(2,1)S(1)} %collective-permute-done.21.a, bf16[512,512]{1,0:T(8,128)(2,1)S(1)} %collective-permute-done.22.b, bf16[512,512]{1,0:T(8,128)(2,1)S(1)} %collective-permute-done.17.fr, ...), custom_call_target="tpu_custom_call" | custom-call | flops 28999999488 | tf_op jit(solution)/shard_map/pallas_call | solution.py:74
  (50 shorter events, 7.7 us)
Async XLA Ops:
  0.6 6.3 %copy-start.3 = (bf16[1,512,512]{2,1,0:T(8,128)(2,1)S(1)}, bf16[1,512,512]{2,1,0:T(8,128)(2,1)}, u32[]{:S(2)}) copy-start(bf16[1,512,512]{2,1,0:T(8,128)(2,1)} %param.10) | copy-start | bytes 1572868
  0.6 8.6 %copy-start.6 = (s32[1,512,4]{1,2,0:T(4,128)S(1)}, s32[1,512,4]{1,2,0:T(4,128)}, u32[]{:S(2)}) copy-start(s32[1,512,4]{1,2,0:T(4,128)} %param.13) | copy-start | bytes 24580
  0.7 8.6 %copy-start = (s32[1,512,512]{2,1,0:T(8,128)S(1)}, s32[1,512,512]{2,1,0:T(8,128)}, u32[]{:S(2)}) copy-start(s32[1,512,512]{2,1,0:T(8,128)} %param.12) | copy-start | bytes 3145732
  6.2 12.1 %collective-permute-start = (bf16[256,4096]{1,0:T(8,128)(2,1)}, bf16[256,4096]{1,0:T(8,128)(2,1)S(1)}, u32[]{:S(2)}, u32[]{:S(2)}) collective-permute-start(bf16[256,4096]{1,0:T(8,128)(2,1)} %get-tuple-element.75), channel_id=1, source_target_pairs={{0,1},{1,0},{2,3},{3,2},{4,5},{5,4},{6,7},{7,6},{8,9},{9,8},{10,11... | collective-permute-start | bytes 6291464 | tf_op jit(solution)/shard_map/ppermute | solution.py:44
  6.9 13.5 %collective-permute-start.4 = (bf16[512,512]{1,0:T(8,128)(2,1)S(1)}, bf16[512,512]{1,0:T(8,128)(2,1)S(1)}, u32[]{:S(2)}, u32[]{:S(2)}) collective-permute-start(bf16[512,512]{1,0:T(8,128)(2,1)S(1)} %bitcast.6), channel_id=1, source_target_pairs={{0,6},{1,7},{2,0},{3,1},{4,2},{5,3},{6,4},{7,5},{8,14},{9,15},{10,... | collective-permute-start | bytes 1572872 | tf_op jit(solution)/shard_map/ppermute | solution.py:36
  8.9 13.1 %collective-permute-start.3 = (bf16[512,512]{1,0:T(8,128)(2,1)S(1)}, bf16[512,512]{1,0:T(8,128)(2,1)S(1)}, u32[]{:S(2)}, u32[]{:S(2)}) collective-permute-start(bf16[512,512]{1,0:T(8,128)(2,1)S(1)} %bitcast.7), channel_id=1, source_target_pairs={{0,2},{1,3},{2,4},{3,5},{4,6},{5,7},{6,0},{7,1},{8,10},{9,11},{10,... | collective-permute-start | bytes 1572872 | tf_op jit(solution)/shard_map/ppermute | solution.py:32
  8.9 2.5 %collective-permute-start.1 = (bf16[256,640]{1,0:T(8,128)(2,1)}, bf16[256,640]{1,0:T(8,128)(2,1)S(1)}, u32[]{:S(2)}, u32[]{:S(2)}) collective-permute-start(bf16[256,640]{1,0:T(8,128)(2,1)} %get-tuple-element.76), channel_id=1, source_target_pairs={{0,1},{1,0},{2,3},{3,2},{4,5},{5,4},{6,7},{7,6},{8,9},{9,8},{10,11... | collective-permute-start | bytes 983048 | tf_op jit(solution)/shard_map/ppermute | solution.py:44
  9.2 9.1 %copy-start.4 = (bf16[256,512]{1,0:T(8,128)(2,1)S(1)}, bf16[256,512]{1,0:T(8,128)(2,1)}, u32[]{:S(2)}) copy-start(bf16[256,512]{1,0:T(8,128)(2,1)} %refs_3_.1) | copy-start | bytes 786436
  9.2 9.1 %copy-start.5 = (f32[1,8192]{1,0:T(1,128)S(1)}, f32[1,8192]{1,0:T(1,128)}, u32[]{:S(2)}) copy-start(f32[1,8192]{1,0:T(1,128)} %gain.7) | copy-start | bytes 98308
  9.2 9.1 %copy-start.7 = (bf16[256,4096]{1,0:T(8,128)(2,1)S(1)}, bf16[256,4096]{1,0:T(8,128)(2,1)}, u32[]{:S(2)}) copy-start(bf16[256,4096]{1,0:T(8,128)(2,1)} %get-tuple-element.84.own.own_x.refs_0_) | copy-start | bytes 6291460
  9.3 9.1 %copy-start.8 = (f32[256,128]{1,0:T(8,128)S(1)}, f32[256,128]{1,0:T(8,128)}, u32[]{:S(2)}) copy-start(f32[256,128]{1,0:T(8,128)} %get-tuple-element.77.irr.refs_2_) | copy-start | bytes 393220
  9.9 12.1 %collective-permute-start.2 = (bf16[256,512]{1,0:T(8,128)(2,1)S(1)}, bf16[256,512]{1,0:T(8,128)(2,1)S(1)}, u32[]{:S(2)}, u32[]{:S(2)}) collective-permute-start(bf16[256,512]{1,0:T(8,128)(2,1)S(1)} %get-tuple-element.83), channel_id=1, source_target_pairs={{0,64},{16,80},{32,96},{48,112},{64,0},{80,16},{96,32},{112,48},{1... | collective-permute-start | bytes 786440 | tf_op jit(solution)/shard_map/ppermute | solution.py:48
  11.4 29.3 %collective-permute-start.5 = (bf16[512,512]{1,0:T(8,128)(2,1)S(1)}, bf16[512,512]{1,0:T(8,128)(2,1)S(1)}, u32[]{:S(2)}, u32[]{:S(2)}) collective-permute-start(bf16[512,512]{1,0:T(8,128)(2,1)S(1)} %bitcast.8), channel_id=1, source_target_pairs={{0,8},{1,9},{2,10},{3,11},{4,12},{5,13},{6,14},{7,15},{8,0},{9,1},... | collective-permute-start | bytes 1572872 | tf_op jit(solution)/shard_map/ppermute | solution.py:40
  22.1 8.2 %collective-permute-start.8 = (bf16[256,512]{1,0:T(8,128)(2,1)S(1)}, bf16[256,512]{1,0:T(8,128)(2,1)S(1)}, u32[]{:S(2)}, u32[]{:S(2)}) collective-permute-start(bf16[256,512]{1,0:T(8,128)(2,1)S(1)} %add.18), channel_id=1, source_target_pairs={{0,128},{16,144},{32,160},{48,176},{64,192},{80,208},{96,224},{112... | collective-permute-start | bytes 786440 | tf_op jit(solution)/shard_map/ppermute | solution.py:48
  24.8 14.7 %collective-permute-start.6 = (bf16[512,512]{1,0:T(8,128)(2,1)S(1)}, bf16[512,512]{1,0:T(8,128)(2,1)S(1)}, u32[]{:S(2)}, u32[]{:S(2)}) collective-permute-start(bf16[512,512]{1,0:T(8,128)(2,1)S(1)} %collective-permute-done.3.w1.refs_6_), channel_id=1, source_target_pairs={{0,2},{1,3},{2,4},{3,5},{4,6},{5,7},{6,0},{7,1},{8,10},{9,11},{10,... | collective-permute-start | bytes 1572872 | tf_op jit(solution)/shard_map/ppermute | solution.py:32
  24.8 12.9 %collective-permute-start.7 = (bf16[512,512]{1,0:T(8,128)(2,1)S(1)}, bf16[512,512]{1,0:T(8,128)(2,1)S(1)}, u32[]{:S(2)}, u32[]{:S(2)}) collective-permute-start(bf16[512,512]{1,0:T(8,128)(2,1)S(1)} %get-tuple-element.96), channel_id=1, source_target_pairs={{0,6},{1,7},{2,0},{3,1},{4,2},{5,3},{6,4},{7,5},{8,14},{9,15},{10,... | collective-permute-start | bytes 1572872 | tf_op jit(solution)/shard_map/ppermute | solution.py:36
  27.1 22.0 %collective-permute-start.12 = (bf16[512,512]{1,0:T(8,128)(2,1)S(1)}, bf16[512,512]{1,0:T(8,128)(2,1)S(1)}, u32[]{:S(2)}, u32[]{:S(2)}) collective-permute-start(bf16[512,512]{1,0:T(8,128)(2,1)S(1)} %get-tuple-element.110), channel_id=1, source_target_pairs={{0,2},{1,3},{2,4},{3,5},{4,6},{5,7},{6,0},{7,1},{8,10},{9,11},{10,... | collective-permute-start | bytes 1572872 | tf_op jit(solution)/shard_map/ppermute | solution.py:32
  30.4 17.2 %collective-permute-start.10 = (bf16[256,512]{1,0:T(8,128)(2,1)S(1)}, bf16[256,512]{1,0:T(8,128)(2,1)S(1)}, u32[]{:S(2)}, u32[]{:S(2)}) collective-permute-start(bf16[256,512]{1,0:T(8,128)(2,1)S(1)} %add.19), channel_id=1, source_target_pairs={{0,16},{16,0},{32,48},{48,32},{64,80},{80,64},{96,112},{112,96},{1... | collective-permute-start | bytes 786440 | tf_op jit(solution)/shard_map/ppermute | solution.py:54
  37.8 12.0 %collective-permute-start.13 = (bf16[512,512]{1,0:T(8,128)(2,1)S(1)}, bf16[512,512]{1,0:T(8,128)(2,1)S(1)}, u32[]{:S(2)}, u32[]{:S(2)}) collective-permute-start(bf16[512,512]{1,0:T(8,128)(2,1)S(1)} %add.20), channel_id=1, source_target_pairs={{0,6},{1,7},{2,0},{3,1},{4,2},{5,3},{6,4},{7,5},{8,14},{9,15},{10,... | collective-permute-start | bytes 1572872 | tf_op jit(solution)/shard_map/ppermute | solution.py:36
  40.7 26.8 %collective-permute-start.15 = (bf16[512,512]{1,0:T(8,128)(2,1)S(1)}, bf16[512,512]{1,0:T(8,128)(2,1)S(1)}, u32[]{:S(2)}, u32[]{:S(2)}) collective-permute-start(bf16[512,512]{1,0:T(8,128)(2,1)S(1)} %collective-permute-done.5.w3.refs_12_), channel_id=1, source_target_pairs={{0,6},{1,7},{2,0},{3,1},{4,2},{5,3},{6,4},{7,5},{8,14},{9,15},{10,... | collective-permute-start | bytes 1572872 | tf_op jit(solution)/shard_map/ppermute | solution.py:36
  44.2 17.7 %collective-permute-start.9 = (bf16[512,512]{1,0:T(8,128)(2,1)S(1)}, bf16[512,512]{1,0:T(8,128)(2,1)S(1)}, u32[]{:S(2)}, u32[]{:S(2)}) collective-permute-start(bf16[512,512]{1,0:T(8,128)(2,1)S(1)} %collective-permute-done.5.w3.refs_12_), channel_id=1, source_target_pairs={{0,2},{1,3},{2,4},{3,5},{4,6},{5,7},{6,0},{7,1},{8,10},{9,11},{10,... | collective-permute-start | bytes 1572872 | tf_op jit(solution)/shard_map/ppermute | solution.py:32
  47.7 14.3 %collective-permute-start.11 = (bf16[256,512]{1,0:T(8,128)(2,1)S(1)}, bf16[256,512]{1,0:T(8,128)(2,1)S(1)}, u32[]{:S(2)}, u32[]{:S(2)}) collective-permute-start(bf16[256,512]{1,0:T(8,128)(2,1)S(1)} %add.21), channel_id=1, source_target_pairs={{0,32},{16,48},{32,0},{48,16},{64,96},{80,112},{96,64},{112,80},{1... | collective-permute-start | bytes 786440 | tf_op jit(solution)/shard_map/ppermute | solution.py:54
  62.0 12.2 %collective-permute-start.14 = (bf16[512,512]{1,0:T(8,128)(2,1)S(1)}, bf16[512,512]{1,0:T(8,128)(2,1)S(1)}, u32[]{:S(2)}, u32[]{:S(2)}) collective-permute-start(bf16[512,512]{1,0:T(8,128)(2,1)S(1)} %collective-permute-done.9.w1.refs_10_), channel_id=1, source_target_pairs={{0,2},{1,3},{2,4},{3,5},{4,6},{5,7},{6,0},{7,1},{8,10},{9,11},{10,... | collective-permute-start | bytes 1572872 | tf_op jit(solution)/shard_map/ppermute | solution.py:32
  63.4 14.6 %collective-permute-start.19 = (bf16[256,512]{1,0:T(8,128)(2,1)S(1)}, bf16[256,512]{1,0:T(8,128)(2,1)S(1)}, u32[]{:S(2)}, u32[]{:S(2)}) collective-permute-start(bf16[256,512]{1,0:T(8,128)(2,1)S(1)} %add.22.a), channel_id=1, source_target_pairs={{0,64},{16,80},{32,96},{48,112},{64,0},{80,16},{96,32},{112,48},{1... | collective-permute-start | bytes 786440 | tf_op jit(solution)/shard_map/ppermute | solution.py:48
  64.9 27.6 %collective-permute-start.17 = (bf16[512,512]{1,0:T(8,128)(2,1)S(1)}, bf16[512,512]{1,0:T(8,128)(2,1)S(1)}, u32[]{:S(2)}, u32[]{:S(2)}) collective-permute-start(bf16[512,512]{1,0:T(8,128)(2,1)S(1)} %shard_map.132), channel_id=1, source_target_pairs={{0,8},{1,9},{2,10},{3,11},{4,12},{5,13},{6,14},{7,15},{8,0},{9,1},... | collective-permute-start | bytes 1572872 | tf_op jit(solution)/shard_map/ppermute | solution.py:40
  67.6 13.2 %collective-permute-start.18 = (bf16[512,512]{1,0:T(8,128)(2,1)S(1)}, bf16[512,512]{1,0:T(8,128)(2,1)S(1)}, u32[]{:S(2)}, u32[]{:S(2)}) collective-permute-start(bf16[512,512]{1,0:T(8,128)(2,1)S(1)} %get-tuple-element.123), channel_id=1, source_target_pairs={{0,6},{1,7},{2,0},{3,1},{4,2},{5,3},{6,4},{7,5},{8,14},{9,15},{10,... | collective-permute-start | bytes 1572872 | tf_op jit(solution)/shard_map/ppermute | solution.py:36
  74.1 5.2 %copy-start.1 = (f32[512,512]{1,0:T(8,128)S(1)}, f32[512,512]{1,0:T(8,128)}, u32[]{:S(2)}) copy-start(f32[512,512]{1,0:T(8,128)} %m.1) | copy-start | bytes 3145732
  74.2 5.2 %copy-start.2 = (f32[512,512]{1,0:T(8,128)S(1)}, f32[512,512]{1,0:T(8,128)}, u32[]{:S(2)}) copy-start(f32[512,512]{1,0:T(8,128)} %p.1) | copy-start | bytes 3145732
  75.6 16.9 %collective-permute-start.16 = (bf16[256,640]{1,0:T(8,128)(2,1)S(1)}, bf16[256,640]{1,0:T(8,128)(2,1)S(1)}, u32[]{:S(2)}, u32[]{:S(2)}) collective-permute-start(bf16[256,640]{1,0:T(8,128)(2,1)S(1)} %get-tuple-element.120), channel_id=1, source_target_pairs={{0,1},{1,0},{2,3},{3,2},{4,5},{5,4},{6,7},{7,6},{8,9},{9,8},{10,11... | collective-permute-start | bytes 983048 | tf_op jit(solution)/shard_map/ppermute | solution.py:44
  78.0 23.9 %collective-permute-start.21 = (bf16[512,512]{1,0:T(8,128)(2,1)S(1)}, bf16[512,512]{1,0:T(8,128)(2,1)S(1)}, u32[]{:S(2)}, u32[]{:S(2)}) collective-permute-start(bf16[512,512]{1,0:T(8,128)(2,1)S(1)} %get-tuple-element.138), channel_id=1, source_target_pairs={{0,2},{1,3},{2,4},{3,5},{4,6},{5,7},{6,0},{7,1},{8,10},{9,11},{10,... | collective-permute-start | bytes 1572872 | tf_op jit(solution)/shard_map/ppermute | solution.py:32
  81.0 20.9 %collective-permute-start.22 = (bf16[512,512]{1,0:T(8,128)(2,1)S(1)}, bf16[512,512]{1,0:T(8,128)(2,1)S(1)}, u32[]{:S(2)}, u32[]{:S(2)}) collective-permute-start(bf16[512,512]{1,0:T(8,128)(2,1)S(1)} %add.23), channel_id=1, source_target_pairs={{0,6},{1,7},{2,0},{3,1},{4,2},{5,3},{6,4},{7,5},{8,14},{9,15},{10,... | collective-permute-start | bytes 1572872 | tf_op jit(solution)/shard_map/ppermute | solution.py:36
  94.7 5.8 %collective-permute-start.20 = (bf16[256,4096]{1,0:T(8,128)(2,1)S(1)}, bf16[256,4096]{1,0:T(8,128)(2,1)S(1)}, u32[]{:S(2)}, u32[]{:S(2)}) collective-permute-start(bf16[256,4096]{1,0:T(8,128)(2,1)S(1)} %get-tuple-element.132), channel_id=1, source_target_pairs={{0,1},{1,0},{2,3},{3,2},{4,5},{5,4},{6,7},{7,6},{8,9},{9,8},{10,11... | collective-permute-start | bytes 6291464 | tf_op jit(solution)/shard_map/ppermute | solution.py:44

commit v5 on v4

--- a/solution.py
+++ b/solution.py
@@ -433,7 +433,7 @@
         kernel,
         (jax.ShapeDtypeStruct((h, cols), BF16),) * 2,
         (quantized, exponents),
-        cost=1.0,
+        cost=2.5,
         scratch_shapes=[pltpu.VMEM((n, nb), F32)],
     )
 

time: 104 us -> 102 us (0.981)
  the two profiles are of different devices: /device:TPU:9 before, /device:TPU:1 now
where the time goes in v5:
time: 102 us
  waiting for transfers between devices  43.8 us (43%)
  starting transfers between devices  35.5 us (35%)
  Pallas kernels  21.5 us (21%)
    pallas_call x12, Pallas kernels, call(): pl.pallas_call(kernel, out_shape=outs, compiler_params=pltpu.CompilerPara...  21.5 us
    ppermute x2, waiting for transfers between devices, swap_z(): lax.ppermute(v, 'replica', [(x * N_ZL + z, x * N_ZL + (z ^ bit)) for x in...  18.4 us
    ppermute x6, starting transfers between devices, to_down(): return lax.ppermute(v, 'dp', dp_moves(dy=-1))  15.2 us
    ppermute x6, waiting for transfers between devices, to_up(): return lax.ppermute(v, 'dp', dp_moves(dy=1))  10.2 us
    ppermute x2, starting transfers between devices, to_far(): return lax.ppermute(v, 'dp', dp_moves(dz=1))  7.38 us
    ppermute x2, waiting for transfers between devices, to_far(): return lax.ppermute(v, 'dp', dp_moves(dz=1))  6.44 us
    ppermute x6, waiting for transfers between devices, to_down(): return lax.ppermute(v, 'dp', dp_moves(dy=-1))  5.99 us
    ppermute x4, starting transfers between devices, to_core(): return lax.ppermute(v, 'dp', dp_moves(dc=1))  4.63 us
  transfers between devices with their start and end apart: 23, of which 8 were waited for; matrix products, arithmetic and copies ran while one was open for 1% of the time, Pallas kernels for 19%

profile of v5, /device:TPU:1, one launch (start us, length us, event | category | flops | bytes accessed | tf_op | source)
XLA Modules:
  0.0 102.3 jit_solution(5606441301364820264)
XLA Ops:
  0.7 3.6 %collective-permute-start.4 = (bf16[512,512]{1,0:T(8,128)(2,1)}, bf16[512,512]{1,0:T(8,128)(2,1)S(1)}, u32[]{:S(2)}, u32[]{:S(2)}) collective-permute-start(bf16[512,512]{1,0:T(8,128)(2,1)} %bitcast.6), channel_id=1, source_target_pairs={{0,6},{1,7},{2,0},{3,1},{4,2},{5,3},{6,4},{7,5},{8,14},{9,15},{10,... | collective-permute-start | bytes 1572872 | tf_op jit(solution)/shard_map/ppermute | solution.py:36
  4.3 5.4 %shard_map.127 = (bf16[256,4096]{1,0:T(8,128)(2,1)}, bf16[256,4096]{1,0:T(8,128)(2,1)}, bf16[256,640]{1,0:T(8,128)(2,1)}, f32[256,128]{1,0:T(8,128)}) custom-call(bf16[256,8192]{1,0:T(8,128)(2,1)} %tok.1, bf16[256,512]{1,0:T(8,128)(2,1)} %refs_3_.1), custom_call_target="tpu_custom_call" | custom-call | flops 32000000000 | tf_op jit(solution)/shard_map/pallas_call | solution.py:74
  9.7 1.8 %collective-permute-start.1 = (bf16[256,640]{1,0:T(8,128)(2,1)}, bf16[256,640]{1,0:T(8,128)(2,1)S(1)}, u32[]{:S(2)}, u32[]{:S(2)}) collective-permute-start(bf16[256,640]{1,0:T(8,128)(2,1)} %get-tuple-element.76), channel_id=1, source_target_pairs={{0,1},{1,0},{2,3},{3,2},{4,5},{5,4},{6,7},{7,6},{8,9},{9,8},{10,11... | collective-permute-start | bytes 983048 | tf_op jit(solution)/shard_map/ppermute | solution.py:44
  11.6 0.6 shard_map.128
  13.0 6.8 %collective-permute-start.5 = (bf16[512,512]{1,0:T(8,128)(2,1)S(1)}, bf16[512,512]{1,0:T(8,128)(2,1)S(1)}, u32[]{:S(2)}, u32[]{:S(2)}) collective-permute-start(bf16[512,512]{1,0:T(8,128)(2,1)S(1)} %bitcast.8), channel_id=1, source_target_pairs={{0,8},{1,9},{2,10},{3,11},{4,12},{5,13},{6,14},{7,15},{8,0},{9,1},... | collective-permute-start | bytes 1572872 | tf_op jit(solution)/shard_map/ppermute | solution.py:40
  19.8 1.8 %shard_map.129 = (bf16[512,512]{1,0:T(8,128)(2,1)S(1)}, bf16[512,512]{1,0:T(8,128)(2,1)S(1)}, bf16[512,512]{1,0:T(8,128)(2,1)S(1)}, bf16[512,512]{1,0:T(8,128)(2,1)S(1)}) custom-call(bf16[256,4096]{1,0:T(8,128)(2,1)S(1)} %copy-done.7, bf16[256,4096]{1,0:T(8,128)(2,1)S(1)} %collective-permute-done.oth.refs_0_, f32[1,8192]{1,0:T(1,128)S(1)} %copy-done.5, ...), custom_call_target="tpu_custom_call" | custom-call | flops 33999998976 | tf_op jit(solution)/shard_map/pallas_call | solution.py:74
  21.7 2.5 %collective-permute-start.8 = (bf16[256,512]{1,0:T(8,128)(2,1)S(1)}, bf16[256,512]{1,0:T(8,128)(2,1)S(1)}, u32[]{:S(2)}, u32[]{:S(2)}) collective-permute-start(bf16[256,512]{1,0:T(8,128)(2,1)S(1)} %add.18), channel_id=1, source_target_pairs={{0,128},{16,144},{32,160},{48,176},{64,192},{80,208},{96,224},{112... | collective-permute-start | bytes 786440 | tf_op jit(solution)/shard_map/ppermute | solution.py:48
  24.5 2.7 %collective-permute-start.7 = (bf16[512,512]{1,0:T(8,128)(2,1)S(1)}, bf16[512,512]{1,0:T(8,128)(2,1)S(1)}, u32[]{:S(2)}, u32[]{:S(2)}) collective-permute-start(bf16[512,512]{1,0:T(8,128)(2,1)S(1)} %get-tuple-element.96), channel_id=1, source_target_pairs={{0,6},{1,7},{2,0},{3,1},{4,2},{5,3},{6,4},{7,5},{8,14},{9,15},{10,... | collective-permute-start | bytes 1572872 | tf_op jit(solution)/shard_map/ppermute | solution.py:36
  27.2 1.9 %shard_map.130 = (bf16[512,512]{1,0:T(8,128)(2,1)S(1)}, bf16[512,512]{1,0:T(8,128)(2,1)S(1)}, bf16[512,512]{1,0:T(8,128)(2,1)S(1)}, bf16[512,512]{1,0:T(8,128)(2,1)S(1)}, bf16[512,2048]{1,0:T(8,128)(2,1)S(1)}) custom-call(bf16[256,4096]{1,0:T(8,128)(2,1)S(1)} %copy-done.7, bf16[256,4096]{1,0:T(8,128)(2,1)S(1)} %collective-permute-done.oth.refs_0_, ...), custom_call_target="tpu_custom_call" | custom-call | flops 33999998976 | tf_op jit(solution)/shard_map/pallas_call | solution.py:74
  29.1 1.0 %collective-permute-done.8 = bf16[256,512]{1,0:T(8,128)(2,1)S(1)} collective-permute-done((bf16[256,512]{1,0:T(8,128)(2,1)S(1)}, bf16[256,512]{1,0:T(8,128)(2,1)S(1)}, u32[]{:S(2)}, u32[]{:S(2)}) %collective-permute-start.8) | collective-permute-done | bytes 262176 | tf_op jit(solution)/shard_map/ppermute | solution.py:48
  30.2 1.0 collective-permute-start.10
  31.2 6.0 %collective-permute-done.7 = bf16[512,512]{1,0:T(8,128)(2,1)S(1)} collective-permute-done((bf16[512,512]{1,0:T(8,128)(2,1)S(1)}, bf16[512,512]{1,0:T(8,128)(2,1)S(1)}, u32[]{:S(2)}, u32[]{:S(2)}) %collective-permute-start.7) | collective-permute-done | bytes 524320 | tf_op jit(solution)/shard_map/ppermute | solution.py:36
  37.3 3.5 %collective-permute-start.13 = (bf16[512,512]{1,0:T(8,128)(2,1)S(1)}, bf16[512,512]{1,0:T(8,128)(2,1)S(1)}, u32[]{:S(2)}, u32[]{:S(2)}) collective-permute-start(bf16[512,512]{1,0:T(8,128)(2,1)S(1)} %add.20), channel_id=1, source_target_pairs={{0,6},{1,7},{2,0},{3,1},{4,2},{5,3},{6,4},{7,5},{8,14},{9,15},{10,... | collective-permute-start | bytes 1572872 | tf_op jit(solution)/shard_map/ppermute | solution.py:36
  40.8 1.2 %shard_map.131.first = f32[512,512]{1,0:T(8,128)S(1)} custom-call(bf16[512,2048]{1,0:T(8,128)(2,1)S(1)} %get-tuple-element.102.hid, bf16[512,512]{1,0:T(8,128)(2,1)S(1)} %collective-permute-done.6.w0.refs_5_, bf16[512,512]{1,0:T(8,128)(2,1)S(1)} %collective-permute-done.3.w1.refs_6_, bf16[512,512]{1,0:T(8,128)(2,1)S(1)} %collective-permute-done.4.w2.refs_7_, ...), custom_call_target="tpu_custom_call" | custom-call | flops 24999999488 | tf_op jit(solution)/shard_map/pallas_call | solution.py:74
  42.1 1.4 %collective-permute-start.9 = (bf16[512,512]{1,0:T(8,128)(2,1)S(1)}, bf16[512,512]{1,0:T(8,128)(2,1)S(1)}, u32[]{:S(2)}, u32[]{:S(2)}) collective-permute-start(bf16[512,512]{1,0:T(8,128)(2,1)S(1)} %collective-permute-done.5.w3.refs_12_), channel_id=1, source_target_pairs={{0,2},{1,3},{2,4},{3,5},{4,6},{5,7},{6,0},{7,1},{8,10},{9,11},{10,... | collective-permute-start | bytes 1572872 | tf_op jit(solution)/shard_map/ppermute | solution.py:32
  43.6 5.1 %collective-permute-done.10 = bf16[256,512]{1,0:T(8,128)(2,1)S(1)} collective-permute-done((bf16[256,512]{1,0:T(8,128)(2,1)S(1)}, bf16[256,512]{1,0:T(8,128)(2,1)S(1)}, u32[]{:S(2)}, u32[]{:S(2)}) %collective-permute-start.10) | collective-permute-done | bytes 262176 | tf_op jit(solution)/shard_map/ppermute | solution.py:54
  48.7 1.1 %collective-permute-start.11 = (bf16[256,512]{1,0:T(8,128)(2,1)S(1)}, bf16[256,512]{1,0:T(8,128)(2,1)S(1)}, u32[]{:S(2)}, u32[]{:S(2)}) collective-permute-start(bf16[256,512]{1,0:T(8,128)(2,1)S(1)} %add.21), channel_id=1, source_target_pairs={{0,32},{16,48},{32,0},{48,16},{64,96},{80,112},{96,64},{112,80},{1... | collective-permute-start | bytes 786440 | tf_op jit(solution)/shard_map/ppermute | solution.py:54
  50.0 13.3 %collective-permute-done.11 = bf16[256,512]{1,0:T(8,128)(2,1)S(1)} collective-permute-done((bf16[256,512]{1,0:T(8,128)(2,1)S(1)}, bf16[256,512]{1,0:T(8,128)(2,1)S(1)}, u32[]{:S(2)}, u32[]{:S(2)}) %collective-permute-start.11) | collective-permute-done | bytes 262176 | tf_op jit(solution)/shard_map/ppermute | solution.py:54
  63.8 1.0 collective-permute-start.19
  65.4 2.7 %collective-permute-start.18 = (bf16[512,512]{1,0:T(8,128)(2,1)S(1)}, bf16[512,512]{1,0:T(8,128)(2,1)S(1)}, u32[]{:S(2)}, u32[]{:S(2)}) collective-permute-start(bf16[512,512]{1,0:T(8,128)(2,1)S(1)} %get-tuple-element.123), channel_id=1, source_target_pairs={{0,6},{1,7},{2,0},{3,1},{4,2},{5,3},{6,4},{7,5},{8,14},{9,15},{10,... | collective-permute-start | bytes 1572872 | tf_op jit(solution)/shard_map/ppermute | solution.py:36
  68.0 10.2 %collective-permute-done.14.w0.refs_9_ = bf16[512,512]{1,0:T(8,128)(2,1)S(1)} collective-permute-done((bf16[512,512]{1,0:T(8,128)(2,1)S(1)}, bf16[512,512]{1,0:T(8,128)(2,1)S(1)}, u32[]{:S(2)}, u32[]{:S(2)}) %collective-permute-start.14) | collective-permute-done | bytes 524320 | tf_op jit(solution)/shard_map/ppermute | solution.py:32
  78.2 1.5 %shard_map.133 = (f32[256,640]{1,0:T(8,128)S(1)}, bf16[256,640]{1,0:T(8,128)(2,1)S(1)}) custom-call(bf16[256,4096]{1,0:T(8,128)(2,1)S(1)} %copy-done.7, bf16[256,4096]{1,0:T(8,128)(2,1)S(1)} %collective-permute-done.oth.refs_0_, f32[1,8192]{1,0:T(1,128)S(1)} %copy-done.5, f32[256,128]{1,0:T(8,128)S(1)} %copy-done.8, ...), custom_call_target="tpu_custom_call" | custom-call | flops 24999999488 | tf_op jit(solution)/shard_map/pallas_call | solution.py:74
  79.7 1.1 %collective-permute-start.16 = (bf16[256,640]{1,0:T(8,128)(2,1)S(1)}, bf16[256,640]{1,0:T(8,128)(2,1)S(1)}, u32[]{:S(2)}, u32[]{:S(2)}) collective-permute-start(bf16[256,640]{1,0:T(8,128)(2,1)S(1)} %get-tuple-element.120), channel_id=1, source_target_pairs={{0,1},{1,0},{2,3},{3,2},{4,5},{5,4},{6,7},{7,6},{8,9},{9,8},{10,11... | collective-permute-start | bytes 983048 | tf_op jit(solution)/shard_map/ppermute | solution.py:44
  80.9 1.6 %shard_map.134 = (f32[512,512]{1,0:T(8,128)}, f32[512,512]{1,0:T(8,128)}) custom-call(bf16[256,512]{1,0:T(8,128)(2,1)S(1)} %add.22.a, bf16[256,512]{1,0:T(8,128)(2,1)S(1)} %collective-permute-done.19.b, f32[512,512]{1,0:T(8,128)S(1)} %copy-done.1, f32[512,512]{1,0:T(8,128)S(1)} %copy-done.2), custom_call_target="tpu_custom_call" | custom-call | flops 20000000000 | tf_op jit(solution)/shard_map/pallas_call | solution.py:74
  82.6 2.7 %collective-permute-start.22 = (bf16[512,512]{1,0:T(8,128)(2,1)S(1)}, bf16[512,512]{1,0:T(8,128)(2,1)S(1)}, u32[]{:S(2)}, u32[]{:S(2)}) collective-permute-start(bf16[512,512]{1,0:T(8,128)(2,1)S(1)} %add.23), channel_id=1, source_target_pairs={{0,6},{1,7},{2,0},{3,1},{4,2},{5,3},{6,4},{7,5},{8,14},{9,15},{10,... | collective-permute-start | bytes 1572872 | tf_op jit(solution)/shard_map/ppermute | solution.py:36
  85.3 6.4 %collective-permute-done.17.fr = bf16[512,512]{1,0:T(8,128)(2,1)S(1)} collective-permute-done((bf16[512,512]{1,0:T(8,128)(2,1)S(1)}, bf16[512,512]{1,0:T(8,128)(2,1)S(1)}, u32[]{:S(2)}, u32[]{:S(2)}) %collective-permute-start.17) | collective-permute-done | bytes 524320 | tf_op jit(solution)/shard_map/ppermute | solution.py:40
  91.7 2.2 %shard_map.135 = (bf16[256,4096]{1,0:T(8,128)(2,1)S(1)}, bf16[256,512]{1,0:T(8,128)(2,1)}, f32[256,128]{1,0:T(8,128)S(1)}) custom-call(bf16[256,4096]{1,0:T(8,128)(2,1)S(1)} %collective-permute-done.oth.refs_0_, f32[1,8192]{1,0:T(1,128)S(1)} %copy-done.5, bf16[256,640]{1,0:T(8,128)(2,1)S(1)} %collective-permute-done.1.ext.refs_2_, ...), custom_call_target="tpu_custom_call" | custom-call | flops 54999998464 | tf_op jit(solution)/shard_map/pallas_call | solution.py:74
  93.9 1.6 %collective-permute-start.20 = (bf16[256,4096]{1,0:T(8,128)(2,1)S(1)}, bf16[256,4096]{1,0:T(8,128)(2,1)S(1)}, u32[]{:S(2)}, u32[]{:S(2)}) collective-permute-start(bf16[256,4096]{1,0:T(8,128)(2,1)S(1)} %get-tuple-element.132), channel_id=1, source_target_pairs={{0,1},{1,0},{2,3},{3,2},{4,5},{5,4},{6,7},{7,6},{8,9},{9,8},{10,11... | collective-permute-start | bytes 6291464 | tf_op jit(solution)/shard_map/ppermute | solution.py:44
  95.5 2.1 %shard_map.136._ = bf16[256,8192]{1,0:T(8,128)(2,1)} custom-call(bf16[256,4096]{1,0:T(8,128)(2,1)S(1)} %copy-done.7, f32[1,8192]{1,0:T(1,128)S(1)} %copy-done.5, f32[256,128]{1,0:T(8,128)S(1)} %copy-done.8, bf16[256,512]{1,0:T(8,128)(2,1)S(1)} %copy-done.4, f32[256,128]{1,0:T(8,128)S(1)} %get-tuple-element.135.refs_4_, ...), custom_call_target="tpu_custom_call" | custom-call | flops 46999998464 | tf_op jit(solution)/shard_map/pallas_call | solution.py:74
  97.7 1.7 %collective-permute-done.20.arr = bf16[256,4096]{1,0:T(8,128)(2,1)S(1)} collective-permute-done((bf16[256,4096]{1,0:T(8,128)(2,1)S(1)}, bf16[256,4096]{1,0:T(8,128)(2,1)S(1)}, u32[]{:S(2)}, u32[]{:S(2)}) %collective-permute-start.20) | collective-permute-done | bytes 2097184 | tf_op jit(solution)/shard_map/ppermute | solution.py:44
  99.3 1.4 %shard_map.137 = bf16[256,8192]{1,0:T(8,128)(2,1)} custom-call(bf16[256,8192]{1,0:T(8,128)(2,1)} %shard_map.136._, bf16[256,4096]{1,0:T(8,128)(2,1)S(1)} %collective-permute-done.20.arr), custom_call_target="tpu_custom_call", output_to_operand_aliasing={{}: (0, {})} | custom-call | flops 14000000000 | tf_op jit(solution)/shard_map/pallas_call | solution.py:74
  100.7 1.6 %shard_map.138 = (bf16[512,512]{1,0:T(8,128)(2,1)}, bf16[1,512]{1,0:T(2,128)(2,1)}) custom-call(bf16[512,512]{1,0:T(8,128)(2,1)S(1)} %get-tuple-element.97.o, bf16[512,512]{1,0:T(8,128)(2,1)S(1)} %collective-permute-done.21.a, bf16[512,512]{1,0:T(8,128)(2,1)S(1)} %collective-permute-done.22.b, bf16[512,512]{1,0:T(8,128)(2,1)S(1)} %collective-permute-done.17.fr, ...), custom_call_target="tpu_custom_call" | custom-call | flops 28999999488 | tf_op jit(solution)/shard_map/pallas_call | solution.py:74
  (50 shorter events, 3.0 us)
Async XLA Ops:
  0.6 11.0 %copy-start = (s32[1,512,512]{2,1,0:T(8,128)S(1)}, s32[1,512,512]{2,1,0:T(8,128)}, u32[]{:S(2)}) copy-start(s32[1,512,512]{2,1,0:T(8,128)} %param.12) | copy-start | bytes 3145732
  0.6 10.9 %copy-start.6 = (s32[1,512,4]{1,2,0:T(4,128)S(1)}, s32[1,512,4]{1,2,0:T(4,128)}, u32[]{:S(2)}) copy-start(s32[1,512,4]{1,2,0:T(4,128)} %param.13) | copy-start | bytes 24580
  0.7 20.9 %collective-permute-start.4 = (bf16[512,512]{1,0:T(8,128)(2,1)}, bf16[512,512]{1,0:T(8,128)(2,1)S(1)}, u32[]{:S(2)}, u32[]{:S(2)}) collective-permute-start(bf16[512,512]{1,0:T(8,128)(2,1)} %bitcast.6), channel_id=1, source_target_pairs={{0,6},{1,7},{2,0},{3,1},{4,2},{5,3},{6,4},{7,5},{8,14},{9,15},{10,... | collective-permute-start | bytes 1572872 | tf_op jit(solution)/shard_map/ppermute | solution.py:36
  4.3 17.3 %collective-permute-start.3 = (bf16[512,512]{1,0:T(8,128)(2,1)}, bf16[512,512]{1,0:T(8,128)(2,1)S(1)}, u32[]{:S(2)}, u32[]{:S(2)}) collective-permute-start(bf16[512,512]{1,0:T(8,128)(2,1)} %bitcast.7), channel_id=1, source_target_pairs={{0,2},{1,3},{2,4},{3,5},{4,6},{5,7},{6,0},{7,1},{8,10},{9,11},{10,... | collective-permute-start | bytes 1572872 | tf_op jit(solution)/shard_map/ppermute | solution.py:32
  9.7 3.3 %collective-permute-start.1 = (bf16[256,640]{1,0:T(8,128)(2,1)}, bf16[256,640]{1,0:T(8,128)(2,1)S(1)}, u32[]{:S(2)}, u32[]{:S(2)}) collective-permute-start(bf16[256,640]{1,0:T(8,128)(2,1)} %get-tuple-element.76), channel_id=1, source_target_pairs={{0,1},{1,0},{2,3},{3,2},{4,5},{5,4},{6,7},{7,6},{8,9},{9,8},{10,11... | collective-permute-start | bytes 983048 | tf_op jit(solution)/shard_map/ppermute | solution.py:44
  11.5 8.3 %collective-permute-start = (bf16[256,4096]{1,0:T(8,128)(2,1)}, bf16[256,4096]{1,0:T(8,128)(2,1)S(1)}, u32[]{:S(2)}, u32[]{:S(2)}) collective-permute-start(bf16[256,4096]{1,0:T(8,128)(2,1)} %get-tuple-element.75), channel_id=1, source_target_pairs={{0,1},{1,0},{2,3},{3,2},{4,5},{5,4},{6,7},{7,6},{8,9},{9,8},{10,11... | collective-permute-start | bytes 6291464 | tf_op jit(solution)/shard_map/ppermute | solution.py:44
  11.6 1.4 %copy-start.3 = (bf16[1,512,512]{2,1,0:T(8,128)(2,1)S(1)}, bf16[1,512,512]{2,1,0:T(8,128)(2,1)}, u32[]{:S(2)}) copy-start(bf16[1,512,512]{2,1,0:T(8,128)(2,1)} %param.10) | copy-start | bytes 1572868
  11.6 8.2 %copy-start.4 = (bf16[256,512]{1,0:T(8,128)(2,1)S(1)}, bf16[256,512]{1,0:T(8,128)(2,1)}, u32[]{:S(2)}) copy-start(bf16[256,512]{1,0:T(8,128)(2,1)} %refs_3_.1) | copy-start | bytes 786436
  11.6 8.1 %copy-start.5 = (f32[1,8192]{1,0:T(1,128)S(1)}, f32[1,8192]{1,0:T(1,128)}, u32[]{:S(2)}) copy-start(f32[1,8192]{1,0:T(1,128)} %gain.7) | copy-start | bytes 98308
  11.6 8.1 %copy-start.7 = (bf16[256,4096]{1,0:T(8,128)(2,1)S(1)}, bf16[256,4096]{1,0:T(8,128)(2,1)}, u32[]{:S(2)}) copy-start(bf16[256,4096]{1,0:T(8,128)(2,1)} %get-tuple-element.84.own.own_x.refs_0_) | copy-start | bytes 6291460
  11.6 8.1 %copy-start.8 = (f32[256,128]{1,0:T(8,128)S(1)}, f32[256,128]{1,0:T(8,128)}, u32[]{:S(2)}) copy-start(f32[256,128]{1,0:T(8,128)} %get-tuple-element.77.irr.refs_2_) | copy-start | bytes 393220
  12.3 9.3 %collective-permute-start.2 = (bf16[256,512]{1,0:T(8,128)(2,1)S(1)}, bf16[256,512]{1,0:T(8,128)(2,1)S(1)}, u32[]{:S(2)}, u32[]{:S(2)}) collective-permute-start(bf16[256,512]{1,0:T(8,128)(2,1)S(1)} %get-tuple-element.83), channel_id=1, source_target_pairs={{0,64},{16,80},{32,96},{48,112},{64,0},{80,16},{96,32},{112,48},{1... | collective-permute-start | bytes 786440 | tf_op jit(solution)/shard_map/ppermute | solution.py:48
  13.0 29.0 %collective-permute-start.5 = (bf16[512,512]{1,0:T(8,128)(2,1)S(1)}, bf16[512,512]{1,0:T(8,128)(2,1)S(1)}, u32[]{:S(2)}, u32[]{:S(2)}) collective-permute-start(bf16[512,512]{1,0:T(8,128)(2,1)S(1)} %bitcast.8), channel_id=1, source_target_pairs={{0,8},{1,9},{2,10},{3,11},{4,12},{5,13},{6,14},{7,15},{8,0},{9,1},... | collective-permute-start | bytes 1572872 | tf_op jit(solution)/shard_map/ppermute | solution.py:40
  21.7 8.4 %collective-permute-start.8 = (bf16[256,512]{1,0:T(8,128)(2,1)S(1)}, bf16[256,512]{1,0:T(8,128)(2,1)S(1)}, u32[]{:S(2)}, u32[]{:S(2)}) collective-permute-start(bf16[256,512]{1,0:T(8,128)(2,1)S(1)} %add.18), channel_id=1, source_target_pairs={{0,128},{16,144},{32,160},{48,176},{64,192},{80,208},{96,224},{112... | collective-permute-start | bytes 786440 | tf_op jit(solution)/shard_map/ppermute | solution.py:48
  24.2 16.6 %collective-permute-start.6 = (bf16[512,512]{1,0:T(8,128)(2,1)S(1)}, bf16[512,512]{1,0:T(8,128)(2,1)S(1)}, u32[]{:S(2)}, u32[]{:S(2)}) collective-permute-start(bf16[512,512]{1,0:T(8,128)(2,1)S(1)} %collective-permute-done.3.w1.refs_6_), channel_id=1, source_target_pairs={{0,2},{1,3},{2,4},{3,5},{4,6},{5,7},{6,0},{7,1},{8,10},{9,11},{10,... | collective-permute-start | bytes 1572872 | tf_op jit(solution)/shard_map/ppermute | solution.py:32
  24.5 12.6 %collective-permute-start.7 = (bf16[512,512]{1,0:T(8,128)(2,1)S(1)}, bf16[512,512]{1,0:T(8,128)(2,1)S(1)}, u32[]{:S(2)}, u32[]{:S(2)}) collective-permute-start(bf16[512,512]{1,0:T(8,128)(2,1)S(1)} %get-tuple-element.96), channel_id=1, source_target_pairs={{0,6},{1,7},{2,0},{3,1},{4,2},{5,3},{6,4},{7,5},{8,14},{9,15},{10,... | collective-permute-start | bytes 1572872 | tf_op jit(solution)/shard_map/ppermute | solution.py:36
  27.2 22.7 %collective-permute-start.12 = (bf16[512,512]{1,0:T(8,128)(2,1)S(1)}, bf16[512,512]{1,0:T(8,128)(2,1)S(1)}, u32[]{:S(2)}, u32[]{:S(2)}) collective-permute-start(bf16[512,512]{1,0:T(8,128)(2,1)S(1)} %get-tuple-element.110), channel_id=1, source_target_pairs={{0,2},{1,3},{2,4},{3,5},{4,6},{5,7},{6,0},{7,1},{8,10},{9,11},{10,... | collective-permute-start | bytes 1572872 | tf_op jit(solution)/shard_map/ppermute | solution.py:32
  30.2 18.5 %collective-permute-start.10 = (bf16[256,512]{1,0:T(8,128)(2,1)S(1)}, bf16[256,512]{1,0:T(8,128)(2,1)S(1)}, u32[]{:S(2)}, u32[]{:S(2)}) collective-permute-start(bf16[256,512]{1,0:T(8,128)(2,1)S(1)} %add.19), channel_id=1, source_target_pairs={{0,16},{16,0},{32,48},{48,32},{64,80},{80,64},{96,112},{112,96},{1... | collective-permute-start | bytes 786440 | tf_op jit(solution)/shard_map/ppermute | solution.py:54
  37.3 12.6 %collective-permute-start.13 = (bf16[512,512]{1,0:T(8,128)(2,1)S(1)}, bf16[512,512]{1,0:T(8,128)(2,1)S(1)}, u32[]{:S(2)}, u32[]{:S(2)}) collective-permute-start(bf16[512,512]{1,0:T(8,128)(2,1)S(1)} %add.20), channel_id=1, source_target_pairs={{0,6},{1,7},{2,0},{3,1},{4,2},{5,3},{6,4},{7,5},{8,14},{9,15},{10,... | collective-permute-start | bytes 1572872 | tf_op jit(solution)/shard_map/ppermute | solution.py:36
  42.0 23.3 %collective-permute-start.15 = (bf16[512,512]{1,0:T(8,128)(2,1)S(1)}, bf16[512,512]{1,0:T(8,128)(2,1)S(1)}, u32[]{:S(2)}, u32[]{:S(2)}) collective-permute-start(bf16[512,512]{1,0:T(8,128)(2,1)S(1)} %collective-permute-done.5.w3.refs_12_), channel_id=1, source_target_pairs={{0,6},{1,7},{2,0},{3,1},{4,2},{5,3},{6,4},{7,5},{8,14},{9,15},{10,... | collective-permute-start | bytes 1572872 | tf_op jit(solution)/shard_map/ppermute | solution.py:36
  42.1 21.3 %collective-permute-start.9 = (bf16[512,512]{1,0:T(8,128)(2,1)S(1)}, bf16[512,512]{1,0:T(8,128)(2,1)S(1)}, u32[]{:S(2)}, u32[]{:S(2)}) collective-permute-start(bf16[512,512]{1,0:T(8,128)(2,1)S(1)} %collective-permute-done.5.w3.refs_12_), channel_id=1, source_target_pairs={{0,2},{1,3},{2,4},{3,5},{4,6},{5,7},{6,0},{7,1},{8,10},{9,11},{10,... | collective-permute-start | bytes 1572872 | tf_op jit(solution)/shard_map/ppermute | solution.py:32
  48.7 14.6 %collective-permute-start.11 = (bf16[256,512]{1,0:T(8,128)(2,1)S(1)}, bf16[256,512]{1,0:T(8,128)(2,1)S(1)}, u32[]{:S(2)}, u32[]{:S(2)}) collective-permute-start(bf16[256,512]{1,0:T(8,128)(2,1)S(1)} %add.21), channel_id=1, source_target_pairs={{0,32},{16,48},{32,0},{48,16},{64,96},{80,112},{96,64},{112,80},{1... | collective-permute-start | bytes 786440 | tf_op jit(solution)/shard_map/ppermute | solution.py:54
  63.4 14.8 %collective-permute-start.14 = (bf16[512,512]{1,0:T(8,128)(2,1)S(1)}, bf16[512,512]{1,0:T(8,128)(2,1)S(1)}, u32[]{:S(2)}, u32[]{:S(2)}) collective-permute-start(bf16[512,512]{1,0:T(8,128)(2,1)S(1)} %collective-permute-done.9.w1.refs_10_), channel_id=1, source_target_pairs={{0,2},{1,3},{2,4},{3,5},{4,6},{5,7},{6,0},{7,1},{8,10},{9,11},{10,... | collective-permute-start | bytes 1572872 | tf_op jit(solution)/shard_map/ppermute | solution.py:32
  63.8 17.1 %collective-permute-start.19 = (bf16[256,512]{1,0:T(8,128)(2,1)S(1)}, bf16[256,512]{1,0:T(8,128)(2,1)S(1)}, u32[]{:S(2)}, u32[]{:S(2)}) collective-permute-start(bf16[256,512]{1,0:T(8,128)(2,1)S(1)} %add.22.a), channel_id=1, source_target_pairs={{0,64},{16,80},{32,96},{48,112},{64,0},{80,16},{96,32},{112,48},{1... | collective-permute-start | bytes 786440 | tf_op jit(solution)/shard_map/ppermute | solution.py:48
  64.8 27.0 %collective-permute-start.17 = (bf16[512,512]{1,0:T(8,128)(2,1)S(1)}, bf16[512,512]{1,0:T(8,128)(2,1)S(1)}, u32[]{:S(2)}, u32[]{:S(2)}) collective-permute-start(bf16[512,512]{1,0:T(8,128)(2,1)S(1)} %shard_map.132), channel_id=1, source_target_pairs={{0,8},{1,9},{2,10},{3,11},{4,12},{5,13},{6,14},{7,15},{8,0},{9,1},... | collective-permute-start | bytes 1572872 | tf_op jit(solution)/shard_map/ppermute | solution.py:40
  65.4 17.1 %collective-permute-start.18 = (bf16[512,512]{1,0:T(8,128)(2,1)S(1)}, bf16[512,512]{1,0:T(8,128)(2,1)S(1)}, u32[]{:S(2)}, u32[]{:S(2)}) collective-permute-start(bf16[512,512]{1,0:T(8,128)(2,1)S(1)} %get-tuple-element.123), channel_id=1, source_target_pairs={{0,6},{1,7},{2,0},{3,1},{4,2},{5,3},{6,4},{7,5},{8,14},{9,15},{10,... | collective-permute-start | bytes 1572872 | tf_op jit(solution)/shard_map/ppermute | solution.py:36
  78.2 2.6 %copy-start.1 = (f32[512,512]{1,0:T(8,128)S(1)}, f32[512,512]{1,0:T(8,128)}, u32[]{:S(2)}) copy-start(f32[512,512]{1,0:T(8,128)} %m.1) | copy-start | bytes 3145732
  78.2 2.6 %copy-start.2 = (f32[512,512]{1,0:T(8,128)S(1)}, f32[512,512]{1,0:T(8,128)}, u32[]{:S(2)}) copy-start(f32[512,512]{1,0:T(8,128)} %p.1) | copy-start | bytes 3145732
  79.7 12.0 %collective-permute-start.16 = (bf16[256,640]{1,0:T(8,128)(2,1)S(1)}, bf16[256,640]{1,0:T(8,128)(2,1)S(1)}, u32[]{:S(2)}, u32[]{:S(2)}) collective-permute-start(bf16[256,640]{1,0:T(8,128)(2,1)S(1)} %get-tuple-element.120), channel_id=1, source_target_pairs={{0,1},{1,0},{2,3},{3,2},{4,5},{5,4},{6,7},{7,6},{8,9},{9,8},{10,11... | collective-permute-start | bytes 983048 | tf_op jit(solution)/shard_map/ppermute | solution.py:44
  80.9 19.9 %collective-permute-start.21 = (bf16[512,512]{1,0:T(8,128)(2,1)S(1)}, bf16[512,512]{1,0:T(8,128)(2,1)S(1)}, u32[]{:S(2)}, u32[]{:S(2)}) collective-permute-start(bf16[512,512]{1,0:T(8,128)(2,1)S(1)} %get-tuple-element.138), channel_id=1, source_target_pairs={{0,2},{1,3},{2,4},{3,5},{4,6},{5,7},{6,0},{7,1},{8,10},{9,11},{10,... | collective-permute-start | bytes 1572872 | tf_op jit(solution)/shard_map/ppermute | solution.py:32
  82.6 18.1 %collective-permute-start.22 = (bf16[512,512]{1,0:T(8,128)(2,1)S(1)}, bf16[512,512]{1,0:T(8,128)(2,1)S(1)}, u32[]{:S(2)}, u32[]{:S(2)}) collective-permute-start(bf16[512,512]{1,0:T(8,128)(2,1)S(1)} %add.23), channel_id=1, source_target_pairs={{0,6},{1,7},{2,0},{3,1},{4,2},{5,3},{6,4},{7,5},{8,14},{9,15},{10,... | collective-permute-start | bytes 1572872 | tf_op jit(solution)/shard_map/ppermute | solution.py:36
  93.9 5.4 %collective-permute-start.20 = (bf16[256,4096]{1,0:T(8,128)(2,1)S(1)}, bf16[256,4096]{1,0:T(8,128)(2,1)S(1)}, u32[]{:S(2)}, u32[]{:S(2)}) collective-permute-start(bf16[256,4096]{1,0:T(8,128)(2,1)S(1)} %get-tuple-element.132), channel_id=1, source_target_pairs={{0,1},{1,0},{2,3},{3,2},{4,5},{5,4},{6,7},{7,6},{8,9},{9,8},{10,11... | collective-permute-start | bytes 6291464 | tf_op jit(solution)/shard_map/ppermute | solution.py:44
